TPU v7x, 256 devices: a whole 4x4x8 slice. The times are simulated.
256 devices in a mesh: sx: 16 (over y, x), sy: 16 (over z, core).
Axes of the slice: x: 4, y: 4, z: 8, core: 2. Of those that a mesh axis runs over, the one named last changes fastest.
Arguments:
- dual_rhs: float32 [16, 32, 2, 384, 128], P('sx', 'sy'), may hold values from -6 to 6
- scaling: float32 [16, 32, 2, 384], P('sx', 'sy'), may hold values from 0.05 to 0.5
- dual_count: int32 [16, 32, 2], P('sx', 'sy'), may hold values from 1 to 384, as said below
- corner_map: int32 [16, 32, 4], P('sx', 'sy'), may hold values from 0 to 511, as said below
- local_ops: bfloat16 [16, 32, 1536, 1536], P('sx', 'sy'), as said below
- corner_basis: bfloat16 [16, 32, 12, 1536], P('sx', 'sy'), may hold values from -0.3125 to 0.3125
- coarse_inverse: float32 [1536, 1536], P('sx', 'sy'), as said below
Outputs:
- multipliers: float32 [16, 32, 2, 384, 128], P('sx', 'sy')
- residual: float32 [16, 32, 2, 384, 128], P('sx', 'sy')
Inputs may be any that keep to these rules, and one draw needn't show every extreme that they name: Each edge uses its first dual_count rows; some edge uses all 384. `corner_map`: corner k of subdomain (i, j) is 0: +x+y, 1: -x+y, 2: +x-y, 3: -x-y; a corner shared by neighbouring subdomains has one node number, and every node is a corner of four subdomains. `local_ops`: each block is symmetric positive definite. `coarse_inverse`: symmetric positive definite.
All inputs are finite; a program needn't handle non-finite values.
Results may differ from a plain program's by a relative error of at most 0.017.
Values sent between devices are 32-bit elements; how exact they have to be, the bound alone decides.
No kernel may reach another device: no remote copies, remote signals or barrier semaphores. Data moves between devices by JAX's collectives and lax.ppermute only.
A program may use at most 64 MiB of HBM per device.

v0:
```python
import jax
import jax.numpy as jnp
from jax import lax
from jax.sharding import PartitionSpec as P

CS = 3
ITERS = 3


def shifted(array, axis, by):
    count = lax.axis_size(axis)
    return lax.ppermute(array, axis, [(i, (i + by) % count) for i in range(count)])


def inner_product(first, second):
    return jnp.sum(first * second, axis=(0, 1, 2))


def local(dual_rhs, scaling, dual_count, corner_map, local_ops, corner_basis, coarse_inverse):
    highest = lax.Precision.HIGHEST
    dual_load = dual_rhs[0]
    counts = dual_count[0]
    stiffness = local_ops[0]
    basis = corner_basis[0]
    corner_ids = corner_map[0]
    subdomains = dual_load.shape[0]
    side_rows = dual_load.shape[2]
    load_cases = dual_load.shape[3]
    active = (
        lax.broadcasted_iota(jnp.int32, (subdomains, 2, side_rows), 2) < counts[:, :, None]
    ).astype(jnp.float32)[..., None]
    precond = scaling[0][..., None]
    rows_x = coarse_inverse.shape[0]
    cols_y = coarse_inverse.shape[1]
    coarse_order = rows_x * lax.axis_size("sx")
    node_count = coarse_order // CS
    picker = (
        corner_ids.reshape(-1)[None, :]
        == lax.broadcasted_iota(jnp.int32, (node_count, subdomains * 4), 0)
    ).astype(jnp.float32)
    basis_wide = basis.astype(jnp.float32)

    def norm_sum(value):
        return lax.psum(value, ("sx", "sy"))

    multipliers = jnp.zeros_like(dual_load)
    residual = dual_load * active
    direction = precond * residual
    precond_norm = norm_sum(inner_product(residual, direction))
    for iteration in range(ITERS):
        east_part = direction[:, 0] * active[:, 0]
        north_part = direction[:, 1] * active[:, 1]
        west_part = shifted(east_part, "sx", 1)
        from_below = shifted(north_part[subdomains - 1 :], "sy", 1)
        south_part = jnp.concatenate([from_below, north_part[: subdomains - 1]], 0)
        sided_load = jnp.stack([east_part, -west_part, north_part, -south_part], 1)
        sided_load = sided_load.reshape(subdomains, 4 * side_rows, load_cases).astype(jnp.bfloat16)
        local_part = jnp.einsum(
            "sij,sjr->sir", stiffness, sided_load, preferred_element_type=jnp.float32
        )
        operate_partial_value = jnp.einsum(
            "skn,snr->skr", basis, sided_load, preferred_element_type=jnp.float32
        )
        corner_gathered = jnp.dot(
            picker,
            operate_partial_value.reshape(subdomains * 4, CS * load_cases),
            precision=highest,
        )
        assembled = lax.psum(corner_gathered.reshape(coarse_order, load_cases), ("sx", "sy"))
        offset = lax.axis_index("sy") * cols_y
        column_block = lax.dynamic_slice_in_dim(assembled, offset, cols_y, 0)
        product = jnp.dot(coarse_inverse, column_block, precision=highest)
        owned_rows = lax.psum(product, "sy")
        solved = lax.all_gather(owned_rows, "sx", axis=0, tiled=True)
        corner_values = jnp.dot(
            picker.T, solved.reshape(node_count, CS * load_cases), precision=highest
        )
        operate_corner_values = corner_values.reshape(subdomains, 4 * CS, load_cases)
        responses = local_part + jnp.einsum(
            "skn,skr->snr", basis_wide, operate_corner_values, precision=highest
        )
        responses = responses.reshape(subdomains, 4, side_rows, load_cases)
        east_of = shifted(responses[:, 1], "sx", -1)
        from_above = shifted(responses[:1, 3], "sy", -1)
        north_of = jnp.concatenate([responses[1:, 3], from_above], 0)
        image_vec = jnp.stack(
            [
                (responses[:, 0] - east_of) * active[:, 0],
                (responses[:, 2] - north_of) * active[:, 1],
            ],
            1,
        )
        curvature = lax.psum(inner_product(direction, image_vec), ("sx", "sy"))
        step_size = precond_norm / curvature
        multipliers = multipliers + step_size * direction
        residual = residual - step_size * image_vec
        if iteration + 1 < ITERS:
            preconditioned = precond * residual
            norm_next = norm_sum(inner_product(residual, preconditioned))
            direction = preconditioned + norm_next / precond_norm * direction
            precond_norm = norm_next
    return (multipliers[None], residual[None])


def solution(mesh):
    in_specs = (
        P("sx", "sy", None, None, None),
        P("sx", "sy", None, None),
        P("sx", "sy", None),
        P("sx", "sy", None),
        P("sx", "sy", None, None),
        P("sx", "sy", None, None),
        P("sx", "sy"),
    )
    out_specs = (P("sx", "sy", None, None, None), P("sx", "sy", None, None, None))
    return jax.shard_map(local, mesh=mesh, in_specs=in_specs, out_specs=out_specs, check_vma=False)
```

profile of v0, /device:TPU:1, one launch (start us, length us, event | category | flops | bytes accessed | tf_op | source)
XLA Modules:
  0.0 1507.0 jit_solution(3745887559130691722)
XLA Ops:
  10.1 2.1 collective-permute-start
  12.2 2.5 collective-permute-start.1
  15.1 2.3 collective-permute-done.1
  17.4 5.4 collective-permute-done
  24.6 6.9 fusion.4
  31.5 248.0 %all-reduce.5.cloned.1.call-done = f32[1536,128]{1,0:T(8,128)} async-done(((f32[1536,128]{1,0:T(8,128)}), f32[1536,128]{1,0:T(8,128)}) %all-reduce.5.cloned.1.call-update) | async-done | bytes 786448 | tf_op jit(solution)/shard_map/psum | solution.py:69
  280.5 45.7 %psum.86 = f32[96,128]{1,0:T(8,128)S(1)} all-reduce(f32[96,128]{1,0:T(8,128)S(1)} %convolution_bitcast_fusion.2), channel_id=1, replica_groups=mesh['sx'=16,'sy'=16] {'sy'}, use_global_device_ids=true, to_apply=%region_3.0 | all-reduce | flops 12288 | bytes 98304 | tf_op jit(solution)/shard_map/psum | solution.py:73
  326.2 19.4 %all_gather.9 = f32[1536,128]{1,0:T(8,128)S(1)} all-gather(f32[96,128]{1,0:T(8,128)S(1)} %psum.86), channel_id=1, replica_groups=mesh['sx'=16,'sy'=16] {'sx'}, dimensions={0}, use_global_device_ids=true | all-gather | bytes 835584 | tf_op jit(solution)/shard_map/all_gather | solution.py:74
  348.2 2.0 fusion.6
  350.2 1.8 reshape.272
  354.0 8.4 collective-permute-start.3
  365.1 2.5 collective-permute-start.2
  370.6 5.6 collective-permute-done.2
  376.2 1.9 fusion.37
  378.4 76.6 %all-reduce = (f32[128]{0:T(128)S(1)}, f32[128]{0:T(128)S(1)}) all-reduce(f32[128]{0:T(128)S(1)} %get-tuple-element.7, f32[128]{0:T(128)S(1)} %get-tuple-element.6), channel_id=1, replica_groups=mesh['sx'=16,'sy'=16] {'sx','sy'}, use_global_device_ids=true, to_apply=%region_1.0 | all-reduce | flops 256 | bytes 2048 | tf_op jit(solution)/shard_map/psum | solution.py:44
  455.2 74.5 %psum.88 = f32[128]{0:T(128)S(1)} all-reduce(f32[128]{0:T(128)S(1)} %get-tuple-element.10), channel_id=1, replica_groups=mesh['sx'=16,'sy'=16] {'sx','sy'}, use_global_device_ids=true, to_apply=%region_7.0 | all-reduce | flops 128 | bytes 1024 | tf_op jit(solution)/shard_map/psum | solution.py:44
  532.2 2.3 collective-permute-done.5
  534.6 9.2 collective-permute-done.4
  548.6 2.1 reshape.274
  550.7 7.9 fusion.2
  558.6 240.2 %all-reduce.7.cloned.1.call-done = f32[1536,128]{1,0:T(8,128)} async-done(((f32[1536,128]{1,0:T(8,128)}), f32[1536,128]{1,0:T(8,128)}) %all-reduce.7.cloned.1.call-update) | async-done | bytes 786448 | tf_op jit(solution)/shard_map/psum | solution.py:69
  799.8 45.7 %psum.90 = f32[96,128]{1,0:T(8,128)S(1)} all-reduce(f32[96,128]{1,0:T(8,128)S(1)} %convolution_bitcast_fusion.1), channel_id=1, replica_groups=mesh['sx'=16,'sy'=16] {'sy'}, use_global_device_ids=true, to_apply=%region_9.0 | all-reduce | flops 12288 | bytes 98304 | tf_op jit(solution)/shard_map/psum | solution.py:73
  845.5 19.4 %all_gather.10 = f32[1536,128]{1,0:T(8,128)S(1)} all-gather(f32[96,128]{1,0:T(8,128)S(1)} %psum.90), channel_id=1, replica_groups=mesh['sx'=16,'sy'=16] {'sx'}, dimensions={0}, use_global_device_ids=true | all-gather | bytes 835584 | tf_op jit(solution)/shard_map/all_gather | solution.py:74
  867.5 3.4 fusion.7
  870.9 2.7 reshape.277
  873.6 2.5 fusion.65
  876.1 3.6 fusion.64
  881.5 8.4 collective-permute-start.7
  891.0 2.4 collective-permute-start.6
  893.4 1.9 fusion.90
  896.9 1.8 fusion.54
  898.7 3.5 collective-permute-done.6
  902.2 1.9 fusion.38
  904.4 76.7 %psum.91 = f32[128]{0:T(128)S(1)} all-reduce(f32[128]{0:T(128)S(1)} %multiply_reduce_fusion), channel_id=1, replica_groups=mesh['sx'=16,'sy'=16] {'sx','sy'}, use_global_device_ids=true, to_apply=%region_11.0 | all-reduce | flops 128 | bytes 1024 | tf_op jit(solution)/shard_map/psum | solution.py:93
  981.4 74.4 %psum.92 = f32[128]{0:T(128)S(1)} all-reduce(f32[128]{0:T(128)S(1)} %fusion.10), channel_id=1, replica_groups=mesh['sx'=16,'sy'=16] {'sx','sy'}, use_global_device_ids=true, to_apply=%region_13.0 | all-reduce | flops 128 | bytes 1024 | tf_op jit(solution)/shard_map/psum | solution.py:44
  1058.3 2.4 collective-permute-done.9
  1060.7 9.3 collective-permute-done.8
  1071.9 6.9 fusion
  1078.8 241.3 %all-reduce.9.cloned.1.call-done = f32[1536,128]{1,0:T(8,128)} async-done(((f32[1536,128]{1,0:T(8,128)}), f32[1536,128]{1,0:T(8,128)}) %all-reduce.9.cloned.1.call-update) | async-done | bytes 786448 | tf_op jit(solution)/shard_map/psum | solution.py:69
  1321.0 45.7 %psum.94 = f32[96,128]{1,0:T(8,128)S(1)} all-reduce(f32[96,128]{1,0:T(8,128)S(1)} %convolution_bitcast_fusion), channel_id=1, replica_groups=mesh['sx'=16,'sy'=16] {'sy'}, use_global_device_ids=true, to_apply=%region_15.0 | all-reduce | flops 12288 | bytes 98304 | tf_op jit(solution)/shard_map/psum | solution.py:73
  1366.7 20.9 %all_gather.11 = f32[1536,128]{1,0:T(8,128)} all-gather(f32[96,128]{1,0:T(8,128)S(1)} %psum.94), channel_id=1, replica_groups=mesh['sx'=16,'sy'=16] {'sx'}, dimensions={0}, use_global_device_ids=true | all-gather | bytes 835584 | tf_op jit(solution)/shard_map/all_gather | solution.py:74
  1389.4 2.0 fusion.8
  1394.5 8.7 collective-permute-start.11
  1404.8 1.9 copy.126
  1408.3 2.4 collective-permute-start.10
  1410.7 1.9 fusion.89
  1413.7 5.8 collective-permute-done.10
  1420.7 76.4 %psum.95 = f32[128]{0:T(128)S(1)} all-reduce(f32[128]{0:T(128)S(1)} %fusion.12), channel_id=1, replica_groups=mesh['sx'=16,'sy'=16] {'sx','sy'}, use_global_device_ids=true, to_apply=%region_17.0 | all-reduce | flops 128 | bytes 1024 | tf_op jit(solution)/shard_map/psum | solution.py:93
  (130 shorter events, 51.1 us)
Async XLA Ops:
  7.2 15.8 %copy-start = (bf16[1,2,12,1536]{3,1,2,0:T(2,128)(2,1)S(1)}, bf16[1,2,12,1536]{3,1,2,0:T(2,128)(2,1)}, u32[]{:S(2)}) copy-start(bf16[1,2,12,1536]{3,1,2,0:T(2,128)(2,1)} %param.12) | copy-start | bytes 221188
  7.2 272.4 %all-reduce.5.cloned.1.call-start = ((), (), s32[]{:S(2)}) async-start(), calls=%async_computation | async-start | bytes 1572864 | tf_op jit(solution)/shard_map/psum | solution.py:69
  9.8 4.9 copy-start.13
  10.1 12.7 collective-permute-start
  12.2 5.1 collective-permute-start.1
  24.6 255.0 %copy-start.11 = (f32[96,96]{1,0:T(8,128)S(1)}, f32[96,96]{1,0:T(8,128)}, u32[]{:S(2)}) copy-start(f32[96,96]{1,0:T(8,128)} %param.13) | copy-start | bytes 110596
  24.6 774.2 %all-reduce.7.cloned.1.call-start = ((), (), s32[]{:S(2)}) async-start(), calls=%async_computation.1 | async-start | bytes 1572864 | tf_op jit(solution)/shard_map/psum | solution.py:69
  354.0 13.7 copy-start.12
  354.0 15.5 %collective-permute-start.3 = (f32[1,384,128]{2,1,0:T(8,128)}, f32[1,384,128]{2,1,0:T(8,128)}, u32[]{:S(2)}, u32[]{:S(2)}) collective-permute-start(f32[1,384,128]{2,1,0:T(8,128)} %bitcast.21), channel_id=1, source_target_pairs={{0,15},{1,0},{2,1},{3,2},{4,3},{5,4},{6,5},{7,6},{8,7},{9,8},{10,9... | collective-permute-start | bytes 589832 | tf_op jit(solution)/shard_map/ppermute | solution.py:12
  365.1 11.0 collective-permute-start.2
  530.5 13.4 collective-permute-start.4
  530.9 3.6 collective-permute-start.5
  550.7 769.4 %all-reduce.9.cloned.1.call-start = ((), (), s32[]{:S(2)}) async-start(), calls=%async_computation.2 | async-start | bytes 1572864 | tf_op jit(solution)/shard_map/psum | solution.py:69
  881.5 15.4 %collective-permute-start.7 = (f32[1,384,128]{2,1,0:T(8,128)}, f32[1,384,128]{2,1,0:T(8,128)}, u32[]{:S(2)}, u32[]{:S(2)}) collective-permute-start(f32[1,384,128]{2,1,0:T(8,128)} %bitcast.185), channel_id=1, source_target_pairs={{0,15},{1,0},{2,1},{3,2},{4,3},{5,4},{6,5},{7,6},{8,7},{9,8},{10,9... | collective-permute-start | bytes 589832 | tf_op jit(solution)/shard_map/ppermute | solution.py:12
  891.0 5.3 copy-start.10
  891.0 11.3 collective-permute-start.6
  896.3 5.9 copy-start.9
  1056.7 13.4 collective-permute-start.8
  1057.2 3.5 collective-permute-start.9
  1394.5 16.2 %collective-permute-start.11 = (f32[1,384,128]{2,1,0:T(8,128)}, f32[1,384,128]{2,1,0:T(8,128)}, u32[]{:S(2)}, u32[]{:S(2)}) collective-permute-start(f32[1,384,128]{2,1,0:T(8,128)} %bitcast.57), channel_id=1, source_target_pairs={{0,15},{1,0},{2,1},{3,2},{4,3},{5,4},{6,5},{7,6},{8,7},{9,8},{10,9... | collective-permute-start | bytes 589832 | tf_op jit(solution)/shard_map/ppermute | solution.py:12
  1408.3 11.3 copy-start.8
  1408.3 11.3 collective-permute-start.10
  1413.7 83.4 %copy-start.1 = (f32[1,2,2,384,128]{4,3,2,1,0:T(8,128)S(1)}, f32[1,2,2,384,128]{4,3,2,1,0:T(8,128)}, u32[]{:S(2)}) copy-start(f32[1,2,2,384,128]{4,3,2,1,0:T(8,128)} %param.7) | copy-start | bytes 2359300
  1413.7 83.4 %copy-start.2 = (f32[1,2,1,384,128]{4,3,1,2,0:T(8,128)S(1)}, f32[1,2,1,384,128]{4,3,1,2,0:T(8,128)}, u32[]{:S(2)}) copy-start(f32[1,2,1,384,128]{4,3,1,2,0:T(8,128)} %get-tuple-element.38) | copy-start | bytes 1179652
  1413.7 83.4 %copy-start.3 = (f32[1,2,1,384,128]{4,3,1,2,0:T(8,128)S(1)}, f32[1,2,1,384,128]{4,3,1,2,0:T(8,128)}, u32[]{:S(2)}) copy-start(f32[1,2,1,384,128]{4,3,1,2,0:T(8,128)} %fusion.90) | copy-start | bytes 1179652
  1413.7 83.4 %copy-start.4 = (f32[1,2,1,384,128]{4,3,1,2,0:T(8,128)S(1)}, f32[1,2,1,384,128]{4,3,1,2,0:T(8,128)}, u32[]{:S(2)}) copy-start(f32[1,2,1,384,128]{4,3,1,2,0:T(8,128)} %get-tuple-element.35) | copy-start | bytes 1179652
  1413.7 83.4 %copy-start.5 = (f32[1,2,1,384,128]{4,3,1,2,0:T(8,128)S(1)}, f32[1,2,1,384,128]{4,3,1,2,0:T(8,128)}, u32[]{:S(2)}) copy-start(f32[1,2,1,384,128]{4,3,1,2,0:T(8,128)} %get-tuple-element.33) | copy-start | bytes 1179652
  1497.7 1.1 copy-start.6
  1497.8 1.4 copy-start.7
Sparse Core Ops, SparseCore 0:
  24.7 254.8 all-reduce.4
  550.8 248.0 all-reduce.6
  1072.0 248.0 all-reduce.8
where the time goes:
time: 1520 us; the launch traced here: 1510 us
  waiting for transfers between devices  776 us (51%)
  blocking collectives  575 us (38%)
  local copies, waits for them, and re-layouts  42.4 us (3%)
  starting transfers between devices  40.4 us (3%)
  matrix products  38.5 us (3%)
  other arithmetic  20.4 us (1%)
    psum x3, waiting for transfers between devices, local(): lax.psum(corner_gathered.reshape(coarse_order, load_cases), ('sx', 'sy'))  730 us
    psum x3, blocking collectives, norm_sum(): return lax.psum(value, ('sx', 'sy'))  225 us
    psum x2, blocking collectives, local(): curvature = lax.psum(inner_product(direction, image_vec), ('sx', 'sy'))  153 us
    psum x3, blocking collectives, local(): owned_rows = lax.psum(product, 'sy')  137 us
    all_gather x3, blocking collectives, local(): solved = lax.all_gather(owned_rows, 'sx', axis=0, tiled=True)  59.7 us
    ppermute x12, waiting for transfers between devices, shifted(): lax.ppermute(array, axis, [(i, (i + by) % count) for i in range(count)])  45.9 us
    ppermute x12, starting transfers between devices, shifted(): lax.ppermute(array, axis, [(i, (i + by) % count) for i in range(count)])  40.3 us
  transfers between devices with their start and end apart: 15, of which 12 were waited for; matrix products, arithmetic and copies ran while one was open for 3% of the time, Pallas kernels for 0%

commit v1 on v0

v1 whole, which is shorter than its diff:
```python
import functools

import numpy as np
import jax
import jax.numpy as jnp
from jax import lax
from jax.experimental import pallas as pl
from jax.experimental.pallas import tpu as pltpu
from jax.sharding import PartitionSpec as P

CS = 3
NEAR = 16
ROWS = 3 * NEAR
F32, BF16 = jnp.float32, jnp.bfloat16
VMEM = pl.BlockSpec(memory_space=pltpu.VMEM)
SMEM = pl.BlockSpec(memory_space=pltpu.SMEM)


def shifted(array, axis, by):
    count = lax.axis_size(axis)
    return lax.ppermute(array, axis, [(i, (i + by) % count) for i in range(count)])


def along_sy(copies):
    count = lax.axis_size("sy")
    groups = [[2 * z + core for z in range(count // 2)] for core in range(2)]
    same = lax.all_to_all(copies, "sy", 0, 0, tiled=True, axis_index_groups=groups)
    return same, lax.ppermute(same, "sy", [(i, i ^ 1) for i in range(count)])


def vmem_call(body, outs, scratch=(), limit=48):
    return pl.pallas_call(
        body,
        out_shape=outs,
        scratch_shapes=list(scratch),
        compiler_params=pltpu.CompilerParams(vmem_limit_bytes=limit * 2**20),
    )


def split(value):
    high = value.astype(BF16)
    return high, (value - high.astype(F32)).astype(BF16)


def halves(value):
    return jnp.concatenate(split(value), 1)


def multiply(first, second):
    return jnp.dot(first, second, preferred_element_type=F32)


def place_matrices():
    place = [(0, 0), (-1, 0), (0, -1), (-1, -1)]
    out = np.zeros((4, ROWS, 32), np.float32)
    for s in range(2):
        for e in range(2):
            for k, (di, dj) in enumerate(place):
                for c in range(CS):
                    out[2 * s + e, (1 + di) * NEAR + (1 + s + dj) * CS + c, k * CS + c] += 1
                    row = (1 + di + (1 - e)) * NEAR + (1 + s + dj + e) * CS + c
                    out[2 * s + e, row, 16 + k * CS + c] -= 1
    return out


def lane_matrices(gy):
    out = np.zeros((2, 128, gy * NEAR), np.float32)
    for core in range(2):
        for slot in range(gy):
            z, other = slot % (gy // 2), slot // (gy // 2)
            source = 2 * z + (core ^ other)
            for jj in range(4):
                for c in range(CS):
                    j = (2 * source - 1 + jj) % (2 * gy)
                    out[core, j * CS + c, slot * NEAR + jj * CS + c] = 1
    return out


def message_to(out_ref, basis_ref, vector, extra):
    got = multiply(basis_ref[...], halves(vector))
    cases = got.shape[1] // 2
    rows = got[:ROWS, :cases] + got[:ROWS, cases:] + got[ROWS:, :cases]
    index = lax.broadcasted_iota(jnp.int32, rows.shape, 0)
    for k, row in enumerate(extra):
        rows = jnp.where(index == NEAR - 4 + k, row, rows)
    for copy in range(out_ref.shape[0]):
        out_ref[copy] = rows


def column_sum(value):
    return jnp.sum(value, axis=0, keepdims=True)


def begin_body(rhs, gain_in, count, basis, east, above, places, facts, res, w0, act, gain, edges, message):
    side, cases = rhs.shape[1], rhs.shape[2]
    norm = jnp.zeros((1, cases), F32)
    for edge in range(4):
        s, e = divmod(edge, 2)
        index = lax.broadcasted_iota(jnp.int32, (side, cases), 0)
        mask = (index < count[s, e]).astype(F32)
        act[edge] = mask
        gain[edge] = gain_in[edge] * mask
        res[edge] = rhs[edge] * mask
        w0[edge] = gain[edge] * res[edge]
        norm = norm + column_sum(res[edge] * w0[edge])
        own = basis[s, :, 2 * e * side : (2 * e + 1) * side].astype(BF16)
        if e == 0:
            other = east[s].astype(BF16)
        elif s == 0:
            other = basis[1, :, 3 * side :].astype(BF16)
        else:
            other = above[...].astype(BF16)
        place = places[edge].astype(BF16)
        value = multiply(place[:, : 4 * CS], own) + multiply(place[:, 16 : 16 + 4 * CS], other)
        high, low = split(value)
        edges[:ROWS, edge * side : (edge + 1) * side] = high
        edges[ROWS:, edge * side : (edge + 1) * side] = low
    message_to(message, edges, w0[...].reshape(4 * side, cases), [norm, facts[...]])


def load_parts(parts, own, west, below):
    side, cases = own.shape[1], own.shape[2]
    for s in range(2):
        south = -below[...] if s == 0 else -own[1]
        for q, value in enumerate([own[2 * s], -west[s], own[2 * s + 1], south]):
            high, low = split(value)
            parts[s, q * side : (q + 1) * side, :cases] = high
            parts[s, q * side : (q + 1) * side, cases:] = low


def apply_rows(block, parts, s):
    out = multiply(block[0], parts[s])
    cases = out.shape[1] // 2
    return out[:, :cases] + out[:, cases:]


def give_body(own, west, below, block, out, parts):
    step = pl.program_id(0)

    @pl.when(step == 0)
    def _():
        load_parts(parts, own, west, below)

    out[0] = apply_rows(block, parts, step % 2)


def keep_body(own, west, below, block, out, parts):
    step = pl.program_id(0)

    @pl.when(step == 0)
    def _():
        load_parts(parts, own, west, below)

    value = apply_rows(block, parts, step // 2 - step // 4)

    @pl.when(step < 4)
    def _():
        out[step] = value

    @pl.when(step == 4)
    def _():
        out[1] = out[1] - value


def stiffness_call(give, own, west, below, blocks):
    side, cases = own.shape[1], own.shape[2]
    if give:
        steps, body = 3, give_body
        where = lambda t: (jnp.where(t == 2, 3, 1 + 4 * t), 0, 0)
        out_spec = pl.BlockSpec((1, side, cases), lambda t: (t, 0, 0))
        out_shape = jax.ShapeDtypeStruct((3, side, cases), F32)
    else:
        steps, body = 5, keep_body
        where = lambda t: (jnp.where(t == 4, 7, 2 * t), 0, 0)
        out_spec = pl.BlockSpec((4, side, cases), lambda t: (0, 0, 0))
        out_shape = jax.ShapeDtypeStruct((4, side, cases), F32)
    whole = lambda shape: pl.BlockSpec(shape, lambda t: (0,) * len(shape))
    return pl.pallas_call(
        body,
        grid=(steps,),
        in_specs=[
            whole(own.shape),
            whole(west.shape),
            whole(below.shape),
            pl.BlockSpec((1,) + blocks.shape[1:], where),
        ],
        out_specs=out_spec,
        out_shape=out_shape,
        scratch_shapes=[pltpu.VMEM((2, 4 * side, 2 * cases), BF16)],
        compiler_params=pltpu.CompilerParams(vmem_limit_bytes=40 * 2**20),
        cost_estimate=pl.CostEstimate(
            flops=steps * side * 4 * side * cases * 4,
            bytes_accessed=steps * side * 4 * side * 2 + 10 * side * cases * 4,
            transcendentals=0,
        ),
    )(own, west, below, blocks)


def image_body(last, part, east, north, got, edges, act, gain, kappa, previous, *outs):
    side, cases = part.shape[1], part.shape[2]
    total = got[0]
    for k in range(1, got.shape[0]):
        total = total + got[k]
    high, low = split(total)
    twice = jnp.concatenate(
        [jnp.concatenate([high, low], 1), jnp.concatenate([high, jnp.zeros_like(low)], 1)], 0
    )
    u_ref = outs[0]
    first = jnp.zeros((1, cases), F32)
    second = jnp.zeros((1, cases), F32)
    for edge in range(4):
        coarse = lax.dot_general(
            edges[:, edge * side : (edge + 1) * side],
            twice,
            (((0,), (0,)), ((), ())),
            preferred_element_type=F32,
        )
        value = part[edge] + coarse[:, :cases] + coarse[:, cases:]
        if edge % 2 == 0:
            value = value - east[edge // 2]
        elif edge == 3:
            value = value - north[...]
        u_ref[edge] = value * act[edge]
        first = first + column_sum(previous[edge] * u_ref[edge])
        if not last:
            outs[1][edge] = kappa[...] * gain[edge] * value
            second = second + column_sum(outs[1][edge] * u_ref[edge])
    spare = total[NEAR - 8 : NEAR]
    if last:
        outs[1][...] = spare
        outs[2][...] = jnp.broadcast_to(first, outs[2].shape)
    else:
        outs[2][...] = spare
        message_to(outs[3], edges, outs[1][...].reshape(4 * side, cases), [first, second])


def image_call(last, part, east, north, got, edges, act, gain, kappa, previous, copies):
    _, side, cases = part.shape
    field = jax.ShapeDtypeStruct((4, side, cases), F32)
    spare = jax.ShapeDtypeStruct((8, cases), F32)
    if last:
        outs = (field, spare, jax.ShapeDtypeStruct((copies, cases), F32))
    else:
        outs = (field, field, spare, jax.ShapeDtypeStruct((copies, ROWS, cases), F32))
    return vmem_call(functools.partial(image_body, last), outs)(
        part, east, north, got, edges, act, gain, kappa, previous
    )


def pick_body(numbers, me, columns, out, rows):
    gy = numbers.shape[0]
    rows[...] = jnp.zeros_like(rows)
    for j in range(2 * gy):
        node = numbers[j // 2, 2 * me[0] + j % 2]
        for c in range(CS):
            rows[pl.ds(j * CS + c, 1)] = columns[pl.ds(node * CS + c, 1)]
    turned = rows[...].T
    for copy in range(out.shape[0]):
        out[copy] = turned[: out.shape[1]]


def near_body(gx, numbers, me, same, other, out):
    gy = numbers.shape[0]
    block = same.shape[1]
    out[...] = jnp.zeros_like(out)
    core = me[1] % 2
    for jj in range(4):
        j = (2 * me[1] - 1 + jj + 2 * gy) % (2 * gy)
        for i in range(gx):
            node = numbers[j // 2, 2 * i + j % 2]
            owner = node * CS // block
            row = node * CS - owner * block
            mine = owner % 2 == core
            for c in range(CS):
                first = same[owner // 2, pl.ds(row + c, 1)]
                second = other[owner // 2, pl.ds(row + c, 1)]
                out[pl.ds(i * NEAR + jj * CS + c, 1)] = jnp.where(mine, first, second)


def coarse_body(below, own, beyond, lanes, same, other, out):
    gx = out.shape[0]
    cases = same.shape[2]
    lane = lanes[...].astype(BF16)
    value = jnp.zeros((gx * NEAR, cases), F32)
    for ii, source in enumerate([below, own, beyond]):
        pieces = [ref[z, ii * NEAR : (ii + 1) * NEAR] for ref in (same, other) for z in range(same.shape[0])]
        if ii == 0:
            total = pieces[0][NEAR - 8 :]
            for piece in pieces[1:]:
                total = total + piece[NEAR - 8 :]
        gathered = halves(jnp.concatenate(pieces, 0))
        high, low = split(source[...])
        high = multiply(high, lane).astype(BF16)
        low = multiply(low, lane).astype(BF16)
        product = multiply(high, gathered)
        value = value + product[:, :cases] + product[:, cases:] + multiply(low, gathered[:, :cases])
    index = lax.broadcasted_iota(jnp.int32, (8, cases), 0)
    for target in range(gx):
        for ii in range(3):
            at = ((target - 1 + ii) % gx) * NEAR
            out[target, ii * NEAR : ii * NEAR + 8] = value[at : at + 8]
            rest = value[at + 8 : at + 16]
            if ii == 0:
                rest = jnp.where(index < 4, rest, total)
            out[target, ii * NEAR + 8 : ii * NEAR + 16] = rest


def finish_body(kappa_ref, spare0, spare1, spare2, last, w0, w1, w2, u1, u2, u3, res, mult_out, res_out):
    kappa = kappa_ref[...]
    moments = [
        spare0[4:5],
        kappa * spare1[4:5],
        kappa * spare1[5:6],
        kappa * spare2[4:5],
        kappa * spare2[5:6],
        kappa * column_sum(last[...]),
    ]

    def form(first, second, shift):
        total = 0.0
        for i, x in enumerate(first):
            for j, y in enumerate(second):
                total = total + x * y * moments[i + j + shift]
        return total

    one = jnp.ones_like(kappa)
    rho, pi, gamma = [one], [one], []
    rz = moments[0]
    for iteration in range(3):
        step = rz / form(pi, pi, 1)
        gamma = [(gamma[k] if k < len(gamma) else 0.0) + step * pi[k] for k in range(len(pi))]
        rho = [one] + [-value for value in gamma]
        if iteration < 2:
            rz_new = form(rho, rho, 0)
            ratio = rz_new / rz
            pi = [rho[k] + (ratio * pi[k] if k < len(pi) else 0.0) for k in range(len(rho))]
            rz = rz_new
    gamma = [kappa * value for value in gamma]
    for edge in range(4):
        mult_out[edge] = gamma[0] * w0[edge] + gamma[1] * w1[edge] + gamma[2] * w2[edge]
        res_out[edge] = res[edge] - (gamma[0] * u1[edge] + gamma[1] * u2[edge] + gamma[2] * u3[edge])


def local(dual_rhs, scaling, dual_count, corner_map, local_ops, corner_basis, coarse_inverse):
    gx, gy = lax.axis_size("sx"), lax.axis_size("sy")
    a, b = lax.axis_index("sx"), lax.axis_index("sy")
    side, cases = dual_rhs.shape[3], dual_rhs.shape[4]
    rhs = dual_rhs.reshape(4, side, cases)
    blocks = local_ops.reshape(8, side, 4 * side)
    block = coarse_inverse.shape[0]
    order = block * gx
    field = jax.ShapeDtypeStruct((4, side, cases), F32)
    half = gy // 2
    basis = corner_basis[0]

    wide_basis = basis.astype(F32)
    east = shifted(wide_basis[:, :, side : 2 * side], "sx", -1)
    above = shifted(wide_basis[0, :, 3 * side :], "sy", -1)
    numbers = corner_map[0, :, 0].astype(F32)
    corner = local_ops[0, :, :cases, :cases].astype(F32)
    size = jnp.sum(corner * jnp.eye(corner.shape[1], dtype=F32)) / (2 * gx * gy * corner.shape[1])
    size = size + jnp.sum(jnp.abs(coarse_inverse)) / order
    spare = jnp.concatenate([numbers, size[None], jnp.zeros((cases - block - 3,), F32)])
    wide = jnp.concatenate([coarse_inverse, jnp.broadcast_to(spare[None], (block, cases - block))], 1)
    columns_all = lax.all_to_all(
        jnp.broadcast_to(wide[None], (gx, block, cases)), "sx", 0, 0, tiled=True
    )
    known = columns_all[:, 0]
    facts = jnp.concatenate(
        [
            known[:, block : block + 2].reshape(2 * gx),
            jnp.sum(known[:, block + 2])[None],
            jnp.zeros((cases - 2 * gx - 1,), F32),
        ]
    )[None]

    residual, w0, act, gain, edges, message = pl.pallas_call(
        begin_body,
        in_specs=[VMEM, VMEM, SMEM, VMEM, VMEM, VMEM, VMEM, VMEM],
        out_shape=(
            field,
            field,
            field,
            field,
            jax.ShapeDtypeStruct((2 * ROWS, 4 * side), BF16),
            jax.ShapeDtypeStruct((half, ROWS, cases), F32),
        ),
        compiler_params=pltpu.CompilerParams(vmem_limit_bytes=48 * 2**20),
    )(
        rhs,
        scaling.reshape(4, side, 1),
        dual_count[0],
        wide_basis,
        east,
        above,
        jnp.asarray(place_matrices()),
        facts,
    )

    def halo(vector):
        return shifted(vector.reshape(2, 2, side, cases)[:, 0], "sx", 1), shifted(vector[3], "sy", 1)

    def respond(vector, west, below):
        given = stiffness_call(True, vector, west, below, blocks)
        back_east = shifted(given[:2], "sx", -1)
        back_north = shifted(given[2], "sy", -1)
        kept = stiffness_call(False, vector, west, below, blocks)
        return kept, back_east, back_north

    same, other = along_sy(message)
    known = jnp.concatenate([same[:, NEAR - 3], other[:, NEAR - 3]], 0)
    even = b % 2 == 0
    ordered = jnp.where(
        even,
        jnp.stack([same[:, NEAR - 3], other[:, NEAR - 3]], 1),
        jnp.stack([other[:, NEAR - 3], same[:, NEAR - 3]], 1),
    ).reshape(gy, cases)
    kappa = jnp.broadcast_to(4.0 / jnp.sum(known[:, 2 * gx]), (1, cases))
    grid_numbers = ordered.astype(jnp.int32)
    me = jnp.stack([a, b]).astype(jnp.int32)

    turned = pl.pallas_call(
        pick_body,
        in_specs=[SMEM, SMEM, VMEM],
        out_shape=jax.ShapeDtypeStruct((half, block, cases), F32),
        scratch_shapes=[pltpu.VMEM((cases, cases), F32)],
    )(grid_numbers, me, columns_all.reshape(order, cases))
    rows_same, rows_other = along_sy(turned)
    own_part = pl.pallas_call(
        functools.partial(near_body, gx),
        in_specs=[SMEM, SMEM, VMEM, VMEM],
        out_shape=jax.ShapeDtypeStruct((gx * NEAR, cases), F32),
    )(grid_numbers, me, rows_same, rows_other)
    below_part = shifted(own_part, "sx", 1)
    beyond_part = shifted(own_part, "sx", -1)
    lanes = lax.dynamic_index_in_dim(jnp.asarray(lane_matrices(gy)), b % 2, 0, keepdims=False)

    def coarse_solve(same, other):
        send = vmem_call(coarse_body, jax.ShapeDtypeStruct((gx, ROWS, cases), F32))(
            below_part, own_part, beyond_part, lanes, same, other
        )
        return lax.all_to_all(send, "sx", 0, 0, tiled=True)

    def image(last, local_part, got, previous, copies):
        return image_call(last, *local_part, got, edges, act, gain, kappa, previous, copies)

    local0 = respond(w0, *halo(w0))
    got = coarse_solve(same, other)
    u1, w1, spare0, message = image(False, local0, got, w0, half)
    same, other = along_sy(message)
    local1 = respond(w1, *halo(w1))
    got = coarse_solve(same, other)
    u2, w2, spare1, message = image(False, local1, got, w1, half)
    same, other = along_sy(message)
    local2 = respond(w2, *halo(w2))
    got = coarse_solve(same, other)
    u3, spare2, last = image(True, local2, got, w2, gx * gy)
    last = lax.all_to_all(last.reshape(gx * gy, 1, cases), ("sx", "sy"), 0, 0, tiled=True)
    multipliers, residual = vmem_call(finish_body, (field, field))(
        kappa, spare0, spare1, spare2, last.reshape(gx * gy, cases), w0, w1, w2, u1, u2, u3, residual
    )
    shape = dual_rhs.shape
    return multipliers.reshape(shape), residual.reshape(shape)


def solution(mesh):
    in_specs = (
        P("sx", "sy", None, None, None),
        P("sx", "sy", None, None),
        P("sx", "sy", None),
        P("sx", "sy", None),
        P("sx", "sy", None, None),
        P("sx", "sy", None, None),
        P("sx", "sy"),
    )
    out_specs = (P("sx", "sy", None, None, None), P("sx", "sy", None, None, None))
    return jax.shard_map(local, mesh=mesh, in_specs=in_specs, out_specs=out_specs, check_vma=False)
```

time: 1520 us -> 273 us (0.18)
  waiting for transfers between devices: 776 us -> 22 us
  blocking collectives: 575 us -> 61.4 us
  matrix products: 38.5 us -> 0 us
  local copies, waits for them, and re-layouts: 42.4 us -> 75.2 us
  Pallas kernels: 0 us -> 32.7 us
  starting transfers between devices: 40.4 us -> 67.6 us
    psum x3 -> x0, waiting for transfers between devices: 730 us -> none  [local(): lax.psum(corner_gathered.reshape(coarse_order, load_cases), ('sx', 'sy'))]
    psum x8 -> x0, blocking collectives: 515 us -> none  [the longest x3 225 us: norm_sum(): return lax.psum(value, ('sx', 'sy'))]
    all_to_all x0 -> x3, blocking collectives: none -> 61.4 us  [the longest x2 35.9 us: along_sy(): lax.all_to_all(copies, 'sy', 0, 0, tiled=True, axis_index_groups=groups)]
    all_gather x3 -> x0, blocking collectives: 59.7 us -> none  [local(): solved = lax.all_gather(owned_rows, 'sx', axis=0, tiled=True)]
    unnamed x44 -> x130, local copies, waits for them, and re-layouts: 14 us -> 64.8 us
    dot_general x18 -> x0, matrix products: 38.5 us -> none  [the longest x3 21.7 us: local(): jnp.einsum('sij,sjr->sir', stiffness, sided_load, preferred_element_type=...]
    ppermute x12 -> x16, waiting for transfers between devices: 45.9 us -> 7.79 us  [shifted(): lax.ppermute(array, axis, [(i, (i + by) % count) for i in range(count)])]
    pallas_call x0 -> x16, Pallas kernels: none -> 32.7 us  [the longest x6 15.9 us: stiffness_call(): pl.pallas_call(body, grid=(steps,), in_specs=[whole(own.shape), whole(wes...]
  transfers between devices with their start and end apart: 15 -> 26, of which waited for: 12 -> 7; matrix products, arithmetic and copies ran while one was open for 3% -> 5% of each run, Pallas kernels for 0% -> 8%
where the time goes in v1:
time: 273 us; the launch traced here: 271 us
  local copies, waits for them, and re-layouts  75.2 us (28%)
  starting transfers between devices  67.6 us (25%)
  blocking collectives  61.4 us (22%)
  Pallas kernels  32.7 us (12%)
  waiting for transfers between devices  22 us (8%)
  other arithmetic  8.97 us (3%)
  between operations  3.12 us (1%)
    unnamed x130, local copies, waits for them, and re-layouts  64.8 us
    all_to_all x2, blocking collectives, along_sy(): lax.all_to_all(copies, 'sy', 0, 0, tiled=True, axis_index_groups=groups)  35.9 us
    ppermute x16, starting transfers between devices, shifted(): lax.ppermute(array, axis, [(i, (i + by) % count) for i in range(count)])  29 us
    all_to_all x1, blocking collectives, local(): lax.all_to_all(last.reshape(gx * gy, 1, cases), ('sx', 'sy'), 0, 0, tiled...  25.5 us
    pallas_call x6, Pallas kernels, stiffness_call(): pl.pallas_call(body, grid=(steps,), in_specs=[whole(own.shape), whole(wes...  15.9 us
    all_to_all x3, starting transfers between devices, coarse_solve(): return lax.all_to_all(send, 'sx', 0, 0, tiled=True)  12.6 us
    all_to_all x2, starting transfers between devices, along_sy(): lax.all_to_all(copies, 'sy', 0, 0, tiled=True, axis_index_groups=groups)  10.4 us
    all_to_all x2, waiting for transfers between devices, along_sy(): lax.all_to_all(copies, 'sy', 0, 0, tiled=True, axis_index_groups=groups)  8.86 us
  transfers between devices with their start and end apart: 26, of which 7 were waited for; matrix products, arithmetic and copies ran while one was open for 5% of the time, Pallas kernels for 8%

profile of v1, /device:TPU:1, one launch (start us, length us, event | category | flops | bytes accessed | tf_op | source)
XLA Modules:
  0.0 271.0 jit_solution(16639203211424130013)
XLA Ops:
  0.6 1.4 abs_reduce_fusion
  3.5 1.5 fusion
  7.5 7.6 %all-to-all-start = ((f32[16,96,128]{2,1,0:T(8,128)}), f32[16,96,128]{2,1,0:T(8,128)S(1)}, u32[]{:S(2)}, u32[]{:S(2)}) async-start(f32[16,96,128]{2,1,0:T(8,128)} %broadcast_in_dim.30), calls=%async_computation | async-start | bytes 1572864 | tf_op jit(solution)/shard_map/all_to_all | solution.py:365
  17.0 5.0 %collective-permute-start = (f32[2,12,384]{2,1,0:T(8,128)S(1)}, f32[2,12,384]{2,1,0:T(8,128)S(1)}, u32[]{:S(2)}, u32[]{:S(2)}) collective-permute-start(f32[2,12,384]{2,1,0:T(8,128)S(1)} %slice.92), channel_id=1, source_target_pairs={{0,240},{16,0},{32,16},{48,32},{64,48},{80,64},{96,80},{112,96},{1... | collective-permute-start | bytes 110600 | tf_op jit(solution)/shard_map/ppermute | solution.py:21
  22.0 1.3 reshape.75.gain_in
  23.3 5.0 %all-to-all-done = f32[16,96,128]{2,1,0:T(8,128)S(1)} async-done(((f32[16,96,128]{2,1,0:T(8,128)}), f32[16,96,128]{2,1,0:T(8,128)S(1)}, u32[]{:S(2)}, u32[]{:S(2)}) %all-to-all-start) | async-done | bytes 786464 | tf_op jit(solution)/shard_map/all_to_all | solution.py:365
  33.6 1.1 shard_map.104
  35.7 16.7 %all_to_all.45.same = f32[8,48,128]{2,1,0:T(8,128)S(1)} all-to-all(f32[8,48,128]{2,1,0:T(8,128)S(1)} %get-tuple-element.21), channel_id=1, replica_groups={{0,2,4,6,8,10,12,14},{1,3,5,7,9,11,13,15},{16,18,20,22,24,26,28,30},{17..., dimensions={0} | all-to-all | bytes 393216 | tf_op jit(solution)/shard_map/all_to_all | solution.py:27
  52.4 3.6 %collective-permute-start.2 = (f32[8,48,128]{2,1,0:T(8,128)S(1)}, f32[8,48,128]{2,1,0:T(8,128)S(1)}, u32[]{:S(2)}, u32[]{:S(2)}) collective-permute-start(f32[8,48,128]{2,1,0:T(8,128)S(1)} %all_to_all.45.same), channel_id=1, source_target_pairs={{0,1},{1,0},{2,3},{3,2},{4,5},{5,4},{6,7},{7,6},{8,9},{9,8},{10,11... | collective-permute-start | bytes 589832 | tf_op jit(solution)/shard_map/ppermute | solution.py:28
  57.7 2.0 shard_map.107
  59.7 19.2 %all_to_all.46.same = f32[8,96,128]{2,1,0:T(8,128)} all-to-all(f32[8,96,128]{2,1,0:T(8,128)} %shard_map.107), channel_id=1, replica_groups={{0,2,4,6,8,10,12,14},{1,3,5,7,9,11,13,15},{16,18,20,22,24,26,28,30},{17..., dimensions={0} | all-to-all | bytes 786432 | tf_op jit(solution)/shard_map/all_to_all | solution.py:27
  82.0 2.8 %shard_map.108.own = f32[256,128]{1,0:T(8,128)} custom-call(s32[16,128]{1,0:T(8,128)} %bitcast.72, s32[2]{0:T(128)} %pad_add_fusion.me, f32[8,96,128]{2,1,0:T(8,128)} %all_to_all.46.same, f32[8,96,128]{2,1,0:T(8,128)} %collective-permute-done.7.other), custom_call_target="tpu_custom_call" | custom-call | tf_op jit(solution)/shard_map/pallas_call | solution.py:429
  84.8 4.1 %collective-permute-start.9 = (f32[256,128]{1,0:T(8,128)}, f32[256,128]{1,0:T(8,128)S(1)}, u32[]{:S(2)}, u32[]{:S(2)}) collective-permute-start(f32[256,128]{1,0:T(8,128)} %shard_map.108.own), channel_id=1, source_target_pairs={{0,240},{16,0},{32,16},{48,32},{64,48},{80,64},{96,80},{112,96},{1... | collective-permute-start | bytes 393224 | tf_op jit(solution)/shard_map/ppermute | solution.py:21
  90.6 3.9 %collective-permute-done.3.west = f32[2,384,128]{2,1,0:T(8,128)S(1)} collective-permute-done((f32[2,384,128]{2,1,0:T(8,128)}, f32[2,384,128]{2,1,0:T(8,128)S(1)}, u32[]{:S(2)}, u32[]{:S(2)}) %collective-permute-start.3) | collective-permute-done | bytes 393248 | tf_op jit(solution)/shard_map/ppermute | solution.py:21
  95.2 3.7 %copy-done = bf16[1,2,1536,1536]{3,2,1,0:T(8,128)(2,1)S(1)} copy-done((bf16[1,2,1536,1536]{3,2,1,0:T(8,128)(2,1)S(1)}, bf16[1,2,1536,1536]{3,2,1,0:T(8,128)(2,1)}, u32[]{:S(2)}) %copy-start) | copy-done | bytes 9437208
  100.8 1.8 shard_map.106
  107.1 4.2 %all-to-all-start.3 = ((f32[16,48,128]{2,1,0:T(8,128)}), f32[16,48,128]{2,1,0:T(8,128)}, u32[]{:S(2)}, u32[]{:S(2)}) async-start(f32[16,48,128]{2,1,0:T(8,128)} %copy-done.28), calls=%async_computation.3 | async-start | bytes 786432 | tf_op jit(solution)/shard_map/all_to_all | solution.py:442
  112.3 3.7 %copy-done.1 = bf16[1,2,1536,1536]{3,2,1,0:T(8,128)(2,1)S(1)} copy-done((bf16[1,2,1536,1536]{3,2,1,0:T(8,128)(2,1)S(1)}, bf16[1,2,1536,1536]{3,2,1,0:T(8,128)(2,1)}, u32[]{:S(2)}) %copy-start.1) | copy-done | bytes 9437208
  117.9 2.8 %shard_map.105.part = f32[4,384,128]{2,1,0:T(8,128)S(1)} custom-call(f32[4,384,128]{2,1,0:T(8,128)S(1)} %get-tuple-element.22.own.previous.w0, f32[2,384,128]{2,1,0:T(8,128)S(1)} %copy-done.24, f32[384,128]{1,0:T(8,128)S(1)} %copy-done.48, bf16[8,384,1536]{2,1,0:T(8,128)(2,1)S(1)} %bitcast.58), custom_call_target="tpu_custom_call" | custom-call | flops 1509949440 | bytes 7864320 | tf_op jit(solution)/shard_map/pallas_call | solution.py:178
  125.7 1.8 shard_map.110
  129.1 4.0 %all-to-all-start.4 = ((f32[8,48,128]{2,1,0:T(8,128)}), f32[8,48,128]{2,1,0:T(8,128)}, u32[]{:S(2)}, u32[]{:S(2)}) async-start(f32[8,48,128]{2,1,0:T(8,128)} %copy-done.60), calls=%async_computation.4 | async-start | bytes 393216 | tf_op jit(solution)/shard_map/all_to_all | solution.py:27
  133.9 1.5 collective-permute-start.10
  135.3 3.4 %collective-permute-start.11 = (f32[384,128]{1,0:T(8,128)S(1)}, f32[384,128]{1,0:T(8,128)S(1)}, u32[]{:S(2)}, u32[]{:S(2)}) collective-permute-start(f32[384,128]{1,0:T(8,128)S(1)} %slice_bitcast_fusion.7), channel_id=1, source_target_pairs={{0,1},{1,2},{2,3},{3,4},{4,5},{5,6},{6,7},{7,8},{8,9},{9,10},{10,1... | collective-permute-start | bytes 589832 | tf_op jit(solution)/shard_map/ppermute | solution.py:21
  138.8 3.1 %all-to-all-done.4.same = f32[8,48,128]{2,1,0:T(8,128)} async-done(((f32[8,48,128]{2,1,0:T(8,128)}), f32[8,48,128]{2,1,0:T(8,128)}, u32[]{:S(2)}, u32[]{:S(2)}) %all-to-all-start.4) | async-done | bytes 196640 | tf_op jit(solution)/shard_map/all_to_all | solution.py:27
  141.9 3.1 %collective-permute-start.14 = (f32[8,48,128]{2,1,0:T(8,128)}, f32[8,48,128]{2,1,0:T(8,128)S(1)}, u32[]{:S(2)}, u32[]{:S(2)}) collective-permute-start(f32[8,48,128]{2,1,0:T(8,128)} %all-to-all-done.4.same), channel_id=1, source_target_pairs={{0,1},{1,0},{2,3},{3,2},{4,5},{5,4},{6,7},{7,6},{8,9},{9,8},{10,11... | collective-permute-start | bytes 589832 | tf_op jit(solution)/shard_map/ppermute | solution.py:28
  147.0 3.7 %copy-done.2 = bf16[1,2,1536,1536]{3,2,1,0:T(8,128)(2,1)S(1)} copy-done((bf16[1,2,1536,1536]{3,2,1,0:T(8,128)(2,1)S(1)}, bf16[1,2,1536,1536]{3,2,1,0:T(8,128)(2,1)}, u32[]{:S(2)}) %copy-start.2) | copy-done | bytes 9437208
  152.6 1.8 shard_map.112
  155.2 4.4 %collective-permute-start.12 = (f32[2,384,128]{2,1,0:T(8,128)}, f32[2,384,128]{2,1,0:T(8,128)}, u32[]{:S(2)}, u32[]{:S(2)}) collective-permute-start(f32[2,384,128]{2,1,0:T(8,128)} %slice.103), channel_id=1, source_target_pairs={{0,240},{16,0},{32,16},{48,32},{64,48},{80,64},{96,80},{112,96},{1... | collective-permute-start | bytes 1179656 | tf_op jit(solution)/shard_map/ppermute | solution.py:21
  163.2 1.7 shard_map.113
  165.7 4.2 %all-to-all-start.5 = ((f32[16,48,128]{2,1,0:T(8,128)}), f32[16,48,128]{2,1,0:T(8,128)}, u32[]{:S(2)}, u32[]{:S(2)}) async-start(f32[16,48,128]{2,1,0:T(8,128)} %copy-done.30), calls=%async_computation.5 | async-start | bytes 786432 | tf_op jit(solution)/shard_map/all_to_all | solution.py:442
  170.2 3.7 %copy-done.3 = bf16[1,2,1536,1536]{3,2,1,0:T(8,128)(2,1)S(1)} copy-done((bf16[1,2,1536,1536]{3,2,1,0:T(8,128)(2,1)S(1)}, bf16[1,2,1536,1536]{3,2,1,0:T(8,128)(2,1)}, u32[]{:S(2)}) %copy-start.3) | copy-done | bytes 9437208
  175.8 2.8 %shard_map.111.part = f32[4,384,128]{2,1,0:T(8,128)S(1)} custom-call(f32[4,384,128]{2,1,0:T(8,128)S(1)} %get-tuple-element.27.own.previous.w1, f32[2,384,128]{2,1,0:T(8,128)S(1)} %copy-done.27, f32[384,128]{1,0:T(8,128)S(1)} %copy-done.51, bf16[8,384,1536]{2,1,0:T(8,128)(2,1)S(1)} %bitcast.60), custom_call_target="tpu_custom_call" | custom-call | flops 1509949440 | bytes 7864320 | tf_op jit(solution)/shard_map/pallas_call | solution.py:178
  183.4 1.8 shard_map.114
  186.8 6.3 %all-to-all-start.6 = ((f32[8,48,128]{2,1,0:T(8,128)}), f32[8,48,128]{2,1,0:T(8,128)}, u32[]{:S(2)}, u32[]{:S(2)}) async-start(f32[8,48,128]{2,1,0:T(8,128)} %copy-done.61), calls=%async_computation.6 | async-start | bytes 393216 | tf_op jit(solution)/shard_map/all_to_all | solution.py:27
  193.9 1.5 collective-permute-start.15
  196.0 2.2 collective-permute-start.16
  198.2 5.8 %all-to-all-done.6.same = f32[8,48,128]{2,1,0:T(8,128)} async-done(((f32[8,48,128]{2,1,0:T(8,128)}), f32[8,48,128]{2,1,0:T(8,128)}, u32[]{:S(2)}, u32[]{:S(2)}) %all-to-all-start.6) | async-done | bytes 196640 | tf_op jit(solution)/shard_map/all_to_all | solution.py:27
  204.9 3.3 %collective-permute-done.15.west = f32[2,384,128]{2,1,0:T(8,128)} collective-permute-done((f32[2,384,128]{2,1,0:T(8,128)}, f32[2,384,128]{2,1,0:T(8,128)}, u32[]{:S(2)}, u32[]{:S(2)}) %collective-permute-start.15) | collective-permute-done | bytes 393248 | tf_op jit(solution)/shard_map/ppermute | solution.py:21
  208.1 3.7 %copy-done.4 = bf16[1,2,1536,1536]{3,2,1,0:T(8,128)(2,1)S(1)} copy-done((bf16[1,2,1536,1536]{3,2,1,0:T(8,128)(2,1)S(1)}, bf16[1,2,1536,1536]{3,2,1,0:T(8,128)(2,1)}, u32[]{:S(2)}) %copy-start.4) | copy-done | bytes 9437208
  211.8 2.9 %shard_map.116 = f32[3,384,128]{2,1,0:T(8,128)S(1)} custom-call(f32[4,384,128]{2,1,0:T(8,128)S(1)} %get-tuple-element.30.own.previous.w2, f32[2,384,128]{2,1,0:T(8,128)} %collective-permute-done.15.west, f32[384,128]{1,0:T(8,128)} %collective-permute-done.16.below, bf16[8,384,1536]{2,1,0:T(8,128)(2,1)S(1)} %bitcast.61), custom_call_target="tpu_custom_call" | custom-call | flops 905969664 | bytes 5505024 | tf_op jit(solution)/shard_map/pallas_call | solution.py:178
  216.3 1.6 collective-permute-start.17
  218.0 1.7 shard_map.117
  220.5 4.2 %all-to-all-start.7 = ((f32[16,48,128]{2,1,0:T(8,128)}), f32[16,48,128]{2,1,0:T(8,128)}, u32[]{:S(2)}, u32[]{:S(2)}) async-start(f32[16,48,128]{2,1,0:T(8,128)} %copy-done.29), calls=%async_computation.7 | async-start | bytes 786432 | tf_op jit(solution)/shard_map/all_to_all | solution.py:442
  226.8 3.7 %copy-done.5 = bf16[1,2,1536,1536]{3,2,1,0:T(8,128)(2,1)S(1)} copy-done((bf16[1,2,1536,1536]{3,2,1,0:T(8,128)(2,1)S(1)}, bf16[1,2,1536,1536]{3,2,1,0:T(8,128)(2,1)}, u32[]{:S(2)}) %copy-start.5) | copy-done | bytes 9437208
  230.4 3.9 %shard_map.115.part = f32[4,384,128]{2,1,0:T(8,128)S(1)} custom-call(f32[4,384,128]{2,1,0:T(8,128)S(1)} %get-tuple-element.30.own.previous.w2, f32[2,384,128]{2,1,0:T(8,128)} %collective-permute-done.15.west, f32[384,128]{1,0:T(8,128)} %collective-permute-done.16.below, bf16[8,384,1536]{2,1,0:T(8,128)(2,1)S(1)} %bitcast.62), custom_call_target="tpu_custom_call" | custom-call | flops 1509949440 | bytes 7864320 | tf_op jit(solution)/shard_map/pallas_call | solution.py:178
  239.1 1.5 shard_map.118
  240.6 25.5 %all_to_all.47 = f32[256,1,128]{2,1,0:T(1,128)S(1)} all-to-all(f32[256,1,128]{2,1,0:T(1,128)S(1)} %bitcast.68), channel_id=1, replica_groups=mesh['sx'=16,'sy'=16] {'sx','sy'}, dimensions={0} | all-to-all | bytes 262144 | tf_op jit(solution)/shard_map/all_to_all | solution.py:458
  269.5 1.5 shard_map.119
  (190 shorter events, 66.4 us)
Async XLA Ops:
  7.5 20.8 %all-to-all-start = ((f32[16,96,128]{2,1,0:T(8,128)}), f32[16,96,128]{2,1,0:T(8,128)S(1)}, u32[]{:S(2)}, u32[]{:S(2)}) async-start(f32[16,96,128]{2,1,0:T(8,128)} %broadcast_in_dim.30), calls=%async_computation | async-start | bytes 1572864 | tf_op jit(solution)/shard_map/all_to_all | solution.py:365
  16.0 14.0 %copy-start.37 = (f32[2,12,1536]{2,1,0:T(8,128)}, f32[2,12,1536]{2,1,0:T(8,128)S(1)}, u32[]{:S(2)}) copy-start(f32[2,12,1536]{2,1,0:T(8,128)S(1)} %bitcast_convert_fusion.basis) | copy-start | bytes 442372
  16.0 13.9 %collective-permute-start.1 = (f32[12,384]{1,0:T(8,128)S(1)}, f32[12,384]{1,0:T(8,128)S(1)}, u32[]{:S(2)}, u32[]{:S(2)}) collective-permute-start(f32[12,384]{1,0:T(8,128)S(1)} %slice_bitcast_fusion.9), channel_id=1, source_target_pairs={{0,15},{1,0},{2,1},{3,2},{4,3},{5,4},{6,5},{7,6},{8,7},{9,8},{10,9... | collective-permute-start | bytes 55304 | tf_op jit(solution)/shard_map/ppermute | solution.py:21
  17.0 13.0 %collective-permute-start = (f32[2,12,384]{2,1,0:T(8,128)S(1)}, f32[2,12,384]{2,1,0:T(8,128)S(1)}, u32[]{:S(2)}, u32[]{:S(2)}) collective-permute-start(f32[2,12,384]{2,1,0:T(8,128)S(1)} %slice.92), channel_id=1, source_target_pairs={{0,240},{16,0},{32,16},{48,32},{64,48},{80,64},{96,80},{112,96},{1... | collective-permute-start | bytes 110600 | tf_op jit(solution)/shard_map/ppermute | solution.py:21
  28.3 1.7 copy-start.64
  30.9 1.1 copy-start.45
  35.7 88.0 %copy-start.6 = (f32[4,384,128]{2,1,0:T(8,128)}, f32[4,384,128]{2,1,0:T(8,128)S(1)}, u32[]{:S(2)}) copy-start(f32[4,384,128]{2,1,0:T(8,128)S(1)} %get-tuple-element.25.gain) | copy-start | bytes 2359300
  52.4 4.7 %collective-permute-start.2 = (f32[8,48,128]{2,1,0:T(8,128)S(1)}, f32[8,48,128]{2,1,0:T(8,128)S(1)}, u32[]{:S(2)}, u32[]{:S(2)}) collective-permute-start(f32[8,48,128]{2,1,0:T(8,128)S(1)} %all_to_all.45.same), channel_id=1, source_target_pairs={{0,1},{1,0},{2,3},{3,2},{4,5},{5,4},{6,7},{7,6},{8,9},{9,8},{10,11... | collective-permute-start | bytes 589832 | tf_op jit(solution)/shard_map/ppermute | solution.py:28
  57.0 22.4 %copy-start.52 = (f32[8,48,128]{2,1,0:T(8,128)}, f32[8,48,128]{2,1,0:T(8,128)S(1)}, u32[]{:S(2)}) copy-start(f32[8,48,128]{2,1,0:T(8,128)S(1)} %collective-permute-done.2.other) | copy-start | bytes 589828
  79.0 3.1 %collective-permute-start.7 = (f32[8,96,128]{2,1,0:T(8,128)}, f32[8,96,128]{2,1,0:T(8,128)}, u32[]{:S(2)}, u32[]{:S(2)}) collective-permute-start(f32[8,96,128]{2,1,0:T(8,128)} %all_to_all.46.same), channel_id=1, source_target_pairs={{0,1},{1,0},{2,3},{3,2},{4,5},{5,4},{6,7},{7,6},{8,9},{9,8},{10,11... | collective-permute-start | bytes 1179656 | tf_op jit(solution)/shard_map/ppermute | solution.py:28
  80.2 14.2 %collective-permute-start.3 = (f32[2,384,128]{2,1,0:T(8,128)}, f32[2,384,128]{2,1,0:T(8,128)S(1)}, u32[]{:S(2)}, u32[]{:S(2)}) collective-permute-start(f32[2,384,128]{2,1,0:T(8,128)} %slice_bitcast_fusion.2), channel_id=1, source_target_pairs={{0,16},{16,32},{32,48},{48,64},{64,80},{80,96},{96,112},{112,128},... | collective-permute-start | bytes 1179656 | tf_op jit(solution)/shard_map/ppermute | solution.py:21
  81.6 8.3 %collective-permute-start.4 = (f32[384,128]{1,0:T(8,128)}, f32[384,128]{1,0:T(8,128)S(1)}, u32[]{:S(2)}, u32[]{:S(2)}) collective-permute-start(f32[384,128]{1,0:T(8,128)} %slice_bitcast_fusion.8), channel_id=1, source_target_pairs={{0,1},{1,2},{2,3},{3,4},{4,5},{5,6},{6,7},{7,8},{8,9},{9,10},{10,1... | collective-permute-start | bytes 589832 | tf_op jit(solution)/shard_map/ppermute | solution.py:21
  84.8 19.5 %copy-start.16 = (f32[256,128]{1,0:T(8,128)S(1)}, f32[256,128]{1,0:T(8,128)}, u32[]{:S(2)}) copy-start(f32[256,128]{1,0:T(8,128)} %shard_map.108.own) | copy-start | bytes 393220
  84.8 19.5 %collective-permute-start.9 = (f32[256,128]{1,0:T(8,128)}, f32[256,128]{1,0:T(8,128)S(1)}, u32[]{:S(2)}, u32[]{:S(2)}) collective-permute-start(f32[256,128]{1,0:T(8,128)} %shard_map.108.own), channel_id=1, source_target_pairs={{0,240},{16,0},{32,16},{48,32},{64,48},{80,64},{96,80},{112,96},{1... | collective-permute-start | bytes 393224 | tf_op jit(solution)/shard_map/ppermute | solution.py:21
  88.9 15.3 %collective-permute-start.8 = (f32[256,128]{1,0:T(8,128)}, f32[256,128]{1,0:T(8,128)S(1)}, u32[]{:S(2)}, u32[]{:S(2)}) collective-permute-start(f32[256,128]{1,0:T(8,128)} %shard_map.108.own), channel_id=1, source_target_pairs={{0,16},{16,32},{32,48},{48,64},{64,80},{80,96},{96,112},{112,128},... | collective-permute-start | bytes 393224 | tf_op jit(solution)/shard_map/ppermute | solution.py:21
  89.9 14.4 %copy-start.19 = (f32[128,256]{1,0:T(8,128)}, f32[128,256]{1,0:T(8,128)S(1)}, u32[]{:S(2)}) copy-start(f32[128,256]{1,0:T(8,128)S(1)} %dynamic-slice_bitcast_fusion.lanes) | copy-start | bytes 393220
  95.2 3.7 %copy-start = (bf16[1,2,1536,1536]{3,2,1,0:T(8,128)(2,1)S(1)}, bf16[1,2,1536,1536]{3,2,1,0:T(8,128)(2,1)}, u32[]{:S(2)}) copy-start(bf16[1,2,1536,1536]{3,2,1,0:T(8,128)(2,1)} %param.13) | copy-start | bytes 28311556
  100.8 3.5 %copy-start.53 = (f32[8,48,128]{2,1,0:T(8,128)S(1)}, f32[8,48,128]{2,1,0:T(8,128)}, u32[]{:S(2)}) copy-start(f32[8,48,128]{2,1,0:T(8,128)} %copy-done.52) | copy-start | bytes 589828
  103.4 20.2 %collective-permute-start.5 = (f32[2,384,128]{2,1,0:T(8,128)}, f32[2,384,128]{2,1,0:T(8,128)}, u32[]{:S(2)}, u32[]{:S(2)}) collective-permute-start(f32[2,384,128]{2,1,0:T(8,128)} %slice.100), channel_id=1, source_target_pairs={{0,240},{16,0},{32,16},{48,32},{64,48},{80,64},{96,80},{112,96},{1... | collective-permute-start | bytes 1179656 | tf_op jit(solution)/shard_map/ppermute | solution.py:21
  107.1 16.5 %all-to-all-start.3 = ((f32[16,48,128]{2,1,0:T(8,128)}), f32[16,48,128]{2,1,0:T(8,128)}, u32[]{:S(2)}, u32[]{:S(2)}) async-start(f32[16,48,128]{2,1,0:T(8,128)} %copy-done.28), calls=%async_computation.3 | async-start | bytes 786432 | tf_op jit(solution)/shard_map/all_to_all | solution.py:442
  111.4 11.6 %collective-permute-start.6 = (f32[384,128]{1,0:T(8,128)S(1)}, f32[384,128]{1,0:T(8,128)S(1)}, u32[]{:S(2)}, u32[]{:S(2)}) collective-permute-start(f32[384,128]{1,0:T(8,128)S(1)} %slice_bitcast_fusion.5), channel_id=1, source_target_pairs={{0,15},{1,0},{2,1},{3,2},{4,3},{5,4},{6,5},{7,6},{8,7},{9,8},{10,9... | collective-permute-start | bytes 589832 | tf_op jit(solution)/shard_map/ppermute | solution.py:21
  112.3 3.7 %copy-start.1 = (bf16[1,2,1536,1536]{3,2,1,0:T(8,128)(2,1)S(1)}, bf16[1,2,1536,1536]{3,2,1,0:T(8,128)(2,1)}, u32[]{:S(2)}) copy-start(bf16[1,2,1536,1536]{3,2,1,0:T(8,128)(2,1)} %param.13) | copy-start | bytes 28311556
  123.6 1.1 copy-start.10
  129.1 12.8 %all-to-all-start.4 = ((f32[8,48,128]{2,1,0:T(8,128)}), f32[8,48,128]{2,1,0:T(8,128)}, u32[]{:S(2)}, u32[]{:S(2)}) async-start(f32[8,48,128]{2,1,0:T(8,128)} %copy-done.60), calls=%async_computation.4 | async-start | bytes 393216 | tf_op jit(solution)/shard_map/all_to_all | solution.py:27
  133.9 12.4 %collective-permute-start.10 = (f32[2,384,128]{2,1,0:T(8,128)}, f32[2,384,128]{2,1,0:T(8,128)S(1)}, u32[]{:S(2)}, u32[]{:S(2)}) collective-permute-start(f32[2,384,128]{2,1,0:T(8,128)} %slice_bitcast_fusion.1), channel_id=1, source_target_pairs={{0,16},{16,32},{32,48},{48,64},{64,80},{80,96},{96,112},{112,128},... | collective-permute-start | bytes 1179656 | tf_op jit(solution)/shard_map/ppermute | solution.py:21
  135.3 9.6 %collective-permute-start.11 = (f32[384,128]{1,0:T(8,128)S(1)}, f32[384,128]{1,0:T(8,128)S(1)}, u32[]{:S(2)}, u32[]{:S(2)}) collective-permute-start(f32[384,128]{1,0:T(8,128)S(1)} %slice_bitcast_fusion.7), channel_id=1, source_target_pairs={{0,1},{1,2},{2,3},{3,4},{4,5},{5,6},{6,7},{7,8},{8,9},{9,10},{10,1... | collective-permute-start | bytes 589832 | tf_op jit(solution)/shard_map/ppermute | solution.py:21
  141.9 17.7 %collective-permute-start.14 = (f32[8,48,128]{2,1,0:T(8,128)}, f32[8,48,128]{2,1,0:T(8,128)S(1)}, u32[]{:S(2)}, u32[]{:S(2)}) collective-permute-start(f32[8,48,128]{2,1,0:T(8,128)} %all-to-all-done.4.same), channel_id=1, source_target_pairs={{0,1},{1,0},{2,3},{3,2},{4,5},{5,4},{6,7},{7,6},{8,9},{9,8},{10,11... | collective-permute-start | bytes 589832 | tf_op jit(solution)/shard_map/ppermute | solution.py:28
  147.0 3.7 %copy-start.2 = (bf16[1,2,1536,1536]{3,2,1,0:T(8,128)(2,1)S(1)}, bf16[1,2,1536,1536]{3,2,1,0:T(8,128)(2,1)}, u32[]{:S(2)}) copy-start(bf16[1,2,1536,1536]{3,2,1,0:T(8,128)(2,1)} %param.13) | copy-start | bytes 28311556
  155.2 25.0 %collective-permute-start.12 = (f32[2,384,128]{2,1,0:T(8,128)}, f32[2,384,128]{2,1,0:T(8,128)}, u32[]{:S(2)}, u32[]{:S(2)}) collective-permute-start(f32[2,384,128]{2,1,0:T(8,128)} %slice.103), channel_id=1, source_target_pairs={{0,240},{16,0},{32,16},{48,32},{64,48},{80,64},{96,80},{112,96},{1... | collective-permute-start | bytes 1179656 | tf_op jit(solution)/shard_map/ppermute | solution.py:21
  165.7 14.5 %all-to-all-start.5 = ((f32[16,48,128]{2,1,0:T(8,128)}), f32[16,48,128]{2,1,0:T(8,128)}, u32[]{:S(2)}, u32[]{:S(2)}) async-start(f32[16,48,128]{2,1,0:T(8,128)} %copy-done.30), calls=%async_computation.5 | async-start | bytes 786432 | tf_op jit(solution)/shard_map/all_to_all | solution.py:442
  169.9 9.6 %collective-permute-start.13 = (f32[384,128]{1,0:T(8,128)S(1)}, f32[384,128]{1,0:T(8,128)S(1)}, u32[]{:S(2)}, u32[]{:S(2)}) collective-permute-start(f32[384,128]{1,0:T(8,128)S(1)} %slice_bitcast_fusion.4), channel_id=1, source_target_pairs={{0,15},{1,0},{2,1},{3,2},{4,3},{5,4},{6,5},{7,6},{8,7},{9,8},{10,9... | collective-permute-start | bytes 589832 | tf_op jit(solution)/shard_map/ppermute | solution.py:21
  170.2 3.7 %copy-start.3 = (bf16[1,2,1536,1536]{3,2,1,0:T(8,128)(2,1)S(1)}, bf16[1,2,1536,1536]{3,2,1,0:T(8,128)(2,1)}, u32[]{:S(2)}) copy-start(bf16[1,2,1536,1536]{3,2,1,0:T(8,128)(2,1)} %param.13) | copy-start | bytes 28311556
  180.2 1.1 copy-start.7
  186.8 17.2 %all-to-all-start.6 = ((f32[8,48,128]{2,1,0:T(8,128)}), f32[8,48,128]{2,1,0:T(8,128)}, u32[]{:S(2)}, u32[]{:S(2)}) async-start(f32[8,48,128]{2,1,0:T(8,128)} %copy-done.61), calls=%async_computation.6 | async-start | bytes 393216 | tf_op jit(solution)/shard_map/all_to_all | solution.py:27
  193.9 14.3 %collective-permute-start.15 = (f32[2,384,128]{2,1,0:T(8,128)}, f32[2,384,128]{2,1,0:T(8,128)}, u32[]{:S(2)}, u32[]{:S(2)}) collective-permute-start(f32[2,384,128]{2,1,0:T(8,128)} %slice_bitcast_fusion), channel_id=1, source_target_pairs={{0,16},{16,32},{32,48},{48,64},{64,80},{80,96},{96,112},{112,128},... | collective-permute-start | bytes 1179656 | tf_op jit(solution)/shard_map/ppermute | solution.py:21
  196.0 8.8 %collective-permute-start.16 = (f32[384,128]{1,0:T(8,128)}, f32[384,128]{1,0:T(8,128)}, u32[]{:S(2)}, u32[]{:S(2)}) collective-permute-start(f32[384,128]{1,0:T(8,128)} %slice_bitcast_fusion.6), channel_id=1, source_target_pairs={{0,1},{1,2},{2,3},{3,4},{4,5},{5,6},{6,7},{7,8},{8,9},{9,10},{10,1... | collective-permute-start | bytes 589832 | tf_op jit(solution)/shard_map/ppermute | solution.py:21
  204.0 14.0 %collective-permute-start.19 = (f32[8,48,128]{2,1,0:T(8,128)}, f32[8,48,128]{2,1,0:T(8,128)S(1)}, u32[]{:S(2)}, u32[]{:S(2)}) collective-permute-start(f32[8,48,128]{2,1,0:T(8,128)} %all-to-all-done.6.same), channel_id=1, source_target_pairs={{0,1},{1,0},{2,3},{3,2},{4,5},{5,4},{6,7},{7,6},{8,9},{9,8},{10,11... | collective-permute-start | bytes 589832 | tf_op jit(solution)/shard_map/ppermute | solution.py:28
  208.1 3.7 %copy-start.4 = (bf16[1,2,1536,1536]{3,2,1,0:T(8,128)(2,1)S(1)}, bf16[1,2,1536,1536]{3,2,1,0:T(8,128)(2,1)}, u32[]{:S(2)}) copy-start(bf16[1,2,1536,1536]{3,2,1,0:T(8,128)(2,1)} %param.13) | copy-start | bytes 28311556
  211.8 6.1 %copy-start.18 = (f32[256,128]{1,0:T(8,128)S(1)}, f32[256,128]{1,0:T(8,128)}, u32[]{:S(2)}) copy-start(f32[256,128]{1,0:T(8,128)} %shard_map.108.own) | copy-start | bytes 393220
  211.8 6.1 %copy-start.21 = (f32[128,256]{1,0:T(8,128)S(1)}, f32[128,256]{1,0:T(8,128)}, u32[]{:S(2)}) copy-start(f32[128,256]{1,0:T(8,128)} %copy-done.19) | copy-start | bytes 393220
  211.8 6.1 %copy-start.33 = (f32[256,128]{1,0:T(8,128)S(1)}, f32[256,128]{1,0:T(8,128)}, u32[]{:S(2)}) copy-start(f32[256,128]{1,0:T(8,128)} %copy-done.31) | copy-start | bytes 393220
  211.8 6.2 %copy-start.36 = (f32[256,128]{1,0:T(8,128)S(1)}, f32[256,128]{1,0:T(8,128)}, u32[]{:S(2)}) copy-start(f32[256,128]{1,0:T(8,128)} %copy-done.34) | copy-start | bytes 393220
  216.3 19.5 %collective-permute-start.17 = (f32[2,384,128]{2,1,0:T(8,128)}, f32[2,384,128]{2,1,0:T(8,128)}, u32[]{:S(2)}, u32[]{:S(2)}) collective-permute-start(f32[2,384,128]{2,1,0:T(8,128)} %slice.106), channel_id=1, source_target_pairs={{0,240},{16,0},{32,16},{48,32},{64,48},{80,64},{96,80},{112,96},{1... | collective-permute-start | bytes 1179656 | tf_op jit(solution)/shard_map/ppermute | solution.py:21
  220.5 15.4 %all-to-all-start.7 = ((f32[16,48,128]{2,1,0:T(8,128)}), f32[16,48,128]{2,1,0:T(8,128)}, u32[]{:S(2)}, u32[]{:S(2)}) async-start(f32[16,48,128]{2,1,0:T(8,128)} %copy-done.29), calls=%async_computation.7 | async-start | bytes 786432 | tf_op jit(solution)/shard_map/all_to_all | solution.py:442
  225.6 9.6 %collective-permute-start.18 = (f32[384,128]{1,0:T(8,128)S(1)}, f32[384,128]{1,0:T(8,128)S(1)}, u32[]{:S(2)}, u32[]{:S(2)}) collective-permute-start(f32[384,128]{1,0:T(8,128)S(1)} %slice_bitcast_fusion.3), channel_id=1, source_target_pairs={{0,15},{1,0},{2,1},{3,2},{4,3},{5,4},{6,5},{7,6},{8,7},{9,8},{10,9... | collective-permute-start | bytes 589832 | tf_op jit(solution)/shard_map/ppermute | solution.py:21
  226.8 3.7 %copy-start.5 = (bf16[1,2,1536,1536]{3,2,1,0:T(8,128)(2,1)S(1)}, bf16[1,2,1536,1536]{3,2,1,0:T(8,128)(2,1)}, u32[]{:S(2)}) copy-start(bf16[1,2,1536,1536]{3,2,1,0:T(8,128)(2,1)} %param.13) | copy-start | bytes 28311556
  235.9 1.1 copy-start.8
  266.1 1.1 copy-start.40
  (43 other events, 37.1 us)

commit v2 on v1

v2 whole, which is shorter than its diff:
```python
import functools
import math

import numpy as np
import jax
import jax.numpy as jnp
from jax import lax
from jax.experimental import pallas as pl
from jax.experimental.pallas import tpu as pltpu
from jax.sharding import PartitionSpec as P

CS = 3
NEAR = 16
ROWS = 3 * NEAR
F32, BF16 = jnp.float32, jnp.bfloat16
SMEM = pl.BlockSpec(memory_space=pltpu.SMEM)


def shifted(array, axis, by):
    count = lax.axis_size(axis)
    return lax.ppermute(array, axis, [(i, (i + by) % count) for i in range(count)])


def along_sy(copies):
    count = lax.axis_size("sy")
    groups = [[2 * z + core for z in range(count // 2)] for core in range(2)]
    same = lax.all_to_all(copies, "sy", 0, 0, tiled=True, axis_index_groups=groups)
    return same, lax.ppermute(same, "sy", [(i, i ^ 1) for i in range(count)])


def kernel_call(body, outs, operands, scalars=0, blocks=None, scratch=()):
    whole = lambda array: pl.BlockSpec(array.shape, lambda t: (0,) * len(array.shape))
    specs = [SMEM] * scalars + [whole(array) for array in operands[scalars:]]
    if blocks is not None:
        specs.append(pl.BlockSpec(memory_space=pltpu.HBM))
        operands = tuple(operands) + (blocks,)
    several = isinstance(outs, tuple)
    moved = sum(4 * math.prod(array.shape) for array in operands) + sum(
        4 * math.prod(array.shape) for array in (outs if several else (outs,))
    )
    return pl.pallas_call(
        body,
        grid=(1,),
        in_specs=specs,
        out_specs=tuple(whole(array) for array in outs) if several else whole(outs),
        out_shape=outs,
        scratch_shapes=list(scratch),
        compiler_params=pltpu.CompilerParams(vmem_limit_bytes=32 * 2**20),
        cost_estimate=pl.CostEstimate(flops=4 * moved, bytes_accessed=moved, transcendentals=0),
    )(*operands)


def split(value):
    high = value.astype(BF16)
    return high, (value - high.astype(F32)).astype(BF16)


def halves(value):
    return jnp.concatenate(split(value), 1)


def multiply(first, second):
    return jnp.dot(first, second, preferred_element_type=F32)


def place_matrices():
    place = [(0, 0), (-1, 0), (0, -1), (-1, -1)]
    out = np.zeros((4, ROWS, 32), np.float32)
    for s in range(2):
        for e in range(2):
            for k, (di, dj) in enumerate(place):
                for c in range(CS):
                    out[2 * s + e, (1 + di) * NEAR + (1 + s + dj) * CS + c, k * CS + c] += 1
                    row = (1 + di + (1 - e)) * NEAR + (1 + s + dj + e) * CS + c
                    out[2 * s + e, row, 16 + k * CS + c] -= 1
    return out


def lane_matrices(gy):
    out = np.zeros((2, 128, gy * NEAR), np.float32)
    for core in range(2):
        for slot in range(gy):
            z, other = slot % (gy // 2), slot // (gy // 2)
            source = 2 * z + (core ^ other)
            for jj in range(4):
                for c in range(CS):
                    j = (2 * source - 1 + jj) % (2 * gy)
                    out[core, j * CS + c, slot * NEAR + jj * CS + c] = 1
    return out


def message_to(out_ref, basis_ref, parts, extra):
    got = multiply(basis_ref[...], parts[...].reshape(basis_ref.shape[1], parts.shape[2]))
    cases = got.shape[1] // 2
    rows = got[:ROWS, :cases] + got[:ROWS, cases:] + got[ROWS:, :cases]
    index = lax.broadcasted_iota(jnp.int32, rows.shape, 0)
    for k, row in enumerate(extra):
        rows = jnp.where(index == NEAR - 4 + k, row, rows)
    for copy in range(out_ref.shape[0]):
        out_ref[copy] = rows


def column_sum(value):
    return jnp.sum(value, axis=0, keepdims=True)


def wide_body(me, corner, coarse, out):
    block = coarse.shape[0]
    count = out.shape[0]
    lane = lax.broadcasted_iota(jnp.int32, (block, out.shape[2] - block), 1)
    spare = jnp.where(lane == 2 * me[0], corner[0, 0], 0) + jnp.where(lane == 2 * me[0] + 1, corner[1, 0], 0)
    wide = jnp.concatenate([coarse[...], spare.astype(F32)], 1)
    for copy in range(count):
        out[copy] = wide


def begin_body(count, corner, rhs, gain_in, basis, east, above, places, coarse, tiles, res, east0, north0, north1, act, gain, edges, message, parts):
    side, cases = rhs.shape[1], rhs.shape[2]
    norm = jnp.zeros((1, cases), F32)
    for edge in range(4):
        s, e = divmod(edge, 2)
        index = lax.broadcasted_iota(jnp.int32, (side, cases), 0)
        mask = (index < count[s, e]).astype(F32)
        act[edge] = mask
        gain[edge] = gain_in[edge] * mask
        res[edge] = rhs[edge] * mask
        value = gain[edge] * res[edge]
        norm = norm + column_sum(res[edge] * value)
        put_edge(edge, value, east0, north0, north1, parts)
        own = basis[s, :, 2 * e * side : (2 * e + 1) * side].astype(BF16)
        if e == 0:
            other = east[s].astype(BF16)
        elif s == 0:
            other = basis[1, :, 3 * side :].astype(BF16)
        else:
            other = above[...].astype(BF16)
        place = places[edge].astype(BF16)
        value = multiply(place[:, : 4 * CS], own) + multiply(place[:, 16 : 16 + 4 * CS], other)
        high, low = split(value)
        edges[:ROWS, edge * side : (edge + 1) * side] = high
        edges[ROWS:, edge * side : (edge + 1) * side] = low
    lane = lax.broadcasted_iota(jnp.int32, (1, cases), 1)
    numbers = jnp.where(lane == 0, corner[0, 0], 0) + jnp.where(lane == 1, corner[1, 0], 0)
    index = lax.broadcasted_iota(jnp.int32, (cases, cases), 0)
    diagonal = index == lax.broadcasted_iota(jnp.int32, (cases, cases), 1)
    size = jnp.zeros((1, cases), F32)
    for s in range(2):
        tile = tiles[s].astype(F32)
        size = size + jnp.sum(jnp.where(diagonal, tile, 0.0)) / (512.0 * cases)
    size = size + jnp.sum(jnp.abs(coarse[...])) / (16.0 * coarse.shape[0])
    message_to(message, edges, parts, [norm, numbers.astype(F32), size])


def put_edge(edge, value, east, north0, north1, parts):
    side = value.shape[0]
    if edge % 2 == 0:
        east[edge // 2] = value
    elif edge == 1:
        north0[...] = value
    else:
        north1[...] = value
    high, low = split(value)
    parts[edge, :, : value.shape[1]] = high
    parts[edge, :, value.shape[1] :] = low


def apply_rows(block, parts):
    out = multiply(block, parts)
    cases = out.shape[1] // 2
    return out[:, :cases] + out[:, cases:]


def fetch(blocks, held, arrived, wanted):
    copies = [pltpu.make_async_copy(blocks.at[k], held.at[n], arrived.at[n]) for n, k in enumerate(wanted)]
    for copy in copies:
        copy.start()
    return copies


def give_body(own_east, own_north0, own_north1, west, below, blocks, out_east, out_north, parts, held, arrived):
    copies = fetch(blocks, held, arrived, (1, 3, 5))
    side = west.shape[1]
    own_north = (own_north0, own_north1)
    for s in range(2):
        parts[s, :side] = halves(own_east[s])
        parts[s, side : 2 * side] = halves(-west[s])
        parts[s, 2 * side : 3 * side] = halves(own_north[s][...])
    parts[0, 3 * side :] = halves(-below[...])
    parts[1, 3 * side :] = halves(-own_north0[...])
    copies[0].wait()
    out_east[0] = apply_rows(held[0], parts[0])
    copies[1].wait()
    out_north[...] = apply_rows(held[1], parts[0])
    copies[2].wait()
    out_east[1] = apply_rows(held[2], parts[1])


def keep_body(parts, blocks, out, held, arrived):
    copies = fetch(blocks, held, arrived, (0, 2, 7, 4, 6))
    for n, (edge, s) in enumerate([(0, 0), (1, 0), (1, 1), (2, 1), (3, 1)]):
        copies[n].wait()
        value = apply_rows(held[n], parts[s])
        out[edge] = out[edge] - value if n == 2 else value


def image_body(last, part, east, north, got, edges, act, gain, kappa_in, prev_east, prev_north0, prev_north1, *outs):
    side, cases = part.shape[1], part.shape[2]
    total = got[0]
    for k in range(1, got.shape[0]):
        total = total + got[k]
    if kappa_in is None:
        kappa = 4.0 / total[NEAR - 2 : NEAR - 1]
    else:
        kappa = kappa_in[0:1]
    high, low = split(total)
    twice = jnp.concatenate(
        [jnp.concatenate([high, low], 1), jnp.concatenate([high, jnp.zeros_like(low)], 1)], 0
    )
    u_ref = outs[0]
    first = jnp.zeros((1, cases), F32)
    second = jnp.zeros((1, cases), F32)
    previous = [prev_east[0], prev_north0[...], prev_east[1], prev_north1[...]]
    for edge in range(4):
        coarse = lax.dot_general(
            edges[:, edge * side : (edge + 1) * side],
            twice,
            (((0,), (0,)), ((), ())),
            preferred_element_type=F32,
        )
        value = part[edge] + coarse[:, :cases] + coarse[:, cases:]
        if edge % 2 == 0:
            value = value - east[edge // 2]
        elif edge == 3:
            value = value - north[...]
        image = value * act[edge]
        u_ref[edge] = image
        first = first + column_sum(previous[edge] * image)
        if not last:
            following = kappa * gain[edge] * value
            second = second + column_sum(following * image)
            put_edge(edge, following, outs[1], outs[2], outs[3], outs[-1])
    if last:
        outs[1][...] = total[NEAR - 8 : NEAR]
        outs[2][...] = jnp.broadcast_to(first, outs[2].shape)
    else:
        outs[4][...] = jnp.broadcast_to(kappa, outs[4].shape)
        outs[5][...] = total[NEAR - 8 : NEAR]
        message_to(outs[6], edges, outs[-1], [first, second])


def image_call(last, part, east, north, got, edges, act, gain, kappa, previous, copies):
    _, side, cases = part.shape
    shape = lambda *dims: jax.ShapeDtypeStruct(dims + (cases,), F32)
    scratch = ()
    if last:
        outs = (shape(4, side), shape(8), shape(copies))
    else:
        outs = (
            shape(4, side),
            shape(2, side),
            shape(side),
            shape(side),
            shape(8),
            shape(8),
            shape(copies, ROWS),
        )
        scratch = (pltpu.VMEM((4, side, 2 * cases), BF16),)
    body = functools.partial(image_body, last)
    operands = (part, east, north, got, edges, act, gain)
    if kappa is None:
        body = lambda *refs: image_body(last, *refs[:7], None, *refs[7:])
    else:
        operands = operands + (kappa,)
    return kernel_call(body, outs, operands + tuple(previous), scratch=scratch)


def slot_of(source, core, half):
    return source // 2 + half * ((source + core) % 2)


def pick_body(numbers, me, columns, out, rows):
    half = numbers.shape[0] // 2
    block = out.shape[1]
    rows[...] = jnp.zeros_like(rows)
    core = me[1] % 2
    for j in range(4 * half):
        node = numbers[slot_of(j // 2, core, half), j % 2]
        for c in range(CS):
            at = node * CS + c
            rows[pl.ds(j * CS + c, 1)] = columns[pl.ds(at // block, 1), pl.ds(at % block, 1)].reshape(1, -1)
    turned = rows[...].T[:block]
    known = jnp.zeros((1, turned.shape[1]), F32)
    for k in range(columns.shape[0]):
        known = known + columns[k, :1]
    lane = lax.broadcasted_iota(jnp.int32, turned.shape, 1)
    turned = jnp.where(lane >= block, known, turned)
    for copy in range(half):
        out[copy] = turned


def near_body(gx, numbers, me, same, other, out):
    half = same.shape[0]
    block = same.shape[1]
    out[...] = jnp.zeros_like(out)
    core = me[1] % 2
    lane = lax.broadcasted_iota(jnp.int32, (1, same.shape[2]), 1)
    for jj in range(4):
        j = (2 * me[1] - 1 + jj + 4 * half) % (4 * half)
        slot = slot_of(j // 2, core, half)
        for i in range(gx):
            node = numbers[slot, 2 * i + j % 2]
            owner = node * CS // block
            row = node * CS - owner * block
            mine = owner % 2 == core
            for c in range(CS):
                first = same[pl.ds(owner // 2, 1), pl.ds(row + c, 1)].reshape(1, -1)
                second = other[pl.ds(owner // 2, 1), pl.ds(row + c, 1)].reshape(1, -1)
                value = jnp.where(mine, first, second)
                out[pl.ds(i * NEAR + jj * CS + c, 1)] = jnp.where(lane < block, value, 0.0)


def coarse_body(count, lanes, *refs):
    sources, (same, other, *near, out) = refs[:count], refs[count:]
    gx = out.shape[0]
    cases = same.shape[2]
    lane = lanes[...].astype(BF16)
    value = jnp.zeros((gx * NEAR, cases), F32)
    for ii, source in enumerate(sources):
        pieces = [ref[z, ii * NEAR : (ii + 1) * NEAR] for ref in (same, other) for z in range(same.shape[0])]
        if ii == 0:
            total = pieces[0][NEAR - 8 :]
            for piece in pieces[1:]:
                total = total + piece[NEAR - 8 :]
        if near:
            middle = [ref[z, NEAR : 2 * NEAR] for ref in (same, other) for z in range(same.shape[0])]
            pieces = [
                middle[k] + sum(ref[k // ref.shape[1], k % ref.shape[1]] for ref in near)
                for k in range(len(middle))
            ]
        gathered = halves(jnp.concatenate(pieces, 0))
        high, low = split(source[...])
        high = multiply(high, lane).astype(BF16)
        low = multiply(low, lane).astype(BF16)
        product = multiply(high, gathered)
        value = value + product[:, :cases] + product[:, cases:] + multiply(low, gathered[:, :cases])
    index = lax.broadcasted_iota(jnp.int32, (8, cases), 0)
    for target in range(gx):
        for ii in range(3):
            at = ((target - 1 + ii) % gx) * NEAR
            out[target, ii * NEAR : ii * NEAR + 8] = value[at : at + 8]
            rest = value[at + 8 : at + 16]
            if ii == 0:
                rest = jnp.where(index < 4, rest, total)
            out[target, ii * NEAR + 8 : ii * NEAR + 16] = rest


def finish_body(kappa_ref, spare0, spare1, spare2, last, *refs):
    fields, (u1, u2, u3, res, mult_out, res_out) = refs[:9], refs[9:]
    kappa = kappa_ref[0:1]
    moments = [
        spare0[4:5],
        kappa * spare1[4:5],
        kappa * spare1[5:6],
        kappa * spare2[4:5],
        kappa * spare2[5:6],
        kappa * column_sum(last[...]),
    ]

    def form(first, second, shift):
        total = 0.0
        for i, x in enumerate(first):
            for j, y in enumerate(second):
                total = total + x * y * moments[i + j + shift]
        return total

    one = jnp.ones_like(kappa)
    rho, pi, gamma = [one], [one], []
    rz = moments[0]
    for iteration in range(3):
        step = rz / form(pi, pi, 1)
        gamma = [(gamma[k] if k < len(gamma) else 0.0) + step * pi[k] for k in range(len(pi))]
        rho = [one] + [-value for value in gamma]
        if iteration < 2:
            rz_new = form(rho, rho, 0)
            ratio = rz_new / rz
            pi = [rho[k] + (ratio * pi[k] if k < len(pi) else 0.0) for k in range(len(rho))]
            rz = rz_new
    gamma = [kappa * value for value in gamma]
    for edge in range(4):
        total = 0.0
        for k in range(3):
            east, north0, north1 = fields[3 * k : 3 * k + 3]
            value = east[edge // 2] if edge % 2 == 0 else (north0, north1)[edge // 2][...]
            total = total + gamma[k] * value
        mult_out[edge] = total
        res_out[edge] = res[edge] - (gamma[0] * u1[edge] + gamma[1] * u2[edge] + gamma[2] * u3[edge])


def local(dual_rhs, scaling, dual_count, corner_map, local_ops, corner_basis, coarse_inverse):
    gx, gy = lax.axis_size("sx"), lax.axis_size("sy")
    a, b = lax.axis_index("sx"), lax.axis_index("sy")
    side, cases = dual_rhs.shape[3], dual_rhs.shape[4]
    rhs = dual_rhs.reshape(4, side, cases)
    blocks = local_ops.reshape(8, side, 4 * side)
    block = coarse_inverse.shape[0]
    half = gy // 2
    basis = corner_basis[0]
    me = jnp.stack([a, b]).astype(jnp.int32)
    shape = lambda *dims: jax.ShapeDtypeStruct(dims + (cases,), F32)
    field = shape(4, side)
    double = lambda *dims: jax.ShapeDtypeStruct(dims + (2 * cases,), BF16)
    wide = kernel_call(wide_body, shape(gx, block), (me, corner_map[0], coarse_inverse), 2)
    columns_all = lax.all_to_all(wide, "sx", 0, 0, tiled=True)
    wide_basis = basis.astype(F32)
    east = shifted(wide_basis[:, :, side : 2 * side], "sx", -1)
    above = shifted(wide_basis[0, :, 3 * side :], "sy", -1)

    residual, *w0, act, gain, edges, message = kernel_call(
        begin_body,
        (
            field,
            shape(2, side),
            shape(side),
            shape(side),
            field,
            field,
            jax.ShapeDtypeStruct((2 * ROWS, 4 * side), BF16),
            shape(half, ROWS),
        ),
        (
            dual_count[0],
            corner_map[0],
            rhs,
            scaling.reshape(4, side, 1),
            wide_basis,
            east,
            above,
            jnp.asarray(place_matrices()),
            coarse_inverse,
            local_ops[0, :, :cases, :cases],
        ),
        2,
        scratch=(pltpu.VMEM((4, side, 2 * cases), BF16),),
    )
    message, columns_all = lax.optimization_barrier((message, columns_all))

    def halo(vector):
        return shifted(vector[0], "sx", 1), shifted(vector[2], "sy", 1)

    def held(count):
        return (pltpu.VMEM((count,) + blocks.shape[1:], BF16), pltpu.SemaphoreType.DMA((count,)))

    def give(own, west, below):
        given_east, given_north, parts = kernel_call(
            give_body,
            (shape(2, side), shape(side), double(2, 4 * side)),
            (*own, west, below),
            blocks=blocks,
            scratch=held(3),
        )
        return parts, shifted(given_east, "sx", -1), shifted(given_north, "sy", -1)

    def keep(parts):
        return kernel_call(keep_body, field, (parts,), blocks=blocks, scratch=held(5))

    west, below = halo(w0)
    same, other = along_sy(message)
    lower = shifted(jnp.stack([same[:, :NEAR], other[:, :NEAR]]), "sx", -1)
    upper = shifted(jnp.stack([same[:, 2 * NEAR :], other[:, 2 * NEAR :]]), "sx", 1)
    numbers = jnp.concatenate([same[:, NEAR - 3, :2], other[:, NEAR - 3, :2]], 0).astype(jnp.int32)
    turned = kernel_call(
        pick_body, shape(half, block), (numbers, me, columns_all), 2, scratch=(pltpu.VMEM((cases, cases), F32),)
    )
    turned, west, below = lax.optimization_barrier((turned, west, below))
    parts, back_east, back_north = give(w0, west, below)
    kept = keep(parts)
    rows_same, rows_other = along_sy(turned)
    rows_same, rows_other, kept, lower, upper = lax.optimization_barrier(
        (rows_same, rows_other, kept, lower, upper)
    )
    numbers = jnp.concatenate([rows_same[:, 0, block:], rows_other[:, 0, block:]], 0).astype(jnp.int32)
    own_part = kernel_call(
        functools.partial(near_body, gx), shape(gx * NEAR), (numbers, me, rows_same, rows_other), 2
    )
    below_part = shifted(own_part, "sx", 1)
    beyond_part = shifted(own_part, "sx", -1)
    lanes = lax.dynamic_index_in_dim(jnp.asarray(lane_matrices(gy)), b % 2, 0, keepdims=False)

    def coarse_solve(sources, *arrived):
        send = kernel_call(
            functools.partial(coarse_body, len(sources)),
            shape(gx, ROWS),
            (lanes, *sources, *arrived),
        )
        return lax.all_to_all(send, "sx", 0, 0, tiled=True)

    got = coarse_solve((own_part,), same, other, lower, upper)
    u1, *w1, kappa, spare0, message = image_call(
        False, kept, back_east, back_north, got, edges, act, gain, None, w0, half
    )
    sources = (below_part, own_part, beyond_part)
    west, below = halo(w1)
    same, other = along_sy(message)
    parts, back_east, back_north = give(w1, west, below)
    got = coarse_solve(sources, same, other)
    kept = keep(parts)
    u2, *w2, _, spare1, message = image_call(
        False, kept, back_east, back_north, got, edges, act, gain, kappa, w1, half
    )
    west, below = halo(w2)
    same, other = along_sy(message)
    parts, back_east, back_north = give(w2, west, below)
    got = coarse_solve(sources, same, other)
    kept = keep(parts)
    u3, spare2, last = image_call(
        True, kept, back_east, back_north, got, edges, act, gain, kappa, w2, gx * gy
    )
    last = lax.all_to_all(last.reshape(gx * gy, 1, cases), ("sx", "sy"), 0, 0, tiled=True)
    multipliers, residual = kernel_call(
        finish_body,
        (field, field),
        (kappa, spare0, spare1, spare2, last.reshape(gx * gy, cases), *w0, *w1, *w2, u1, u2, u3, residual),
    )
    return multipliers.reshape(dual_rhs.shape), residual.reshape(dual_rhs.shape)


def solution(mesh):
    in_specs = (
        P("sx", "sy", None, None, None),
        P("sx", "sy", None, None),
        P("sx", "sy", None),
        P("sx", "sy", None),
        P("sx", "sy", None, None),
        P("sx", "sy", None, None),
        P("sx", "sy"),
    )
    out_specs = (P("sx", "sy", None, None, None), P("sx", "sy", None, None, None))
    return jax.shard_map(local, mesh=mesh, in_specs=in_specs, out_specs=out_specs, check_vma=False)
```

time: 273 us -> 271 us (level)
  blocking collectives: 61.4 us -> 25.3 us
  waiting for transfers between devices: 22 us -> 44.7 us
  starting transfers between devices: 67.6 us -> 82.1 us
  Pallas kernels: 32.7 us -> 43.9 us
  other arithmetic: 8.97 us -> 0.2 us
  local copies, waits for them, and re-layouts: 75.2 us -> 71 us
    all_to_all x2 -> x0, blocking collectives: 35.9 us -> none  [along_sy(): lax.all_to_all(copies, 'sy', 0, 0, tiled=True, axis_index_groups=groups)]
    all_to_all x2 -> x4, waiting for transfers between devices: 8.86 us -> 31.3 us  [along_sy(): lax.all_to_all(copies, 'sy', 0, 0, tiled=True, axis_index_groups=groups)]
    pallas_call x16 -> x17, Pallas kernels: 32.7 us -> 43.9 us  [kernel_call(): pl.pallas_call(body, grid=(1,), in_specs=specs, out_specs=tuple((whole(ar...]
    all_to_all x2 -> x4, starting transfers between devices: 10.4 us -> 18.4 us  [along_sy(): lax.all_to_all(copies, 'sy', 0, 0, tiled=True, axis_index_groups=groups)]
    ppermute x16 -> x18, starting transfers between devices: 29 us -> 34 us  [shifted(): lax.ppermute(array, axis, [(i, (i + by) % count) for i in range(count)])]
    all_to_all x1, waiting for transfers between devices: 4.97 us -> 0.01 us  [local(): columns_all = lax.all_to_all(wide, 'sx', 0, 0, tiled=True)]
    reduce_sum x4 -> x0, other arithmetic: 4.36 us -> none  [the longest x1 1.49 us: local(): jnp.sum(corner * jnp.eye(corner.shape[1], dtype=F32))]
    squeeze x9 -> x2, local copies, waits for them, and re-layouts: 4.68 us -> 0.92 us  [the longest x1 0.85 us: local(): local_ops[0, :, :cases, :cases]]
  transfers between devices with their start and end apart: 26 -> 30, of which waited for: 7 -> 9; matrix products, arithmetic and copies ran while one was open for 5% -> 2% of each run, Pallas kernels for 8% -> 13%
where the time goes in v2:
time: 271 us; the launch traced here: 268 us
  starting transfers between devices  82.1 us (30%)
  local copies, waits for them, and re-layouts  71 us (26%)
  waiting for transfers between devices  44.7 us (16%)
  Pallas kernels  43.9 us (16%)
  blocking collectives  25.3 us (9%)
    unnamed x174, local copies, waits for them, and re-layouts  65.4 us
    pallas_call x17, Pallas kernels, kernel_call(): pl.pallas_call(body, grid=(1,), in_specs=specs, out_specs=tuple((whole(ar...  43.9 us
    ppermute x18, starting transfers between devices, shifted(): lax.ppermute(array, axis, [(i, (i + by) % count) for i in range(count)])  34 us
    all_to_all x4, waiting for transfers between devices, along_sy(): lax.all_to_all(copies, 'sy', 0, 0, tiled=True, axis_index_groups=groups)  31.3 us
    all_to_all x1, blocking collectives, local(): lax.all_to_all(last.reshape(gx * gy, 1, cases), ('sx', 'sy'), 0, 0, tiled...  25.3 us
    all_to_all x4, starting transfers between devices, along_sy(): lax.all_to_all(copies, 'sy', 0, 0, tiled=True, axis_index_groups=groups)  18.4 us
    all_to_all x3, starting transfers between devices, coarse_solve(): return lax.all_to_all(send, 'sx', 0, 0, tiled=True)  11.5 us
    ppermute x4, starting transfers between devices, along_sy(): return (same, lax.ppermute(same, 'sy', [(i, i ^ 1) for i in range(count)]))  10.4 us
  transfers between devices with their start and end apart: 30, of which 9 were waited for; matrix products, arithmetic and copies ran while one was open for 2% of the time, Pallas kernels for 13%

profile of v2, /device:TPU:1, one launch (start us, length us, event | category | flops | bytes accessed | tf_op | source)
XLA Modules:
  0.0 268.5 jit_solution(13124190525976994653)
XLA Ops:
  2.7 1.6 shard_map.105
  4.3 7.7 %all-to-all-start = ((f32[16,96,128]{2,1,0:T(8,128)}), f32[16,96,128]{2,1,0:T(8,128)S(1)}, u32[]{:S(2)}, u32[]{:S(2)}) async-start(f32[16,96,128]{2,1,0:T(8,128)} %shard_map.105), calls=%async_computation | async-start | bytes 1572864 | tf_op jit(solution)/shard_map/all_to_all | solution.py:413
  13.0 5.0 %collective-permute-start = (f32[2,12,384]{2,1,0:T(8,128)S(1)}, f32[2,12,384]{2,1,0:T(8,128)S(1)}, u32[]{:S(2)}, u32[]{:S(2)}) collective-permute-start(f32[2,12,384]{2,1,0:T(8,128)S(1)} %slice.44), channel_id=1, source_target_pairs={{0,240},{16,0},{32,16},{48,32},{64,48},{80,64},{96,80},{112,96},{1... | collective-permute-start | bytes 110600 | tf_op jit(solution)/shard_map/ppermute | solution.py:21
  18.8 1.5 reshape.35.gain_in
  21.0 1.9 collective-permute-done.east
  33.1 8.2 %all-to-all-start.1 = ((f32[8,48,128]{2,1,0:T(8,128)}), f32[8,48,128]{2,1,0:T(8,128)S(1)}, u32[]{:S(2)}, u32[]{:S(2)}) async-start(f32[8,48,128]{2,1,0:T(8,128)} %copy-done.66), calls=%async_computation.1 | async-start | bytes 393216 | tf_op jit(solution)/shard_map/all_to_all | solution.py:27
  42.6 7.4 %all-to-all-done.1.refs_1_ = f32[8,48,128]{2,1,0:T(8,128)S(1)} async-done(((f32[8,48,128]{2,1,0:T(8,128)}), f32[8,48,128]{2,1,0:T(8,128)S(1)}, u32[]{:S(2)}, u32[]{:S(2)}) %all-to-all-start.1) | async-done | bytes 196640 | tf_op jit(solution)/shard_map/all_to_all | solution.py:27
  50.0 3.2 %collective-permute-start.2 = (f32[8,48,128]{2,1,0:T(8,128)S(1)}, f32[8,48,128]{2,1,0:T(8,128)}, u32[]{:S(2)}, u32[]{:S(2)}) collective-permute-start(f32[8,48,128]{2,1,0:T(8,128)S(1)} %all-to-all-done.1.refs_1_), channel_id=1, source_target_pairs={{0,1},{1,0},{2,3},{3,2},{4,5},{5,4},{6,7},{7,6},{8,9},{9,8},{10,11... | collective-permute-start | bytes 589832 | tf_op jit(solution)/shard_map/ppermute | solution.py:28
  56.0 1.5 shard_map.106
  58.2 3.5 %all-to-all-start.2 = ((f32[8,96,128]{2,1,0:T(8,128)}), f32[8,96,128]{2,1,0:T(8,128)S(1)}, u32[]{:S(2)}, u32[]{:S(2)}) async-start(f32[8,96,128]{2,1,0:T(8,128)} %copy-done.41), calls=%async_computation.2 | async-start | bytes 786432 | tf_op jit(solution)/shard_map/all_to_all | solution.py:27
  62.6 11.6 %all-to-all-done.2.same = f32[8,96,128]{2,1,0:T(8,128)S(1)} async-done(((f32[8,96,128]{2,1,0:T(8,128)}), f32[8,96,128]{2,1,0:T(8,128)S(1)}, u32[]{:S(2)}, u32[]{:S(2)}) %all-to-all-start.2) | async-done | bytes 393248 | tf_op jit(solution)/shard_map/all_to_all | solution.py:27
  74.2 3.0 %collective-permute-start.5 = (f32[8,96,128]{2,1,0:T(8,128)S(1)}, f32[8,96,128]{2,1,0:T(8,128)S(1)}, u32[]{:S(2)}, u32[]{:S(2)}) collective-permute-start(f32[8,96,128]{2,1,0:T(8,128)S(1)} %all-to-all-done.2.same), channel_id=1, source_target_pairs={{0,1},{1,0},{2,3},{3,2},{4,5},{5,4},{6,7},{7,6},{8,9},{9,8},{10,11... | collective-permute-start | bytes 1179656 | tf_op jit(solution)/shard_map/ppermute | solution.py:28
  78.2 4.5 %collective-permute-start.6 = (f32[2,8,16,128]{3,2,1,0:T(8,128)S(1)}, f32[2,8,16,128]{3,2,1,0:T(8,128)S(1)}, u32[]{:S(2)}, u32[]{:S(2)}) collective-permute-start(f32[2,8,16,128]{3,2,1,0:T(8,128)S(1)} %pad_maximum_fusion), channel_id=1, source_target_pairs={{0,240},{16,0},{32,16},{48,32},{64,48},{80,64},{96,80},{112,96},{1... | collective-permute-start | bytes 393224 | tf_op jit(solution)/shard_map/ppermute | solution.py:21
  82.8 3.7 %copy-done = bf16[1,2,1536,1536]{3,2,1,0:T(8,128)(2,1)S(1)} copy-done((bf16[1,2,1536,1536]{3,2,1,0:T(8,128)(2,1)S(1)}, bf16[1,2,1536,1536]{3,2,1,0:T(8,128)(2,1)}, u32[]{:S(2)}) %copy-start) | copy-done | bytes 9437208
  87.5 4.7 %shard_map.107 = (f32[2,384,128]{2,1,0:T(8,128)}, f32[384,128]{1,0:T(8,128)S(1)}, bf16[2,1536,256]{2,1,0:T(8,128)(2,1)S(1)}) custom-call(f32[2,384,128]{2,1,0:T(8,128)S(1)} %get-tuple-element.50.own_east.refs_7_.refs_0_, f32[384,128]{1,0:T(8,128)S(1)} %copy-done.16, f32[384,128]{1,0:T(8,128)S(1)} %copy-done.20, f32[2,384,128]{2,1,0:T(8,128)} %collective-permute-done.3.west, ...), custom_call_target="tpu_custom_call" | custom-call | flops 95944704 | bytes 23986176 | tf_op jit(solution)/shard_map/pallas_call | solution.py:41
  92.2 5.0 %collective-permute-start.8 = (f32[2,384,128]{2,1,0:T(8,128)}, f32[2,384,128]{2,1,0:T(8,128)}, u32[]{:S(2)}, u32[]{:S(2)}) collective-permute-start(f32[2,384,128]{2,1,0:T(8,128)} %get-tuple-element.58), channel_id=1, source_target_pairs={{0,240},{16,0},{32,16},{48,32},{64,48},{80,64},{96,80},{112,96},{1... | collective-permute-start | bytes 1179656 | tf_op jit(solution)/shard_map/ppermute | solution.py:21
  97.3 4.7 %shard_map.108.refs_0_ = f32[4,384,128]{2,1,0:T(8,128)S(1)} custom-call(bf16[2,1536,256]{2,1,0:T(8,128)(2,1)S(1)} %get-tuple-element.56.parts, bf16[8,384,1536]{2,1,0:T(8,128)(2,1)S(1)} %bitcast.35), custom_call_target="tpu_custom_call" | custom-call | flops 91226112 | bytes 22806528 | tf_op jit(solution)/shard_map/pallas_call | solution.py:41
  102.5 1.7 shard_map.109.refs_0_.refs_1_
  106.9 3.6 %all-to-all-start.3 = ((f32[16,48,128]{2,1,0:T(8,128)}), f32[16,48,128]{2,1,0:T(8,128)S(1)}, u32[]{:S(2)}, u32[]{:S(2)}) async-start(f32[16,48,128]{2,1,0:T(8,128)} %copy-done.42), calls=%async_computation.3 | async-start | bytes 786432 | tf_op jit(solution)/shard_map/all_to_all | solution.py:495
  111.3 4.7 %collective-permute-done.9.refs_2_ = f32[384,128]{1,0:T(8,128)S(1)} collective-permute-done((f32[384,128]{1,0:T(8,128)}, f32[384,128]{1,0:T(8,128)S(1)}, u32[]{:S(2)}, u32[]{:S(2)}) %collective-permute-start.9) | collective-permute-done | bytes 196640 | tf_op jit(solution)/shard_map/ppermute | solution.py:21
  116.7 3.0 %all-to-all-done.3.refs_3_ = f32[16,48,128]{2,1,0:T(8,128)S(1)} async-done(((f32[16,48,128]{2,1,0:T(8,128)}), f32[16,48,128]{2,1,0:T(8,128)S(1)}, u32[]{:S(2)}, u32[]{:S(2)}) %all-to-all-start.3) | async-done | bytes 393248 | tf_op jit(solution)/shard_map/all_to_all | solution.py:495
  124.2 1.8 shard_map.111
  129.0 3.4 %all-to-all-start.4 = ((f32[8,48,128]{2,1,0:T(8,128)}), f32[8,48,128]{2,1,0:T(8,128)S(1)}, u32[]{:S(2)}, u32[]{:S(2)}) async-start(f32[8,48,128]{2,1,0:T(8,128)} %copy-done.67), calls=%async_computation.4 | async-start | bytes 393216 | tf_op jit(solution)/shard_map/all_to_all | solution.py:27
  132.6 3.6 %collective-permute-start.11 = (f32[384,128]{1,0:T(8,128)}, f32[384,128]{1,0:T(8,128)S(1)}, u32[]{:S(2)}, u32[]{:S(2)}) collective-permute-start(f32[384,128]{1,0:T(8,128)} %copy-done.27), channel_id=1, source_target_pairs={{0,1},{1,2},{2,3},{3,4},{4,5},{5,6},{6,7},{7,8},{8,9},{9,10},{10,1... | collective-permute-start | bytes 589832 | tf_op jit(solution)/shard_map/ppermute | solution.py:21
  136.2 4.8 %all-to-all-done.4.refs_3_ = f32[8,48,128]{2,1,0:T(8,128)S(1)} async-done(((f32[8,48,128]{2,1,0:T(8,128)}), f32[8,48,128]{2,1,0:T(8,128)S(1)}, u32[]{:S(2)}, u32[]{:S(2)}) %all-to-all-start.4) | async-done | bytes 196640 | tf_op jit(solution)/shard_map/all_to_all | solution.py:27
  140.9 3.6 %collective-permute-start.16 = (f32[8,48,128]{2,1,0:T(8,128)S(1)}, f32[8,48,128]{2,1,0:T(8,128)S(1)}, u32[]{:S(2)}, u32[]{:S(2)}) collective-permute-start(f32[8,48,128]{2,1,0:T(8,128)S(1)} %all-to-all-done.4.refs_3_), channel_id=1, source_target_pairs={{0,1},{1,0},{2,3},{3,2},{4,5},{5,4},{6,7},{7,6},{8,9},{9,8},{10,11... | collective-permute-start | bytes 589832 | tf_op jit(solution)/shard_map/ppermute | solution.py:28
  146.0 3.7 %copy-done.1 = bf16[1,2,1536,1536]{3,2,1,0:T(8,128)(2,1)S(1)} copy-done((bf16[1,2,1536,1536]{3,2,1,0:T(8,128)(2,1)S(1)}, bf16[1,2,1536,1536]{3,2,1,0:T(8,128)(2,1)}, u32[]{:S(2)}) %copy-start.1) | copy-done | bytes 9437208
  151.6 3.7 %shard_map.112 = (f32[2,384,128]{2,1,0:T(8,128)}, f32[384,128]{1,0:T(8,128)}, bf16[2,1536,256]{2,1,0:T(8,128)(2,1)S(1)}) custom-call(f32[2,384,128]{2,1,0:T(8,128)S(1)} %get-tuple-element.69.own_east.prev_east.refs_3_, f32[384,128]{1,0:T(8,128)S(1)} %copy-done.24, f32[384,128]{1,0:T(8,128)S(1)} %copy-done.28, ...), custom_call_target="tpu_custom_call" | custom-call | flops 95944704 | bytes 23986176 | tf_op jit(solution)/shard_map/pallas_call | solution.py:41
  156.4 4.3 %collective-permute-start.12 = (f32[2,384,128]{2,1,0:T(8,128)}, f32[2,384,128]{2,1,0:T(8,128)}, u32[]{:S(2)}, u32[]{:S(2)}) collective-permute-start(f32[2,384,128]{2,1,0:T(8,128)} %get-tuple-element.73), channel_id=1, source_target_pairs={{0,240},{16,0},{32,16},{48,32},{64,48},{80,64},{96,80},{112,96},{1... | collective-permute-start | bytes 1179656 | tf_op jit(solution)/shard_map/ppermute | solution.py:21
  160.7 1.5 shard_map.114
  163.6 3.8 %all-to-all-start.5 = ((f32[16,48,128]{2,1,0:T(8,128)}), f32[16,48,128]{2,1,0:T(8,128)S(1)}, u32[]{:S(2)}, u32[]{:S(2)}) async-start(f32[16,48,128]{2,1,0:T(8,128)} %shard_map.114), calls=%async_computation.5 | async-start | bytes 786432 | tf_op jit(solution)/shard_map/all_to_all | solution.py:495
  168.2 3.7 %copy-done.2 = bf16[1,2,1536,1536]{3,2,1,0:T(8,128)(2,1)S(1)} copy-done((bf16[1,2,1536,1536]{3,2,1,0:T(8,128)(2,1)S(1)}, bf16[1,2,1536,1536]{3,2,1,0:T(8,128)(2,1)}, u32[]{:S(2)}) %copy-start.2) | copy-done | bytes 9437208
  173.3 4.7 %shard_map.113.part = f32[4,384,128]{2,1,0:T(8,128)S(1)} custom-call(bf16[2,1536,256]{2,1,0:T(8,128)(2,1)S(1)} %copy-done.44, bf16[8,384,1536]{2,1,0:T(8,128)(2,1)S(1)} %bitcast.37), custom_call_target="tpu_custom_call" | custom-call | flops 91226112 | bytes 22806528 | tf_op jit(solution)/shard_map/pallas_call | solution.py:41
  184.3 2.3 shard_map.115
  189.4 3.4 %all-to-all-start.6 = ((f32[8,48,128]{2,1,0:T(8,128)}), f32[8,48,128]{2,1,0:T(8,128)S(1)}, u32[]{:S(2)}, u32[]{:S(2)}) async-start(f32[8,48,128]{2,1,0:T(8,128)} %copy-done.68), calls=%async_computation.6 | async-start | bytes 393216 | tf_op jit(solution)/shard_map/all_to_all | solution.py:27
  194.2 1.8 collective-permute-start.18
  196.0 7.6 %all-to-all-done.6.refs_3_ = f32[8,48,128]{2,1,0:T(8,128)S(1)} async-done(((f32[8,48,128]{2,1,0:T(8,128)}), f32[8,48,128]{2,1,0:T(8,128)S(1)}, u32[]{:S(2)}, u32[]{:S(2)}) %all-to-all-start.6) | async-done | bytes 196640 | tf_op jit(solution)/shard_map/all_to_all | solution.py:27
  204.2 2.7 %collective-permute-done.17.west = f32[2,384,128]{2,1,0:T(8,128)S(1)} collective-permute-done((f32[2,384,128]{2,1,0:T(8,128)S(1)}, f32[2,384,128]{2,1,0:T(8,128)S(1)}, u32[]{:S(2)}, u32[]{:S(2)}) %collective-permute-start.17) | collective-permute-done | bytes 393248 | tf_op jit(solution)/shard_map/ppermute | solution.py:21
  206.9 3.7 %copy-done.3 = bf16[1,2,1536,1536]{3,2,1,0:T(8,128)(2,1)S(1)} copy-done((bf16[1,2,1536,1536]{3,2,1,0:T(8,128)(2,1)S(1)}, bf16[1,2,1536,1536]{3,2,1,0:T(8,128)(2,1)}, u32[]{:S(2)}) %copy-start.3) | copy-done | bytes 9437208
  212.5 3.7 %shard_map.116 = (f32[2,384,128]{2,1,0:T(8,128)}, f32[384,128]{1,0:T(8,128)S(1)}, bf16[2,1536,256]{2,1,0:T(8,128)(2,1)S(1)}) custom-call(f32[2,384,128]{2,1,0:T(8,128)S(1)} %get-tuple-element.77.own_east.prev_east.refs_6_, f32[384,128]{1,0:T(8,128)S(1)} %copy-done.32, f32[384,128]{1,0:T(8,128)S(1)} %copy-done.35, ...), custom_call_target="tpu_custom_call" | custom-call | flops 95944704 | bytes 23986176 | tf_op jit(solution)/shard_map/pallas_call | solution.py:41
  217.3 2.0 collective-permute-start.19
  219.4 1.5 shard_map.118
  220.9 4.2 %all-to-all-start.7 = ((f32[16,48,128]{2,1,0:T(8,128)}), f32[16,48,128]{2,1,0:T(8,128)}, u32[]{:S(2)}, u32[]{:S(2)}) async-start(f32[16,48,128]{2,1,0:T(8,128)} %shard_map.118), calls=%async_computation.7 | async-start | bytes 786432 | tf_op jit(solution)/shard_map/all_to_all | solution.py:495
  225.6 3.7 %copy-done.4 = bf16[1,2,1536,1536]{3,2,1,0:T(8,128)(2,1)S(1)} copy-done((bf16[1,2,1536,1536]{3,2,1,0:T(8,128)(2,1)S(1)}, bf16[1,2,1536,1536]{3,2,1,0:T(8,128)(2,1)}, u32[]{:S(2)}) %copy-start.4) | copy-done | bytes 9437208
  230.7 4.7 %shard_map.117.part = f32[4,384,128]{2,1,0:T(8,128)S(1)} custom-call(bf16[2,1536,256]{2,1,0:T(8,128)(2,1)S(1)} %copy-done.46, bf16[8,384,1536]{2,1,0:T(8,128)(2,1)S(1)} %bitcast.39), custom_call_target="tpu_custom_call" | custom-call | flops 91226112 | bytes 22806528 | tf_op jit(solution)/shard_map/pallas_call | solution.py:41
  240.0 1.7 shard_map.119
  241.7 25.3 %all_to_all.45 = f32[256,1,128]{2,1,0:T(1,128)S(1)} all-to-all(f32[256,1,128]{2,1,0:T(1,128)S(1)} %bitcast.42), channel_id=1, replica_groups=mesh['sx'=16,'sy'=16] {'sx','sy'}, dimensions={0} | all-to-all | bytes 262144 | tf_op jit(solution)/shard_map/all_to_all | solution.py:518
  267.0 1.5 shard_map.120
  (225 shorter events, 63.2 us)
Async XLA Ops:
  0.6 18.2 %copy-start.86 = (f32[1,2,2,384]{3,2,1,0:T(2,128)S(1)}, f32[1,2,2,384]{3,2,1,0:T(2,128)}, u32[]{:S(2)}) copy-start(f32[1,2,2,384]{3,2,1,0:T(2,128)} %param.10) | copy-start | bytes 18436
  2.7 9.3 %copy-start.84 = (bf16[1,2,12,1536]{3,1,2,0:T(2,128)(2,1)S(1)}, bf16[1,2,12,1536]{3,1,2,0:T(2,128)(2,1)}, u32[]{:S(2)}) copy-start(bf16[1,2,12,1536]{3,1,2,0:T(2,128)(2,1)} %param.14) | copy-start | bytes 221188
  4.3 19.3 %copy-start.70 = (f32[96,96]{1,0:T(8,128)S(1)}, f32[96,96]{1,0:T(8,128)}, u32[]{:S(2)}) copy-start(f32[96,96]{1,0:T(8,128)} %coarse.3) | copy-start | bytes 110596
  4.3 28.8 %all-to-all-start = ((f32[16,96,128]{2,1,0:T(8,128)}), f32[16,96,128]{2,1,0:T(8,128)S(1)}, u32[]{:S(2)}, u32[]{:S(2)}) async-start(f32[16,96,128]{2,1,0:T(8,128)} %shard_map.105), calls=%async_computation | async-start | bytes 1572864 | tf_op jit(solution)/shard_map/all_to_all | solution.py:413
  12.0 8.3 %collective-permute-start.1 = (f32[12,384]{1,0:T(8,128)S(1)}, f32[12,384]{1,0:T(8,128)S(1)}, u32[]{:S(2)}, u32[]{:S(2)}) collective-permute-start(f32[12,384]{1,0:T(8,128)S(1)} %slice_bitcast_fusion.5), channel_id=1, source_target_pairs={{0,15},{1,0},{2,1},{3,2},{4,3},{5,4},{6,5},{7,6},{8,7},{9,8},{10,9... | collective-permute-start | bytes 55304 | tf_op jit(solution)/shard_map/ppermute | solution.py:21
  13.0 9.9 %collective-permute-start = (f32[2,12,384]{2,1,0:T(8,128)S(1)}, f32[2,12,384]{2,1,0:T(8,128)S(1)}, u32[]{:S(2)}, u32[]{:S(2)}) collective-permute-start(f32[2,12,384]{2,1,0:T(8,128)S(1)} %slice.44), channel_id=1, source_target_pairs={{0,240},{16,0},{32,16},{48,32},{64,48},{80,64},{96,80},{112,96},{1... | collective-permute-start | bytes 110600 | tf_op jit(solution)/shard_map/ppermute | solution.py:21
  33.1 25.1 %copy-start.19 = (f32[384,128]{1,0:T(8,128)}, f32[384,128]{1,0:T(8,128)S(1)}, u32[]{:S(2)}) copy-start(f32[384,128]{1,0:T(8,128)S(1)} %get-tuple-element.51.own_north1.refs_9_.refs_2_) | copy-start | bytes 589828
  33.1 87.4 %copy-start.6 = (bf16[96,1536]{1,0:T(8,128)(2,1)}, bf16[96,1536]{1,0:T(8,128)(2,1)S(1)}, u32[]{:S(2)}) copy-start(bf16[96,1536]{1,0:T(8,128)(2,1)S(1)} %get-tuple-element.64.refs_4_.edges) | copy-start | bytes 884740
  33.1 16.9 %all-to-all-start.1 = ((f32[8,48,128]{2,1,0:T(8,128)}), f32[8,48,128]{2,1,0:T(8,128)S(1)}, u32[]{:S(2)}, u32[]{:S(2)}) async-start(f32[8,48,128]{2,1,0:T(8,128)} %copy-done.66), calls=%async_computation.1 | async-start | bytes 393216 | tf_op jit(solution)/shard_map/all_to_all | solution.py:27
  41.3 16.9 %collective-permute-start.3 = (f32[2,384,128]{2,1,0:T(8,128)S(1)}, f32[2,384,128]{2,1,0:T(8,128)}, u32[]{:S(2)}, u32[]{:S(2)}) collective-permute-start(f32[2,384,128]{2,1,0:T(8,128)S(1)} %get-tuple-element.50.own_east.refs_7_.refs_0_), channel_id=1, source_target_pairs={{0,16},{16,32},{32,48},{48,64},{64,80},{80,96},{96,112},{112,128},... | collective-permute-start | bytes 1179656 | tf_op jit(solution)/shard_map/ppermute | solution.py:21
  50.0 4.4 %collective-permute-start.2 = (f32[8,48,128]{2,1,0:T(8,128)S(1)}, f32[8,48,128]{2,1,0:T(8,128)}, u32[]{:S(2)}, u32[]{:S(2)}) collective-permute-start(f32[8,48,128]{2,1,0:T(8,128)S(1)} %all-to-all-done.1.refs_1_), channel_id=1, source_target_pairs={{0,1},{1,0},{2,3},{3,2},{4,5},{5,4},{6,7},{7,6},{8,9},{9,8},{10,11... | collective-permute-start | bytes 589832 | tf_op jit(solution)/shard_map/ppermute | solution.py:28
  53.2 4.3 %collective-permute-start.4 = (f32[384,128]{1,0:T(8,128)S(1)}, f32[384,128]{1,0:T(8,128)}, u32[]{:S(2)}, u32[]{:S(2)}) collective-permute-start(f32[384,128]{1,0:T(8,128)S(1)} %get-tuple-element.51.own_north1.refs_9_.refs_2_), channel_id=1, source_target_pairs={{0,1},{1,2},{2,3},{3,4},{4,5},{5,6},{6,7},{7,8},{8,9},{9,10},{10,1... | collective-permute-start | bytes 589832 | tf_op jit(solution)/shard_map/ppermute | solution.py:21
  57.5 25.3 %copy-start.85 = (f32[2,128,256]{2,1,0:T(8,128)S(1)}, f32[2,128,256]{2,1,0:T(8,128)}, u32[]{:S(2)}) copy-start(f32[2,128,256]{2,1,0:T(8,128)} %constant.29.clone) | copy-start | bytes 786436
  57.5 25.3 %copy-start.16 = (f32[384,128]{1,0:T(8,128)S(1)}, f32[384,128]{1,0:T(8,128)}, u32[]{:S(2)}) copy-start(f32[384,128]{1,0:T(8,128)} %copy-done.15) | copy-start | bytes 589828
  58.2 16.0 %all-to-all-start.2 = ((f32[8,96,128]{2,1,0:T(8,128)}), f32[8,96,128]{2,1,0:T(8,128)S(1)}, u32[]{:S(2)}, u32[]{:S(2)}) async-start(f32[8,96,128]{2,1,0:T(8,128)} %copy-done.41), calls=%async_computation.2 | async-start | bytes 786432 | tf_op jit(solution)/shard_map/all_to_all | solution.py:27
  74.2 27.8 %collective-permute-start.5 = (f32[8,96,128]{2,1,0:T(8,128)S(1)}, f32[8,96,128]{2,1,0:T(8,128)S(1)}, u32[]{:S(2)}, u32[]{:S(2)}) collective-permute-start(f32[8,96,128]{2,1,0:T(8,128)S(1)} %all-to-all-done.2.same), channel_id=1, source_target_pairs={{0,1},{1,0},{2,3},{3,2},{4,5},{5,4},{6,7},{7,6},{8,9},{9,8},{10,11... | collective-permute-start | bytes 1179656 | tf_op jit(solution)/shard_map/ppermute | solution.py:28
  78.2 23.9 %collective-permute-start.6 = (f32[2,8,16,128]{3,2,1,0:T(8,128)S(1)}, f32[2,8,16,128]{3,2,1,0:T(8,128)S(1)}, u32[]{:S(2)}, u32[]{:S(2)}) collective-permute-start(f32[2,8,16,128]{3,2,1,0:T(8,128)S(1)} %pad_maximum_fusion), channel_id=1, source_target_pairs={{0,240},{16,0},{32,16},{48,32},{64,48},{80,64},{96,80},{112,96},{1... | collective-permute-start | bytes 393224 | tf_op jit(solution)/shard_map/ppermute | solution.py:21
  82.7 19.4 %collective-permute-start.7 = (f32[2,8,16,128]{3,2,1,0:T(8,128)S(1)}, f32[2,8,16,128]{3,2,1,0:T(8,128)S(1)}, u32[]{:S(2)}, u32[]{:S(2)}) collective-permute-start(f32[2,8,16,128]{3,2,1,0:T(8,128)S(1)} %pad_maximum_fusion.1), channel_id=1, source_target_pairs={{0,16},{16,32},{32,48},{48,64},{64,80},{80,96},{96,112},{112,128},... | collective-permute-start | bytes 393224 | tf_op jit(solution)/shard_map/ppermute | solution.py:21
  82.8 21.4 %copy-start.9 = (f32[128,256]{1,0:T(8,128)}, f32[128,256]{1,0:T(8,128)S(1)}, u32[]{:S(2)}) copy-start(f32[128,256]{1,0:T(8,128)S(1)} %dynamic-slice_bitcast_fusion.lanes) | copy-start | bytes 393220
  92.2 9.8 %copy-start.82 = (f32[384,128]{1,0:T(8,128)}, f32[384,128]{1,0:T(8,128)S(1)}, u32[]{:S(2)}) copy-start(f32[384,128]{1,0:T(8,128)S(1)} %get-tuple-element.59) | copy-start | bytes 589828
  92.2 24.4 %collective-permute-start.8 = (f32[2,384,128]{2,1,0:T(8,128)}, f32[2,384,128]{2,1,0:T(8,128)}, u32[]{:S(2)}, u32[]{:S(2)}) collective-permute-start(f32[2,384,128]{2,1,0:T(8,128)} %get-tuple-element.58), channel_id=1, source_target_pairs={{0,240},{16,0},{32,16},{48,32},{64,48},{80,64},{96,80},{112,96},{1... | collective-permute-start | bytes 1179656 | tf_op jit(solution)/shard_map/ppermute | solution.py:21
  106.9 12.8 %all-to-all-start.3 = ((f32[16,48,128]{2,1,0:T(8,128)}), f32[16,48,128]{2,1,0:T(8,128)S(1)}, u32[]{:S(2)}, u32[]{:S(2)}) async-start(f32[16,48,128]{2,1,0:T(8,128)} %copy-done.42), calls=%async_computation.3 | async-start | bytes 786432 | tf_op jit(solution)/shard_map/all_to_all | solution.py:495
  110.4 5.5 %collective-permute-start.9 = (f32[384,128]{1,0:T(8,128)}, f32[384,128]{1,0:T(8,128)S(1)}, u32[]{:S(2)}, u32[]{:S(2)}) collective-permute-start(f32[384,128]{1,0:T(8,128)} %copy-done.82), channel_id=1, source_target_pairs={{0,15},{1,0},{2,1},{3,2},{4,3},{5,4},{6,5},{7,6},{8,7},{9,8},{10,9... | collective-permute-start | bytes 589832 | tf_op jit(solution)/shard_map/ppermute | solution.py:21
  129.0 12.0 %all-to-all-start.4 = ((f32[8,48,128]{2,1,0:T(8,128)}), f32[8,48,128]{2,1,0:T(8,128)S(1)}, u32[]{:S(2)}, u32[]{:S(2)}) async-start(f32[8,48,128]{2,1,0:T(8,128)} %copy-done.67), calls=%async_computation.4 | async-start | bytes 393216 | tf_op jit(solution)/shard_map/all_to_all | solution.py:27
  132.4 13.7 %collective-permute-start.10 = (f32[2,384,128]{2,1,0:T(8,128)S(1)}, f32[2,384,128]{2,1,0:T(8,128)S(1)}, u32[]{:S(2)}, u32[]{:S(2)}) collective-permute-start(f32[2,384,128]{2,1,0:T(8,128)S(1)} %get-tuple-element.69.own_east.prev_east.refs_3_), channel_id=1, source_target_pairs={{0,16},{16,32},{32,48},{48,64},{64,80},{80,96},{96,112},{112,128},... | collective-permute-start | bytes 1179656 | tf_op jit(solution)/shard_map/ppermute | solution.py:21
  132.6 13.4 %collective-permute-start.11 = (f32[384,128]{1,0:T(8,128)}, f32[384,128]{1,0:T(8,128)S(1)}, u32[]{:S(2)}, u32[]{:S(2)}) collective-permute-start(f32[384,128]{1,0:T(8,128)} %copy-done.27), channel_id=1, source_target_pairs={{0,1},{1,2},{2,3},{3,4},{4,5},{5,6},{6,7},{7,8},{8,9},{9,10},{10,1... | collective-permute-start | bytes 589832 | tf_op jit(solution)/shard_map/ppermute | solution.py:21
  140.9 19.7 %collective-permute-start.16 = (f32[8,48,128]{2,1,0:T(8,128)S(1)}, f32[8,48,128]{2,1,0:T(8,128)S(1)}, u32[]{:S(2)}, u32[]{:S(2)}) collective-permute-start(f32[8,48,128]{2,1,0:T(8,128)S(1)} %all-to-all-done.4.refs_3_), channel_id=1, source_target_pairs={{0,1},{1,0},{2,3},{3,2},{4,5},{5,4},{6,7},{7,6},{8,9},{9,8},{10,11... | collective-permute-start | bytes 589832 | tf_op jit(solution)/shard_map/ppermute | solution.py:28
  144.6 16.1 %collective-permute-start.15 = (f32[256,128]{1,0:T(8,128)}, f32[256,128]{1,0:T(8,128)S(1)}, u32[]{:S(2)}, u32[]{:S(2)}) collective-permute-start(f32[256,128]{1,0:T(8,128)} %copy-done.12), channel_id=1, source_target_pairs={{0,240},{16,0},{32,16},{48,32},{64,48},{80,64},{96,80},{112,96},{1... | collective-permute-start | bytes 393224 | tf_op jit(solution)/shard_map/ppermute | solution.py:21
  145.5 15.2 %collective-permute-start.14 = (f32[256,128]{1,0:T(8,128)}, f32[256,128]{1,0:T(8,128)S(1)}, u32[]{:S(2)}, u32[]{:S(2)}) collective-permute-start(f32[256,128]{1,0:T(8,128)} %copy-done.12), channel_id=1, source_target_pairs={{0,16},{16,32},{32,48},{48,64},{64,80},{80,96},{96,112},{112,128},... | collective-permute-start | bytes 393224 | tf_op jit(solution)/shard_map/ppermute | solution.py:21
  151.6 9.1 %copy-start.10 = (f32[128,256]{1,0:T(8,128)S(1)}, f32[128,256]{1,0:T(8,128)}, u32[]{:S(2)}) copy-start(f32[128,256]{1,0:T(8,128)} %copy-done.9) | copy-start | bytes 393220
  151.6 9.1 %copy-start.13 = (f32[256,128]{1,0:T(8,128)S(1)}, f32[256,128]{1,0:T(8,128)}, u32[]{:S(2)}) copy-start(f32[256,128]{1,0:T(8,128)} %copy-done.12) | copy-start | bytes 393220
  156.4 22.3 %collective-permute-start.12 = (f32[2,384,128]{2,1,0:T(8,128)}, f32[2,384,128]{2,1,0:T(8,128)}, u32[]{:S(2)}, u32[]{:S(2)}) collective-permute-start(f32[2,384,128]{2,1,0:T(8,128)} %get-tuple-element.73), channel_id=1, source_target_pairs={{0,240},{16,0},{32,16},{48,32},{64,48},{80,64},{96,80},{112,96},{1... | collective-permute-start | bytes 1179656 | tf_op jit(solution)/shard_map/ppermute | solution.py:21
  163.6 15.2 %all-to-all-start.5 = ((f32[16,48,128]{2,1,0:T(8,128)}), f32[16,48,128]{2,1,0:T(8,128)S(1)}, u32[]{:S(2)}, u32[]{:S(2)}) async-start(f32[16,48,128]{2,1,0:T(8,128)} %shard_map.114), calls=%async_computation.5 | async-start | bytes 786432 | tf_op jit(solution)/shard_map/all_to_all | solution.py:495
  167.4 10.7 %collective-permute-start.13 = (f32[384,128]{1,0:T(8,128)}, f32[384,128]{1,0:T(8,128)S(1)}, u32[]{:S(2)}, u32[]{:S(2)}) collective-permute-start(f32[384,128]{1,0:T(8,128)} %get-tuple-element.74), channel_id=1, source_target_pairs={{0,15},{1,0},{2,1},{3,2},{4,3},{5,4},{6,5},{7,6},{8,7},{9,8},{10,9... | collective-permute-start | bytes 589832 | tf_op jit(solution)/shard_map/ppermute | solution.py:21
  189.4 14.2 %all-to-all-start.6 = ((f32[8,48,128]{2,1,0:T(8,128)}), f32[8,48,128]{2,1,0:T(8,128)S(1)}, u32[]{:S(2)}, u32[]{:S(2)}) async-start(f32[8,48,128]{2,1,0:T(8,128)} %copy-done.68), calls=%async_computation.6 | async-start | bytes 393216 | tf_op jit(solution)/shard_map/all_to_all | solution.py:27
  192.8 14.1 %collective-permute-start.17 = (f32[2,384,128]{2,1,0:T(8,128)S(1)}, f32[2,384,128]{2,1,0:T(8,128)S(1)}, u32[]{:S(2)}, u32[]{:S(2)}) collective-permute-start(f32[2,384,128]{2,1,0:T(8,128)S(1)} %get-tuple-element.77.own_east.prev_east.refs_6_), channel_id=1, source_target_pairs={{0,16},{16,32},{32,48},{48,64},{64,80},{80,96},{96,112},{112,128},... | collective-permute-start | bytes 1179656 | tf_op jit(solution)/shard_map/ppermute | solution.py:21
  194.2 10.0 %collective-permute-start.18 = (f32[384,128]{1,0:T(8,128)}, f32[384,128]{1,0:T(8,128)S(1)}, u32[]{:S(2)}, u32[]{:S(2)}) collective-permute-start(f32[384,128]{1,0:T(8,128)} %copy-done.34), channel_id=1, source_target_pairs={{0,1},{1,2},{2,3},{3,4},{4,5},{5,6},{6,7},{7,8},{8,9},{9,10},{10,1... | collective-permute-start | bytes 589832 | tf_op jit(solution)/shard_map/ppermute | solution.py:21
  203.6 15.7 %collective-permute-start.21 = (f32[8,48,128]{2,1,0:T(8,128)S(1)}, f32[8,48,128]{2,1,0:T(8,128)S(1)}, u32[]{:S(2)}, u32[]{:S(2)}) collective-permute-start(f32[8,48,128]{2,1,0:T(8,128)S(1)} %all-to-all-done.6.refs_3_), channel_id=1, source_target_pairs={{0,1},{1,0},{2,3},{3,2},{4,5},{5,4},{6,7},{7,6},{8,9},{9,8},{10,11... | collective-permute-start | bytes 589832 | tf_op jit(solution)/shard_map/ppermute | solution.py:28
  217.3 18.8 %collective-permute-start.19 = (f32[2,384,128]{2,1,0:T(8,128)}, f32[2,384,128]{2,1,0:T(8,128)}, u32[]{:S(2)}, u32[]{:S(2)}) collective-permute-start(f32[2,384,128]{2,1,0:T(8,128)} %get-tuple-element.81), channel_id=1, source_target_pairs={{0,240},{16,0},{32,16},{48,32},{64,48},{80,64},{96,80},{112,96},{1... | collective-permute-start | bytes 1179656 | tf_op jit(solution)/shard_map/ppermute | solution.py:21
  220.9 15.2 %all-to-all-start.7 = ((f32[16,48,128]{2,1,0:T(8,128)}), f32[16,48,128]{2,1,0:T(8,128)}, u32[]{:S(2)}, u32[]{:S(2)}) async-start(f32[16,48,128]{2,1,0:T(8,128)} %shard_map.118), calls=%async_computation.7 | async-start | bytes 786432 | tf_op jit(solution)/shard_map/all_to_all | solution.py:495
  225.1 10.3 %collective-permute-start.20 = (f32[384,128]{1,0:T(8,128)}, f32[384,128]{1,0:T(8,128)S(1)}, u32[]{:S(2)}, u32[]{:S(2)}) collective-permute-start(f32[384,128]{1,0:T(8,128)} %copy-done.83), channel_id=1, source_target_pairs={{0,15},{1,0},{2,1},{3,2},{4,3},{5,4},{6,5},{7,6},{8,7},{9,8},{10,9... | collective-permute-start | bytes 589832 | tf_op jit(solution)/shard_map/ppermute | solution.py:21
  239.9 27.1 %copy-start.18 = (f32[384,128]{1,0:T(8,128)S(1)}, f32[384,128]{1,0:T(8,128)}, u32[]{:S(2)}) copy-start(f32[384,128]{1,0:T(8,128)} %copy-done.15) | copy-start | bytes 589828
  239.9 27.1 %copy-start.22 = (f32[384,128]{1,0:T(8,128)S(1)}, f32[384,128]{1,0:T(8,128)}, u32[]{:S(2)}) copy-start(f32[384,128]{1,0:T(8,128)} %copy-done.19) | copy-start | bytes 589828
  239.9 27.1 %copy-start.26 = (f32[384,128]{1,0:T(8,128)S(1)}, f32[384,128]{1,0:T(8,128)}, u32[]{:S(2)}) copy-start(f32[384,128]{1,0:T(8,128)} %copy-done.23) | copy-start | bytes 589828
  239.9 27.1 %copy-start.30 = (f32[384,128]{1,0:T(8,128)S(1)}, f32[384,128]{1,0:T(8,128)}, u32[]{:S(2)}) copy-start(f32[384,128]{1,0:T(8,128)} %copy-done.27) | copy-start | bytes 589828
  239.9 27.1 %copy-start.51 = (f32[4,384,128]{2,1,0:T(8,128)S(1)}, f32[4,384,128]{2,1,0:T(8,128)}, u32[]{:S(2)}) copy-start(f32[4,384,128]{2,1,0:T(8,128)} %copy-done.50) | copy-start | bytes 2359300
  239.9 27.1 %copy-start.53 = (f32[4,384,128]{2,1,0:T(8,128)S(1)}, f32[4,384,128]{2,1,0:T(8,128)}, u32[]{:S(2)}) copy-start(f32[4,384,128]{2,1,0:T(8,128)} %copy-done.52) | copy-start | bytes 2359300
  239.9 27.1 %copy-start.55 = (f32[4,384,128]{2,1,0:T(8,128)S(1)}, f32[4,384,128]{2,1,0:T(8,128)}, u32[]{:S(2)}) copy-start(f32[4,384,128]{2,1,0:T(8,128)} %copy-done.54) | copy-start | bytes 2359300
  (69 other events, 111.3 us)

commit v3 on v2

v3 whole, which is shorter than its diff:
```python
import functools
import math

import numpy as np
import jax
import jax.numpy as jnp
from jax import lax
from jax.experimental import pallas as pl
from jax.experimental.pallas import tpu as pltpu
from jax.sharding import PartitionSpec as P

CS = 3
NEAR = 16
ROWS = 3 * NEAR
F32, BF16 = jnp.float32, jnp.bfloat16
SMEM = pl.BlockSpec(memory_space=pltpu.SMEM)


def shifted(array, axis, by):
    count = lax.axis_size(axis)
    return lax.ppermute(array, axis, [(i, (i + by) % count) for i in range(count)])


def along_sy(copies, beside=None):
    count = lax.axis_size("sy")
    groups = [[2 * z + core for z in range(count // 2)] for core in range(2)]
    same = lax.all_to_all(copies, "sy", 0, 0, tiled=True, axis_index_groups=groups)
    if beside is not None:
        same, beside = lax.optimization_barrier((same, beside))
    other = lax.ppermute(same, "sy", [(i, i ^ 1) for i in range(count)])
    return (same, other) if beside is None else (same, other, beside)


class Arriving:
    def __init__(self, source, held, arrived):
        self.copy = pltpu.make_async_copy(source, held, arrived)
        self.copy.start()
        self.held, self.shape, self.waiting = held, held.shape, True

    def settle(self):
        if self.waiting:
            self.copy.wait()
        self.waiting = False

    def __getitem__(self, index):
        self.settle()
        return self.held[index]


class Leaving:
    def __init__(self, held, target, arrived):
        self.copy = pltpu.make_async_copy(held, target, arrived)
        self.held, self.shape, self.sent = held, held.shape, False

    def __getitem__(self, index):
        return self.held[index]

    def __setitem__(self, index, value):
        self.held[index] = value

    def send(self):
        if not self.sent:
            self.copy.start()
        self.sent = True


def kernel_call(body, outs, operands, scalars=0, raw=(), scratch=(), fast=(), fast_outs=()):
    several = isinstance(outs, tuple)
    outs = outs if several else (outs,)
    operands = tuple(operands)
    count_in, count_out = len(operands), len(outs)
    slow_in = [k for k in range(scalars, count_in) if k not in fast]
    slow_out = [k for k in range(count_out) if k not in fast_outs]
    held = [pltpu.VMEM(operands[k].shape, operands[k].dtype) for k in slow_in]
    held += [pltpu.VMEM(outs[k].shape, outs[k].dtype) for k in slow_out]
    arrays = list(operands) + list(raw)
    moved = sum(4 * math.prod(array.shape) for array in arrays + list(outs))

    def wrapped(*refs):
        refs = list(refs)
        ins, refs = refs[: len(arrays)], refs[len(arrays) :]
        results, refs = refs[:count_out], refs[count_out:]
        buffers, refs = refs[: len(held)], refs[len(held) :]
        arrived, extra = refs[0], refs[1:]
        for n, k in enumerate(slow_in):
            ins[k] = Arriving(ins[k], buffers[n], arrived.at[n])
        for n, k in enumerate(slow_out, len(slow_in)):
            results[k] = Leaving(buffers[n], results[k], arrived.at[n])
        body(*ins, *results, *extra)
        for k in slow_in:
            ins[k].settle()
        for k in slow_out:
            results[k].send()
        for k in slow_out:
            results[k].copy.wait()

    def spec(k):
        return SMEM if k < scalars else pl.BlockSpec(memory_space=pltpu.VMEM if k in fast else pltpu.HBM)

    arrays = [
        array if k < scalars or k in fast else pltpu.with_memory_space_constraint(array, pltpu.HBM)
        for k, array in enumerate(arrays)
    ]
    out_specs = tuple(
        pl.BlockSpec(memory_space=pltpu.VMEM if k in fast_outs else pltpu.HBM) for k in range(count_out)
    )
    out_shape = tuple(
        (pltpu.VMEM if k in fast_outs else pltpu.HBM)(array.shape, array.dtype) for k, array in enumerate(outs)
    )
    got = pl.pallas_call(
        wrapped,
        in_specs=[spec(k) for k in range(len(arrays))],
        out_specs=out_specs,
        out_shape=out_shape,
        scratch_shapes=held + [pltpu.SemaphoreType.DMA((max(len(held), 1),))] + list(scratch),
        compiler_params=pltpu.CompilerParams(vmem_limit_bytes=16 * 2**20),
        cost_estimate=pl.CostEstimate(flops=4 * moved, bytes_accessed=moved, transcendentals=0),
    )(*arrays)
    return tuple(got) if several else got[0]


def split(value):
    high = value.astype(BF16)
    return high, (value - high.astype(F32)).astype(BF16)


def halves(value):
    return jnp.concatenate(split(value), 1)


def multiply(first, second):
    return jnp.dot(first, second, preferred_element_type=F32)


def place_matrices():
    place = [(0, 0), (-1, 0), (0, -1), (-1, -1)]
    out = np.zeros((4, ROWS, 32), np.float32)
    for s in range(2):
        for e in range(2):
            for k, (di, dj) in enumerate(place):
                for c in range(CS):
                    out[2 * s + e, (1 + di) * NEAR + (1 + s + dj) * CS + c, k * CS + c] += 1
                    row = (1 + di + (1 - e)) * NEAR + (1 + s + dj + e) * CS + c
                    out[2 * s + e, row, 16 + k * CS + c] -= 1
    return out


def lane_matrices(gy):
    out = np.zeros((2, 128, gy * NEAR), np.float32)
    for core in range(2):
        for slot in range(gy):
            z, other = slot % (gy // 2), slot // (gy // 2)
            source = 2 * z + (core ^ other)
            for jj in range(4):
                for c in range(CS):
                    j = (2 * source - 1 + jj) % (2 * gy)
                    out[core, j * CS + c, slot * NEAR + jj * CS + c] = 1
    return out


def message_to(out_ref, basis_ref, parts, extra):
    got = multiply(basis_ref[...], parts[...].reshape(basis_ref.shape[1], parts.shape[2]))
    cases = got.shape[1] // 2
    rows = got[:ROWS, :cases] + got[:ROWS, cases:] + got[ROWS:, :cases]
    index = lax.broadcasted_iota(jnp.int32, rows.shape, 0)
    for k, row in enumerate(extra):
        rows = jnp.where(index == NEAR - 4 + k, row, rows)
    for copy in range(out_ref.shape[0]):
        out_ref[copy] = rows
    return rows


def column_sum(value):
    return jnp.sum(value, axis=0, keepdims=True)


def wide_body(me, corner, coarse, out):
    block = coarse.shape[0]
    count = out.shape[0]
    lane = lax.broadcasted_iota(jnp.int32, (block, out.shape[2] - block), 1)
    spare = jnp.where(lane == 2 * me[0], corner[0, 0], 0) + jnp.where(lane == 2 * me[0] + 1, corner[1, 0], 0)
    wide = jnp.concatenate([coarse[...], spare.astype(F32)], 1)
    for copy in range(count):
        out[copy] = wide


def begin_body(count, corner, rhs, scaling, basis, east, above, places, coarse, blocks, *refs):
    res, east0, north0, north1, gain, edges, message, parts, tiles, moved = refs
    side, cases = rhs.shape[1], rhs.shape[2]
    copies = [
        pltpu.make_async_copy(blocks.at[4 * s, pl.ds(0, cases), pl.ds(0, cases)], tiles.at[s], moved.at[s])
        for s in range(2)
    ]
    for copy in copies:
        copy.start()
    high, low = split(scaling[...])
    least = (scaling[...] - high.astype(F32) - low.astype(F32)).astype(BF16)
    thirds = jnp.concatenate([high.astype(F32), low.astype(F32), least.astype(F32)], 0).astype(BF16)
    row = lax.broadcasted_iota(jnp.int32, (12, cases), 0)
    norm = jnp.zeros((1, cases), F32)
    for edge in range(4):
        s, e = divmod(edge, 2)
        index = lax.broadcasted_iota(jnp.int32, (side, cases), 0)
        mask = index < count[s, e]
        chosen = (row % 4 == edge).astype(F32).astype(BF16)
        wide = lax.dot_general(thirds, chosen, (((0,), (0,)), ((), ())), preferred_element_type=F32)
        gain[edge] = jnp.where(mask, wide, 0.0)
        res[edge] = jnp.where(mask, rhs[edge], 0.0)
        value = gain[edge] * res[edge]
        norm = norm + column_sum(res[edge] * value)
        put_edge(edge, value, east0, north0, north1, parts)
        own = basis[s, :, 2 * e * side : (2 * e + 1) * side].astype(BF16)
        if e == 0:
            other = east[s].astype(BF16)
        elif s == 0:
            other = basis[1, :, 3 * side :].astype(BF16)
        else:
            other = above[...].astype(BF16)
        place = places[edge].astype(BF16)
        value = multiply(place[:, : 4 * CS], own) + multiply(place[:, 16 : 16 + 4 * CS], other)
        high, low = split(value)
        edges[:ROWS, edge * side : (edge + 1) * side] = high
        edges[ROWS:, edge * side : (edge + 1) * side] = low
    for ref in (east0, north1, north0, res, gain, edges):
        ref.send()
    lane = lax.broadcasted_iota(jnp.int32, (1, cases), 1)
    numbers = jnp.where(lane == 0, corner[0, 0], 0) + jnp.where(lane == 1, corner[1, 0], 0)
    index = lax.broadcasted_iota(jnp.int32, (cases, cases), 0)
    diagonal = index == lax.broadcasted_iota(jnp.int32, (cases, cases), 1)
    size = jnp.zeros((1, cases), F32)
    for s in range(2):
        copies[s].wait()
        tile = tiles[s].astype(F32)
        size = size + jnp.sum(jnp.where(diagonal, tile, 0.0)) / (512.0 * cases)
    size = size + jnp.sum(jnp.abs(coarse[...])) / (16.0 * coarse.shape[0])
    message_to(message, edges, parts, [norm, numbers.astype(F32), size])


def put_edge(edge, value, east, north0, north1, parts):
    side = value.shape[0]
    if edge % 2 == 0:
        east[edge // 2] = value
    elif edge == 1:
        north0[...] = value
    else:
        north1[...] = value
    high, low = split(value)
    parts[edge, :, : value.shape[1]] = high
    parts[edge, :, value.shape[1] :] = low


def apply_rows(block, parts):
    out = multiply(block, parts)
    cases = out.shape[1] // 2
    return out[:, :cases] + out[:, cases:]


def fetch(source, held, arrived, wanted):
    copies = [pltpu.make_async_copy(source.at[k], held.at[n], arrived.at[n]) for n, k in enumerate(wanted)]
    for copy in copies:
        copy.start()
    return copies


def weighed(parts, s, q, out):
    side, cases = out.shape
    rows = parts[s, q * side : (q + 1) * side]
    return column_sum((rows[:, :cases].astype(F32) + rows[:, cases:].astype(F32)) * out)


GIVEN = (1, 5, 3)


def give_body(own_east, own_north0, own_north1, west, below, blocks, out_east, out_north, parts, product, held, arrived):
    copies = fetch(blocks, held, arrived, GIVEN)
    side = west.shape[1]
    for s in range(2):
        parts[s, side : 2 * side] = halves(-west[s])
    parts[0, 3 * side :] = halves(-below[...])
    for s in range(2):
        parts[s, :side] = halves(own_east[s])
    parts[0, 2 * side : 3 * side] = halves(own_north0[...])
    parts[1, 3 * side :] = halves(-own_north0[...])
    parts[1, 2 * side : 3 * side] = halves(own_north1[...])
    total = 0.0
    for n, (s, q) in enumerate([(0, 1), (1, 1), (0, 3)]):
        copies[n].wait()
        value = apply_rows(held[n], parts[s])
        if n < 2:
            out_east[s] = value
        else:
            out_north[...] = value
        if n == 1:
            out_east.send()
        total = total + weighed(parts, s, q, value)
    product[...] = jnp.broadcast_to(total, product.shape)


def keep_body(parts, product_in, blocks, out, product, held, arrived):
    copies = fetch(blocks, held, arrived, (0, 2, 7, 4, 6))
    total = product_in[0:1]
    for n, (edge, s, q) in enumerate([(0, 0, 0), (1, 0, 2), (1, 1, 3), (2, 1, 0), (3, 1, 2)]):
        copies[n].wait()
        value = apply_rows(held[n], parts[s])
        total = total + weighed(parts, s, q, value)
        out[edge] = out[edge] - value if n == 2 else value
    product[...] = jnp.broadcast_to(total, product.shape)


def sum_body(product, rows, got, out):
    total = got[0]
    for k in range(1, got.shape[0]):
        total = total + got[k]
    index = lax.broadcasted_iota(jnp.int32, total.shape, 0) % NEAR
    value = product[0:1] + column_sum(jnp.where(index < 4 * CS, rows[...] * total, 0.0))
    out[...] = jnp.broadcast_to(value, out.shape)


def arrange_body(lanes, below, own, beyond, *outs):
    lane = lanes[...].astype(BF16)
    width = lane.shape[1]
    for ii, source in enumerate([below, own, beyond]):
        high, low = split(source[...])
        high = multiply(high, lane).astype(BF16)
        low = multiply(low, lane).astype(BF16)
        outs[0][:, ii * width : (ii + 1) * width] = high
        outs[1][:, ii * width : (ii + 1) * width] = low


def row_pieces(same, other, ii):
    return [ref[z, ii * NEAR : (ii + 1) * NEAR] for ref in (same, other) for z in range(same.shape[0])]


def lay_out(value, first, out):
    gx, cases = out.shape[0], out.shape[2]
    total = first[0][NEAR - 8 :]
    for piece in first[1:]:
        total = total + piece[NEAR - 8 :]
    index = lax.broadcasted_iota(jnp.int32, (8, cases), 0)
    for target in range(gx):
        for ii in range(3):
            at = ((target - 1 + ii) % gx) * NEAR
            out[target, ii * NEAR : ii * NEAR + 8] = value[at : at + 8]
            rest = value[at + 8 : at + 16]
            if ii == 0:
                rest = jnp.where(index < 4, rest, total)
            out[target, ii * NEAR + 8 : ii * NEAR + 16] = rest


def coarse_body(high, low, same, other, out):
    cases = same.shape[2]
    pieces = [row_pieces(same, other, ii) for ii in range(3)]
    gathered = halves(jnp.concatenate(pieces[0] + pieces[1] + pieces[2], 0))
    product = multiply(high[...], gathered)
    value = product[:, :cases] + product[:, cases:] + multiply(low[...], gathered[:, :cases])
    lay_out(value, pieces[0], out)


def first_coarse_body(lanes, own, same, other, lower, upper, out):
    cases = same.shape[2]
    lane = lanes[...].astype(BF16)
    high, low = split(own[...])
    high = multiply(high, lane).astype(BF16)
    low = multiply(low, lane).astype(BF16)
    middle = row_pieces(same, other, 1)
    half = same.shape[0]
    pieces = [
        middle[k] + lower[k // half, k % half] + upper[k // half, k % half] for k in range(2 * half)
    ]
    gathered = halves(jnp.concatenate(pieces, 0))
    product = multiply(high, gathered)
    value = product[:, :cases] + product[:, cases:] + multiply(low, gathered[:, :cases])
    lay_out(value, row_pieces(same, other, 0), out)


def image_body(last, part, east, north, got, edges, gain, *refs):
    side, cases = part.shape[1], part.shape[2]
    if last:
        u_ref, spare = refs
    else:
        (prev_east, prev_north0, prev_north1), refs = refs[:3], refs[3:]
        kappa_in, refs = (refs[0], refs[1:]) if len(refs) == 10 else (None, refs)
        u_ref, w_east, w_north0, w_north1, kappa_out, spare, rows_out, message, own = refs
    total = got[0]
    for k in range(1, got.shape[0]):
        total = total + got[k]
    high, low = split(total)
    twice = jnp.concatenate(
        [jnp.concatenate([high, low], 1), jnp.concatenate([high, jnp.zeros_like(low)], 1)], 0
    )
    spare[...] = total[NEAR - 8 : NEAR]
    if not last:
        kappa = 4.0 / total[NEAR - 2 : NEAR - 1] if kappa_in is None else kappa_in[0:1]
        kappa_out[...] = jnp.broadcast_to(kappa, kappa_out.shape)
    first = jnp.zeros((1, cases), F32)
    second = jnp.zeros((1, cases), F32)
    for edge in (1, 3, 0, 2):
        coarse = lax.dot_general(
            edges[:, edge * side : (edge + 1) * side],
            twice,
            (((0,), (0,)), ((), ())),
            preferred_element_type=F32,
        )
        value = part[edge] + coarse[:, :cases] + coarse[:, cases:]
        if edge % 2 == 0:
            value = value - east[edge // 2]
        elif edge == 3:
            value = value - north[...]
        image = jnp.where(gain[edge] > 0.0, value, 0.0)
        u_ref[edge] = image
        if not last:
            previous = (prev_north0, prev_north1)[edge // 2][...] if edge % 2 else prev_east[edge // 2]
            first = first + column_sum(previous * image)
            following = kappa * gain[edge] * value
            second = second + column_sum(following * image)
            put_edge(edge, following, w_east, w_north0, w_north1, own)
    if last:
        return
    for ref in (w_east, w_north1, w_north0, u_ref):
        ref.send()
    rows_out[...] = message_to(message, edges, own, [first, second])


def image_call(part, east, north, got, edges, gain, previous, kappa, copies):
    _, side, cases = part.shape
    shape = lambda *dims: jax.ShapeDtypeStruct(dims + (cases,), F32)
    outs = (
        shape(4, side),
        shape(2, side),
        shape(side),
        shape(side),
        shape(8),
        shape(8),
        shape(ROWS),
        shape(copies, ROWS),
    )
    operands = (part, east, north, got, edges, gain, *previous) + (() if kappa is None else (kappa,))
    return kernel_call(
        functools.partial(image_body, False),
        outs,
        operands,
        scratch=(pltpu.VMEM((4, side, 2 * cases), BF16),),
        fast=range(4),
    )


def slot_of(source, core, half):
    return source // 2 + half * ((source + core) % 2)


def pick_body(numbers, me, columns, out, rows):
    half = numbers.shape[0] // 2
    block = out.shape[1]
    rows[...] = jnp.zeros_like(rows)
    core = me[1] % 2
    for j in range(4 * half):
        node = numbers[slot_of(j // 2, core, half), j % 2]
        for c in range(CS):
            at = node * CS + c
            rows[pl.ds(j * CS + c, 1)] = columns[pl.ds(at // block, 1), pl.ds(at % block, 1)].reshape(1, -1)
    turned = rows[...].T[:block]
    known = jnp.zeros((1, turned.shape[1]), F32)
    for k in range(columns.shape[0]):
        known = known + columns[k, :1]
    lane = lax.broadcasted_iota(jnp.int32, turned.shape, 1)
    turned = jnp.where(lane >= block, known, turned)
    for copy in range(half):
        out[copy] = turned


def near_body(gx, numbers, me, same, other, out):
    half = same.shape[0]
    block = same.shape[1]
    out[...] = jnp.zeros(out.shape, F32)
    core = me[1] % 2
    lane = lax.broadcasted_iota(jnp.int32, (1, same.shape[2]), 1)
    for jj in range(4):
        j = (2 * me[1] - 1 + jj + 4 * half) % (4 * half)
        slot = slot_of(j // 2, core, half)
        for i in range(gx):
            node = numbers[slot, block + 2 * i + j % 2]
            owner = node * CS // block
            row = node * CS - owner * block
            mine = owner % 2 == core
            for c in range(CS):
                first = same[pl.ds(owner // 2, 1), pl.ds(row + c, 1)].reshape(1, -1)
                second = other[pl.ds(owner // 2, 1), pl.ds(row + c, 1)].reshape(1, -1)
                value = jnp.where(mine, first, second)
                out[pl.ds(i * NEAR + jj * CS + c, 1)] = jnp.where(lane < block, value, 0.0)


def finish_body(kappa_ref, spare0, spare1, spare2, last, *refs):
    (res, *fields), (u1, u2, u3, mult_out, res_out) = refs[:10], refs[10:]
    kappa = kappa_ref[0:1]
    moments = [
        spare0[4:5],
        kappa * spare1[4:5],
        kappa * spare1[5:6],
        kappa * spare2[4:5],
        kappa * spare2[5:6],
        kappa * column_sum(last[...]),
    ]

    def form(first, second, shift):
        total = 0.0
        for i, x in enumerate(first):
            for j, y in enumerate(second):
                total = total + x * y * moments[i + j + shift]
        return total

    one = jnp.ones_like(kappa)
    rho, pi, gamma = [one], [one], []
    rz = moments[0]
    for iteration in range(3):
        step = rz / form(pi, pi, 1)
        gamma = [(gamma[k] if k < len(gamma) else 0.0) + step * pi[k] for k in range(len(pi))]
        rho = [one] + [-value for value in gamma]
        if iteration < 2:
            rz_new = form(rho, rho, 0)
            ratio = rz_new / rz
            pi = [rho[k] + (ratio * pi[k] if k < len(pi) else 0.0) for k in range(len(rho))]
            rz = rz_new
    gamma = [kappa * value for value in gamma]
    for edge in range(4):
        total = 0.0
        for k in range(3):
            east, north0, north1 = fields[3 * k : 3 * k + 3]
            value = east[edge // 2] if edge % 2 == 0 else (north0, north1)[edge // 2][...]
            total = total + gamma[k] * value
        mult_out[edge] = total
    mult_out.send()
    for edge in range(4):
        res_out[edge] = res[edge] - (gamma[0] * u1[edge] + gamma[1] * u2[edge] + gamma[2] * u3[edge])


def local(dual_rhs, scaling, dual_count, corner_map, local_ops, corner_basis, coarse_inverse):
    gx, gy = lax.axis_size("sx"), lax.axis_size("sy")
    a, b = lax.axis_index("sx"), lax.axis_index("sy")
    side, cases = dual_rhs.shape[3], dual_rhs.shape[4]
    rhs = dual_rhs.reshape(4, side, cases)
    blocks = local_ops.reshape(8, side, 4 * side)
    block = coarse_inverse.shape[0]
    half = gy // 2
    basis = corner_basis[0]
    me = jnp.stack([a, b]).astype(jnp.int32)
    shape = lambda *dims: jax.ShapeDtypeStruct(dims + (cases,), F32)
    field = shape(4, side)
    double = lambda *dims: jax.ShapeDtypeStruct(dims + (2 * cases,), BF16)
    wide = kernel_call(wide_body, shape(gx, block), (me, corner_map[0], coarse_inverse), 2)
    columns_all = lax.all_to_all(wide, "sx", 0, 0, tiled=True)
    wide_basis = basis.astype(F32)
    east = shifted(wide_basis[:, :, side : 2 * side], "sx", -1)
    above = shifted(wide_basis[0, :, 3 * side :], "sy", -1)

    residual, *w0, gain, edges, message = kernel_call(
        begin_body,
        (
            field,
            shape(2, side),
            shape(side),
            shape(side),
            field,
            jax.ShapeDtypeStruct((2 * ROWS, 4 * side), BF16),
            shape(half, ROWS),
        ),
        (
            dual_count[0],
            corner_map[0],
            rhs,
            scaling.reshape(4, side),
            wide_basis,
            east,
            above,
            jnp.asarray(place_matrices()),
            coarse_inverse,
        ),
        2,
        raw=(blocks,),
        scratch=(
            pltpu.VMEM((4, side, 2 * cases), BF16),
            pltpu.VMEM((2, cases, cases), BF16),
            pltpu.SemaphoreType.DMA((2,)),
        ),
        fast=(4, 5, 6),
    )
    message, columns_all = lax.optimization_barrier((message, columns_all))

    def halo(vector):
        return shifted(vector[0], "sx", 1), shifted(vector[2], "sy", 1)

    def held(count):
        return (pltpu.VMEM((count,) + blocks.shape[1:], BF16), pltpu.SemaphoreType.DMA((count,)))

    def give(own, west, below):
        given_east, given_north, parts, product = kernel_call(
            give_body,
            (shape(2, side), shape(side), double(2, 4 * side), shape(8)),
            (*own, west, below),
            raw=(blocks,),
            scratch=held(3),
            fast=(3, 4),
            fast_outs=(2,),
        )
        return (parts, product), shifted(given_east, "sx", -1), shifted(given_north, "sy", -1)

    def keep(given):
        return kernel_call(
            keep_body, (field, shape(8)), given, raw=(blocks,), scratch=held(5), fast=(0,), fast_outs=(0,)
        )

    west, below = halo(w0)
    same, other = along_sy(message)
    lower = shifted(jnp.stack([same[:, :NEAR], other[:, :NEAR]]), "sx", -1)
    upper = shifted(jnp.stack([same[:, 2 * NEAR :], other[:, 2 * NEAR :]]), "sx", 1)
    numbers = jnp.concatenate([same[:, NEAR - 3], other[:, NEAR - 3]], 0).astype(jnp.int32)
    turned = kernel_call(
        pick_body,
        shape(half, block),
        (numbers, me, columns_all),
        2,
        scratch=(pltpu.VMEM((cases, cases), F32),),
        fast=(2,),
    )
    turned, west, below = lax.optimization_barrier((turned, west, below))
    given, back_east, back_north = give(w0, west, below)
    kept, _ = keep(given)
    rows_same, rows_other, (kept, lower, upper) = along_sy(turned, (kept, lower, upper))
    numbers = jnp.concatenate([rows_same[:, 0], rows_other[:, 0]], 0).astype(jnp.int32)
    own_part = kernel_call(
        functools.partial(near_body, gx),
        shape(gx * NEAR),
        (numbers, me, rows_same, rows_other),
        2,
        fast=(2, 3),
    )
    below_part = shifted(own_part, "sx", 1)
    beyond_part = shifted(own_part, "sx", -1)
    lanes = lax.dynamic_index_in_dim(jnp.asarray(lane_matrices(gy)), b % 2, 0, keepdims=False)

    send = kernel_call(
        first_coarse_body,
        shape(gx, ROWS),
        (lanes, own_part, same, other, lower, upper),
        fast=range(2, 6),
    )
    got = lax.all_to_all(send, "sx", 0, 0, tiled=True)
    u1, *w1, kappa, spare0, _, message = image_call(
        kept, back_east, back_north, got, edges, gain, w0, None, half
    )
    w_shape = jax.ShapeDtypeStruct((gx * NEAR, ROWS * gy), BF16)
    high, low = kernel_call(
        arrange_body, (w_shape, w_shape), (lanes, below_part, own_part, beyond_part), fast=(1, 3)
    )

    def coarse_solve(same, other):
        send = kernel_call(coarse_body, shape(gx, ROWS), (high, low, same, other), fast=(2, 3))
        return lax.all_to_all(send, "sx", 0, 0, tiled=True)

    west, below = halo(w1)
    same, other = along_sy(message)
    given, back_east, back_north = give(w1, west, below)
    got = coarse_solve(same, other)
    kept, _ = keep(given)
    u2, *w2, _, spare1, rows, message = image_call(
        kept, back_east, back_north, got, edges, gain, w1, kappa, half
    )
    west, below = halo(w2)
    same, other = along_sy(message)
    given, back_east, back_north = give(w2, west, below)
    got = coarse_solve(same, other)
    kept, product = keep(given)
    last = kernel_call(sum_body, shape(gx * gy), (product, rows, got), fast=(2,))
    last = lax.all_to_all(last.reshape(gx * gy, 1, cases), ("sx", "sy"), 0, 0, tiled=True)
    u3, spare2 = kernel_call(
        functools.partial(image_body, True),
        (field, shape(8)),
        (kept, back_east, back_north, got, edges, gain),
        fast=range(4),
    )
    multipliers, residual = kernel_call(
        finish_body,
        (field, field),
        (
            kappa,
            spare0,
            spare1,
            spare2,
            last.reshape(gx * gy, cases),
            residual,
            *w0,
            *w1,
            *w2,
            u1,
            u2,
            u3,
        ),
        fast=(4,),
    )
    return multipliers.reshape(dual_rhs.shape), residual.reshape(dual_rhs.shape)


def solution(mesh):
    in_specs = (
        P("sx", "sy", None, None, None),
        P("sx", "sy", None, None),
        P("sx", "sy", None),
        P("sx", "sy", None),
        P("sx", "sy", None, None),
        P("sx", "sy", None, None),
        P("sx", "sy"),
    )
    out_specs = (P("sx", "sy", None, None, None), P("sx", "sy", None, None, None))
    return jax.shard_map(local, mesh=mesh, in_specs=in_specs, out_specs=out_specs, check_vma=False)
```

time: 271 us -> 223 us (0.82)
  local copies, waits for them, and re-layouts: 71 us -> 2.27 us
  Pallas kernels: 43.9 us -> 68.4 us
  starting transfers between devices: 82.1 us -> 95.5 us
  blocking collectives: 25.3 us -> 12 us
  waiting for transfers between devices: 44.7 us -> 41.8 us
    unnamed x174 -> x24, local copies, waits for them, and re-layouts: 65.4 us -> 0.73 us
    pallas_call x17 -> x19, Pallas kernels: 43.9 us -> 68.4 us  [kernel_call(): pl.pallas_call(wrapped, in_specs=[spec(k) for k in range(len(arrays))], o...]
    all_to_all x4 -> x3, waiting for transfers between devices: 31.3 us -> 12.1 us  [along_sy(): lax.all_to_all(copies, 'sy', 0, 0, tiled=True, axis_index_groups=groups)]
    all_to_all x1, blocking collectives: 25.3 us -> 12 us  [along_sy(): lax.all_to_all(copies, 'sy', 0, 0, tiled=True, axis_index_groups=groups)]
    all_to_all x0 -> x2, starting transfers between devices: none -> 12.3 us  [the longest x1 8.77 us: local(): lax.all_to_all(last.reshape(gx * gy, 1, cases), ('sx', 'sy'), 0, 0, tiled...]
    ppermute x18, waiting for transfers between devices: 9.38 us -> 18.2 us  [shifted(): lax.ppermute(array, axis, [(i, (i + by) % count) for i in range(count)])]
    all_to_all x0 -> x2, waiting for transfers between devices: none -> 7.75 us  [the longest x1 4.05 us: local(): got = lax.all_to_all(send, 'sx', 0, 0, tiled=True)]
    ppermute x4, starting transfers between devices: 10.4 us -> 14.1 us  [along_sy(): other = lax.ppermute(same, 'sy', [(i, i ^ 1) for i in range(count)])]
  transfers between devices with their start and end apart: 30 -> 30, of which waited for: 9 -> 13; matrix products, arithmetic and copies ran while one was open for 2% -> 1% of each run, Pallas kernels for 13% -> 25%
where the time goes in v3:
time: 223 us; the launch traced here: 222 us
  starting transfers between devices  95.5 us (43%)
  Pallas kernels  68.4 us (31%)
  waiting for transfers between devices  41.8 us (19%)
  blocking collectives  12 us (5%)
  local copies, waits for them, and re-layouts  2.27 us (1%)
    pallas_call x19, Pallas kernels, kernel_call(): pl.pallas_call(wrapped, in_specs=[spec(k) for k in range(len(arrays))], o...  68.4 us
    ppermute x18, starting transfers between devices, shifted(): lax.ppermute(array, axis, [(i, (i + by) % count) for i in range(count)])  34.1 us
    all_to_all x3, starting transfers between devices, along_sy(): lax.all_to_all(copies, 'sy', 0, 0, tiled=True, axis_index_groups=groups)  18.5 us
    ppermute x18, waiting for transfers between devices, shifted(): lax.ppermute(array, axis, [(i, (i + by) % count) for i in range(count)])  18.2 us
    ppermute x4, starting transfers between devices, along_sy(): other = lax.ppermute(same, 'sy', [(i, i ^ 1) for i in range(count)])  14.1 us
    all_to_all x3, waiting for transfers between devices, along_sy(): lax.all_to_all(copies, 'sy', 0, 0, tiled=True, axis_index_groups=groups)  12.1 us
    all_to_all x1, blocking collectives, along_sy(): lax.all_to_all(copies, 'sy', 0, 0, tiled=True, axis_index_groups=groups)  12 us
    all_to_all x2, starting transfers between devices, coarse_solve(): return lax.all_to_all(send, 'sx', 0, 0, tiled=True)  8.82 us
  transfers between devices with their start and end apart: 30, of which 13 were waited for; matrix products, arithmetic and copies ran while one was open for 1% of the time, Pallas kernels for 25%

profile of v3, /device:TPU:1, one launch (start us, length us, event | category | flops | bytes accessed | tf_op | source)
XLA Modules:
  0.0 221.5 jit_solution(10479800892320075875)
XLA Ops:
  1.4 2.4 %shard_map.105 = f32[16,96,128]{2,1,0:T(8,128)} custom-call(s32[2]{0:T(128)S(1)} %pad_add_fusion.refs_0_.refs_1_, s32[2,4]{1,0:T(2,128)S(1)} %bitcast.35, f32[96,96]{1,0:T(8,128)} %refs_2_.1), custom_call_target="tpu_custom_call" | custom-call | flops 3293344 | bytes 823336 | tf_op jit(solution)/shard_map/pallas_call | solution.py:110
  3.8 7.6 %all-to-all-start = ((f32[16,96,128]{2,1,0:T(8,128)}), f32[16,96,128]{2,1,0:T(8,128)S(1)}, u32[]{:S(2)}, u32[]{:S(2)}) async-start(f32[16,96,128]{2,1,0:T(8,128)} %shard_map.105), calls=%async_computation | async-start | bytes 1572864 | tf_op jit(solution)/shard_map/all_to_all | solution.py:550
  11.4 4.8 %collective-permute-start = (f32[2,12,384]{2,1,0:T(8,128)S(1)}, f32[2,12,384]{2,1,0:T(8,128)S(1)}, u32[]{:S(2)}, u32[]{:S(2)}) collective-permute-start(f32[2,12,384]{2,1,0:T(8,128)S(1)} %slice.40), channel_id=1, source_target_pairs={{0,240},{16,0},{32,16},{48,32},{64,48},{80,64},{96,80},{112,96},{1... | collective-permute-start | bytes 110600 | tf_op jit(solution)/shard_map/ppermute | solution.py:21
  18.3 2.7 %collective-permute-done.1.refs_6_ = f32[12,384]{1,0:T(8,128)S(1)} collective-permute-done((f32[12,384]{1,0:T(8,128)S(1)}, f32[12,384]{1,0:T(8,128)S(1)}, u32[]{:S(2)}, u32[]{:S(2)}) %collective-permute-start.1) | collective-permute-done | bytes 18464 | tf_op jit(solution)/shard_map/ppermute | solution.py:21
  22.3 3.9 %shard_map.104 = (f32[4,384,128]{2,1,0:T(8,128)}, f32[2,384,128]{2,1,0:T(8,128)}, f32[384,128]{1,0:T(8,128)}, f32[384,128]{1,0:T(8,128)}, f32[4,384,128]{2,1,0:T...) custom-call(s32[2,2]{1,0:T(2,128)S(1)} %bitcast.37, s32[2,4]{1,0:T(2,128)S(1)} %bitcast.36, ...), custom_call_target="tpu_custom_call" | custom-call | flops 92307648 | bytes 23076912 | tf_op jit(solution)/shard_map/pallas_call | solution.py:110
  26.3 8.2 %all-to-all-start.1 = ((f32[8,48,128]{2,1,0:T(8,128)}), f32[8,48,128]{2,1,0:T(8,128)S(1)}, u32[]{:S(2)}, u32[]{:S(2)}) async-start(f32[8,48,128]{2,1,0:T(8,128)} %get-tuple-element.55), calls=%async_computation.1 | async-start | bytes 393216 | tf_op jit(solution)/shard_map/all_to_all | solution.py:27
  35.8 7.4 %all-to-all-done.1.refs_2_ = f32[8,48,128]{2,1,0:T(8,128)S(1)} async-done(((f32[8,48,128]{2,1,0:T(8,128)}), f32[8,48,128]{2,1,0:T(8,128)S(1)}, u32[]{:S(2)}, u32[]{:S(2)}) %all-to-all-start.1) | async-done | bytes 196640 | tf_op jit(solution)/shard_map/all_to_all | solution.py:27
  43.2 3.2 %collective-permute-start.2 = (f32[8,48,128]{2,1,0:T(8,128)S(1)}, f32[8,48,128]{2,1,0:T(8,128)S(1)}, u32[]{:S(2)}, u32[]{:S(2)}) collective-permute-start(f32[8,48,128]{2,1,0:T(8,128)S(1)} %all-to-all-done.1.refs_2_), channel_id=1, source_target_pairs={{0,1},{1,0},{2,3},{3,2},{4,5},{5,4},{6,7},{7,6},{8,9},{9,8},{10,11... | collective-permute-start | bytes 589832 | tf_op jit(solution)/shard_map/ppermute | solution.py:30
  47.4 2.2 shard_map.106
  49.7 3.5 %all-to-all-start.2 = ((f32[8,96,128]{2,1,0:T(8,128)}), f32[8,96,128]{2,1,0:T(8,128)S(1)}, u32[]{:S(2)}, u32[]{:S(2)}) async-start(f32[8,96,128]{2,1,0:T(8,128)} %shard_map.106), calls=%async_computation.2 | async-start | bytes 786432 | tf_op jit(solution)/shard_map/all_to_all | solution.py:27
  53.2 4.5 %collective-permute-start.5 = (f32[2,8,16,128]{3,2,1,0:T(8,128)S(1)}, f32[2,8,16,128]{3,2,1,0:T(8,128)S(1)}, u32[]{:S(2)}, u32[]{:S(2)}) collective-permute-start(f32[2,8,16,128]{3,2,1,0:T(8,128)S(1)} %pad_maximum_fusion), channel_id=1, source_target_pairs={{0,240},{16,0},{32,16},{48,32},{64,48},{80,64},{96,80},{112,96},{1... | collective-permute-start | bytes 393224 | tf_op jit(solution)/shard_map/ppermute | solution.py:21
  57.8 4.6 %shard_map.107 = (f32[2,384,128]{2,1,0:T(8,128)}, f32[384,128]{1,0:T(8,128)}, bf16[2,1536,256]{2,1,0:T(8,128)(2,1)S(1)}, f32[8,128]{1,0:T(8,128)}) custom-call(f32[2,384,128]{2,1,0:T(8,128)} %get-tuple-element.57.refs_0_.refs_6_, f32[384,128]{1,0:T(8,128)} %get-tuple-element.60.refs_1_.refs_7_, f32[384,128]{1,0:T(8,128)} %get-tuple-element.58.refs_2_.refs_8_, ...), custom_call_target="tpu_custom_call" | custom-call | flops 95961088 | bytes 23990272 | tf_op jit(solution)/shard_map/pallas_call | solution.py:110
  62.5 6.4 %shard_map.108 = (f32[4,384,128]{2,1,0:T(8,128)S(1)}, f32[8,128]{1,0:T(8,128)}) custom-call(bf16[2,1536,256]{2,1,0:T(8,128)(2,1)S(1)} %get-tuple-element.63.refs_0_, f32[8,128]{1,0:T(8,128)} %get-tuple-element.64.refs_1_, bf16[8,384,1536]{2,1,0:T(8,128)(2,1)} %bitcast.40), custom_call_target="tpu_custom_call" | custom-call | flops 91258880 | bytes 22814720 | tf_op jit(solution)/shard_map/pallas_call | solution.py:110
  68.9 3.6 %collective-permute-start.9 = (f32[8,96,128]{2,1,0:T(8,128)S(1)}, f32[8,96,128]{2,1,0:T(8,128)S(1)}, u32[]{:S(2)}, u32[]{:S(2)}) collective-permute-start(f32[8,96,128]{2,1,0:T(8,128)S(1)} %all-to-all-done.2.refs_2_), channel_id=1, source_target_pairs={{0,1},{1,0},{2,3},{3,2},{4,5},{5,4},{6,7},{7,6},{8,9},{9,8},{10,11... | collective-permute-start | bytes 1179656 | tf_op jit(solution)/shard_map/ppermute | solution.py:30
  73.1 5.0 %collective-permute-start.7 = (f32[2,384,128]{2,1,0:T(8,128)S(1)}, f32[2,384,128]{2,1,0:T(8,128)S(1)}, u32[]{:S(2)}, u32[]{:S(2)}) collective-permute-start(f32[2,384,128]{2,1,0:T(8,128)S(1)} %copy-done.8), channel_id=1, source_target_pairs={{0,240},{16,0},{32,16},{48,32},{64,48},{80,64},{96,80},{112,96},{1... | collective-permute-start | bytes 1179656 | tf_op jit(solution)/shard_map/ppermute | solution.py:21
  78.5 2.4 %shard_map.109.refs_1_.refs_2_ = f32[256,128]{1,0:T(8,128)} custom-call(s32[16,128]{1,0:T(8,128)S(1)} %maximum_convert_fusion.1.refs_0_, s32[2]{0:T(128)S(1)} %pad_add_fusion.refs_0_.refs_1_, f32[8,96,128]{2,1,0:T(8,128)S(1)} %all-to-all-done.2.refs_2_, f32[8,96,128]{2,1,0:T(8,128)S(1)} %collective-permute-done.9.refs_3_), custom_call_target="tpu_custom_call" | custom-call | flops 3702816 | bytes 925704 | tf_op jit(solution)/shard_map/pallas_call | solution.py:110
  80.8 2.1 shard_map.110
  82.9 3.6 %all-to-all-start.3 = ((f32[16,48,128]{2,1,0:T(8,128)}), f32[16,48,128]{2,1,0:T(8,128)S(1)}, u32[]{:S(2)}, u32[]{:S(2)}) async-start(f32[16,48,128]{2,1,0:T(8,128)} %shard_map.110), calls=%async_computation.3 | async-start | bytes 786432 | tf_op jit(solution)/shard_map/all_to_all | solution.py:646
  86.8 5.2 %collective-permute-done.8.refs_2_ = f32[384,128]{1,0:T(8,128)S(1)} collective-permute-done((f32[384,128]{1,0:T(8,128)S(1)}, f32[384,128]{1,0:T(8,128)S(1)}, u32[]{:S(2)}, u32[]{:S(2)}) %collective-permute-start.8) | collective-permute-done | bytes 196640 | tf_op jit(solution)/shard_map/ppermute | solution.py:21
  92.0 4.0 %all-to-all-done.3.refs_3_ = f32[16,48,128]{2,1,0:T(8,128)S(1)} async-done(((f32[16,48,128]{2,1,0:T(8,128)}), f32[16,48,128]{2,1,0:T(8,128)S(1)}, u32[]{:S(2)}, u32[]{:S(2)}) %all-to-all-start.3) | async-done | bytes 393248 | tf_op jit(solution)/shard_map/all_to_all | solution.py:646
  96.0 3.7 %shard_map.111 = (f32[4,384,128]{2,1,0:T(8,128)}, f32[2,384,128]{2,1,0:T(8,128)}, f32[384,128]{1,0:T(8,128)}, f32[384,128]{1,0:T(8,128)}, f32[8,128]{1,0:T(8,128...) custom-call(f32[4,384,128]{2,1,0:T(8,128)S(1)} %get-tuple-element.66.refs_0_, ...), custom_call_target="tpu_custom_call" | custom-call | flops 22937600 | bytes 5734400 | tf_op jit(solution)/shard_map/pallas_call | solution.py:110
  99.8 6.9 %all-to-all-start.4 = ((f32[8,48,128]{2,1,0:T(8,128)}), f32[8,48,128]{2,1,0:T(8,128)S(1)}, u32[]{:S(2)}, u32[]{:S(2)}) async-start(f32[8,48,128]{2,1,0:T(8,128)} %get-tuple-element.86), calls=%async_computation.4 | async-start | bytes 393216 | tf_op jit(solution)/shard_map/all_to_all | solution.py:27
  106.9 3.6 %collective-permute-start.11 = (f32[384,128]{1,0:T(8,128)}, f32[384,128]{1,0:T(8,128)S(1)}, u32[]{:S(2)}, u32[]{:S(2)}) collective-permute-start(f32[384,128]{1,0:T(8,128)} %get-tuple-element.78.refs_2_.refs_8_.refs_11_), channel_id=1, source_target_pairs={{0,1},{1,2},{2,3},{3,4},{4,5},{5,6},{6,7},{7,8},{8,9},{9,10},{10,1... | collective-permute-start | bytes 589832 | tf_op jit(solution)/shard_map/ppermute | solution.py:21
  110.5 4.7 %all-to-all-done.4.refs_2_ = f32[8,48,128]{2,1,0:T(8,128)S(1)} async-done(((f32[8,48,128]{2,1,0:T(8,128)}), f32[8,48,128]{2,1,0:T(8,128)S(1)}, u32[]{:S(2)}, u32[]{:S(2)}) %all-to-all-start.4) | async-done | bytes 196640 | tf_op jit(solution)/shard_map/all_to_all | solution.py:27
  115.3 3.7 %collective-permute-start.16 = (f32[8,48,128]{2,1,0:T(8,128)S(1)}, f32[8,48,128]{2,1,0:T(8,128)S(1)}, u32[]{:S(2)}, u32[]{:S(2)}) collective-permute-start(f32[8,48,128]{2,1,0:T(8,128)S(1)} %all-to-all-done.4.refs_2_), channel_id=1, source_target_pairs={{0,1},{1,0},{2,3},{3,2},{4,5},{5,4},{6,7},{7,6},{8,9},{9,8},{10,11... | collective-permute-start | bytes 589832 | tf_op jit(solution)/shard_map/ppermute | solution.py:30
  120.4 4.6 %shard_map.112 = (f32[2,384,128]{2,1,0:T(8,128)}, f32[384,128]{1,0:T(8,128)}, bf16[2,1536,256]{2,1,0:T(8,128)(2,1)S(1)}, f32[8,128]{1,0:T(8,128)}) custom-call(f32[2,384,128]{2,1,0:T(8,128)} %get-tuple-element.76.refs_0_.refs_6_.refs_9_, f32[384,128]{1,0:T(8,128)} %get-tuple-element.77.refs_1_.refs_7_.refs_10_, ...), custom_call_target="tpu_custom_call" | custom-call | flops 95961088 | bytes 23990272 | tf_op jit(solution)/shard_map/pallas_call | solution.py:110
  125.0 3.7 %collective-permute-start.12 = (f32[2,384,128]{2,1,0:T(8,128)}, f32[2,384,128]{2,1,0:T(8,128)S(1)}, u32[]{:S(2)}, u32[]{:S(2)}) collective-permute-start(f32[2,384,128]{2,1,0:T(8,128)} %get-tuple-element.82), channel_id=1, source_target_pairs={{0,240},{16,0},{32,16},{48,32},{64,48},{80,64},{96,80},{112,96},{1... | collective-permute-start | bytes 1179656 | tf_op jit(solution)/shard_map/ppermute | solution.py:21
  128.8 2.3 %shard_map.114 = (bf16[256,768]{1,0:T(8,128)(2,1)}, bf16[256,768]{1,0:T(8,128)(2,1)}) custom-call(f32[128,256]{1,0:T(8,128)} %dynamic-slice_bitcast_fusion.refs_0_, f32[256,128]{1,0:T(8,128)S(1)} %collective-permute-done.14.refs_1_, f32[256,128]{1,0:T(8,128)} %shard_map.109.refs_1_.refs_2_, f32[256,128]{1,0:T(8,128)S(1)} %collective-permute-done.15.refs_3_), custom_call_target="tpu_custom_call" | custom-call | flops 8388608 | bytes 2097152 | tf_op jit(solution)/shard_map/pallas_call | solution.py:110
  131.1 2.5 %shard_map.115 = f32[16,48,128]{2,1,0:T(8,128)} custom-call(bf16[256,768]{1,0:T(8,128)(2,1)} %get-tuple-element.84.refs_0_, bf16[256,768]{1,0:T(8,128)(2,1)} %get-tuple-element.85.refs_1_, f32[8,48,128]{2,1,0:T(8,128)S(1)} %all-to-all-done.4.refs_2_, f32[8,48,128]{2,1,0:T(8,128)S(1)} %collective-permute-done.16.refs_3_), custom_call_target="tpu_custom_call" | custom-call | flops 9437184 | bytes 2359296 | tf_op jit(solution)/shard_map/pallas_call | solution.py:110
  133.6 3.6 %all-to-all-start.5 = ((f32[16,48,128]{2,1,0:T(8,128)}), f32[16,48,128]{2,1,0:T(8,128)S(1)}, u32[]{:S(2)}, u32[]{:S(2)}) async-start(f32[16,48,128]{2,1,0:T(8,128)} %shard_map.115), calls=%async_computation.5 | async-start | bytes 786432 | tf_op jit(solution)/shard_map/all_to_all | solution.py:657
  138.0 6.3 %shard_map.113 = (f32[4,384,128]{2,1,0:T(8,128)S(1)}, f32[8,128]{1,0:T(8,128)}) custom-call(bf16[2,1536,256]{2,1,0:T(8,128)(2,1)S(1)} %get-tuple-element.79.refs_0_, f32[8,128]{1,0:T(8,128)} %get-tuple-element.80.refs_1_, bf16[8,384,1536]{2,1,0:T(8,128)(2,1)} %bitcast.42), custom_call_target="tpu_custom_call" | custom-call | flops 91258880 | bytes 22814720 | tf_op jit(solution)/shard_map/pallas_call | solution.py:110
  144.3 2.1 all-to-all-done.5.refs_3_
  146.4 3.9 %shard_map.116 = (f32[4,384,128]{2,1,0:T(8,128)}, f32[2,384,128]{2,1,0:T(8,128)}, f32[384,128]{1,0:T(8,128)}, f32[384,128]{1,0:T(8,128)}, f32[8,128]{1,0:T(8,128...) custom-call(f32[4,384,128]{2,1,0:T(8,128)S(1)} %get-tuple-element.81.refs_0_, ...), custom_call_target="tpu_custom_call" | custom-call | flops 22953984 | bytes 5738496 | tf_op jit(solution)/shard_map/pallas_call | solution.py:110
  150.3 12.0 %all_to_all.45.refs_2_ = f32[8,48,128]{2,1,0:T(8,128)S(1)} all-to-all(f32[8,48,128]{2,1,0:T(8,128)} %get-tuple-element.96), channel_id=1, replica_groups={{0,2,4,6,8,10,12,14},{1,3,5,7,9,11,13,15},{16,18,20,22,24,26,28,30},{17..., dimensions={0} | all-to-all | bytes 393216 | tf_op jit(solution)/shard_map/all_to_all | solution.py:27
  162.4 3.7 %collective-permute-start.21 = (f32[8,48,128]{2,1,0:T(8,128)S(1)}, f32[8,48,128]{2,1,0:T(8,128)S(1)}, u32[]{:S(2)}, u32[]{:S(2)}) collective-permute-start(f32[8,48,128]{2,1,0:T(8,128)S(1)} %all_to_all.45.refs_2_), channel_id=1, source_target_pairs={{0,1},{1,0},{2,3},{3,2},{4,5},{5,4},{6,7},{7,6},{8,9},{9,8},{10,11... | collective-permute-start | bytes 589832 | tf_op jit(solution)/shard_map/ppermute | solution.py:30
  167.1 2.5 %shard_map.119 = f32[16,48,128]{2,1,0:T(8,128)} custom-call(bf16[256,768]{1,0:T(8,128)(2,1)} %get-tuple-element.84.refs_0_, bf16[256,768]{1,0:T(8,128)(2,1)} %get-tuple-element.85.refs_1_, f32[8,48,128]{2,1,0:T(8,128)S(1)} %all_to_all.45.refs_2_, f32[8,48,128]{2,1,0:T(8,128)S(1)} %collective-permute-done.21.refs_3_), custom_call_target="tpu_custom_call" | custom-call | flops 9437184 | bytes 2359296 | tf_op jit(solution)/shard_map/pallas_call | solution.py:110
  169.6 5.3 %all-to-all-start.7 = ((f32[16,48,128]{2,1,0:T(8,128)}), f32[16,48,128]{2,1,0:T(8,128)S(1)}, u32[]{:S(2)}, u32[]{:S(2)}) async-start(f32[16,48,128]{2,1,0:T(8,128)} %shard_map.119), calls=%async_computation.7 | async-start | bytes 786432 | tf_op jit(solution)/shard_map/all_to_all | solution.py:657
  175.7 2.6 %collective-permute-done.18.refs_4_ = f32[384,128]{1,0:T(8,128)S(1)} collective-permute-done((f32[384,128]{1,0:T(8,128)S(1)}, f32[384,128]{1,0:T(8,128)S(1)}, u32[]{:S(2)}, u32[]{:S(2)}) %collective-permute-start.18) | collective-permute-done | bytes 196640 | tf_op jit(solution)/shard_map/ppermute | solution.py:21
  178.3 2.0 collective-permute-done.17.refs_3_
  180.3 4.6 %shard_map.117 = (f32[2,384,128]{2,1,0:T(8,128)}, f32[384,128]{1,0:T(8,128)}, bf16[2,1536,256]{2,1,0:T(8,128)(2,1)S(1)}, f32[8,128]{1,0:T(8,128)}) custom-call(f32[2,384,128]{2,1,0:T(8,128)} %get-tuple-element.88.refs_0_.refs_12_, f32[384,128]{1,0:T(8,128)} %get-tuple-element.89.refs_1_.refs_13_, f32[384,128]{1,0:T(8,128)} %get-tuple-element.90.refs_2_.refs_14_, ...), custom_call_target="tpu_custom_call" | custom-call | flops 95961088 | bytes 23990272 | tf_op jit(solution)/shard_map/pallas_call | solution.py:110
  185.0 3.0 %collective-permute-start.19 = (f32[2,384,128]{2,1,0:T(8,128)}, f32[2,384,128]{2,1,0:T(8,128)S(1)}, u32[]{:S(2)}, u32[]{:S(2)}) collective-permute-start(f32[2,384,128]{2,1,0:T(8,128)} %get-tuple-element.94), channel_id=1, source_target_pairs={{0,240},{16,0},{32,16},{48,32},{64,48},{80,64},{96,80},{112,96},{1... | collective-permute-start | bytes 1179656 | tf_op jit(solution)/shard_map/ppermute | solution.py:21
  188.0 6.3 %shard_map.118 = (f32[4,384,128]{2,1,0:T(8,128)S(1)}, f32[8,128]{1,0:T(8,128)}) custom-call(bf16[2,1536,256]{2,1,0:T(8,128)(2,1)S(1)} %get-tuple-element.91.refs_0_, f32[8,128]{1,0:T(8,128)} %get-tuple-element.92.refs_1_, bf16[8,384,1536]{2,1,0:T(8,128)(2,1)} %bitcast.44), custom_call_target="tpu_custom_call" | custom-call | flops 91258880 | bytes 22814720 | tf_op jit(solution)/shard_map/pallas_call | solution.py:110
  195.8 8.8 %all-to-all-start.8 = ((f32[256,1,128]{2,1,0:T(1,128)}), f32[256,1,128]{2,1,0:T(1,128)S(1)}, u32[]{:S(2)}, u32[]{:S(2)}) async-start(f32[256,1,128]{2,1,0:T(1,128)} %bitcast.46), calls=%async_computation.8 | async-start | bytes 262144 | tf_op jit(solution)/shard_map/all_to_all | solution.py:673
  204.6 2.3 %collective-permute-start.20 = (f32[384,128]{1,0:T(8,128)S(1)}, f32[384,128]{1,0:T(8,128)S(1)}, u32[]{:S(2)}, u32[]{:S(2)}) collective-permute-start(f32[384,128]{1,0:T(8,128)S(1)} %copy-done.11), channel_id=1, source_target_pairs={{0,15},{1,0},{2,1},{3,2},{4,3},{5,4},{6,5},{7,6},{8,7},{9,8},{10,9... | collective-permute-start | bytes 589832 | tf_op jit(solution)/shard_map/ppermute | solution.py:21
  206.9 4.4 %collective-permute-done.20.refs_2_ = f32[384,128]{1,0:T(8,128)S(1)} collective-permute-done((f32[384,128]{1,0:T(8,128)S(1)}, f32[384,128]{1,0:T(8,128)S(1)}, u32[]{:S(2)}, u32[]{:S(2)}) %collective-permute-start.20) | collective-permute-done | bytes 196640 | tf_op jit(solution)/shard_map/ppermute | solution.py:21
  211.3 2.6 %shard_map.120 = (f32[4,384,128]{2,1,0:T(8,128)}, f32[8,128]{1,0:T(8,128)}) custom-call(f32[4,384,128]{2,1,0:T(8,128)S(1)} %get-tuple-element.93.refs_0_, f32[2,384,128]{2,1,0:T(8,128)S(1)} %collective-permute-done.19.refs_1_, f32[384,128]{1,0:T(8,128)S(1)} %collective-permute-done.20.refs_2_, f32[16,48,128]{2,1,0:T(8,128)S(1)} %all-to-all-done.7.refs_3_.refs_2_, ...), custom_call_target="tpu_custom_call" | custom-call | flops 15745024 | bytes 3936256 | tf_op jit(solution)/shard_map/pallas_call | solution.py:110
  213.9 3.7 %all-to-all-done.8 = f32[256,1,128]{2,1,0:T(1,128)S(1)} async-done(((f32[256,1,128]{2,1,0:T(1,128)}), f32[256,1,128]{2,1,0:T(1,128)S(1)}, u32[]{:S(2)}, u32[]{:S(2)}) %all-to-all-start.8) | async-done | bytes 131104 | tf_op jit(solution)/shard_map/all_to_all | solution.py:673
  217.6 3.8 %shard_map.122 = (f32[4,384,128]{2,1,0:T(8,128)}, f32[4,384,128]{2,1,0:T(8,128)}) custom-call(f32[8,128]{1,0:T(8,128)} %get-tuple-element.74.refs_9_.refs_0_, f32[8,128]{1,0:T(8,128)} %get-tuple-element.75.refs_1_, f32[8,128]{1,0:T(8,128)} %get-tuple-element.87.refs_2_, f32[8,128]{1,0:T(8,128)} %get-tuple-element.97.refs_3_, f32[256,128]{1,0:T(8,128)S(1)} %bitcast.34, ...), custom_call_target="tpu_custom_call" | custom-call | flops 28901376 | bytes 7225344 | tf_op jit(solution)/shard_map/pallas_call | solution.py:110
  (73 shorter events, 13.9 us)
Async XLA Ops:
  0.6 21.7 %copy-start.1 = (s32[1,2,4]{2,1,0:T(2,128)S(1)}, s32[1,2,4]{2,1,0:T(2,128)}, u32[]{:S(2)}) copy-start(s32[1,2,4]{2,1,0:T(2,128)} %param.12) | copy-start | bytes 100
  0.6 17.1 %copy-start.7 = (f32[1,2,2,384]{3,2,1,0:T(2,128)S(1)}, f32[1,2,2,384]{3,2,1,0:T(2,128)}, u32[]{:S(2)}) copy-start(f32[1,2,2,384]{3,2,1,0:T(2,128)} %param.10) | copy-start | bytes 18436
  0.7 21.7 %copy-start.2 = (s32[1,2,2]{2,1,0:T(2,128)S(1)}, s32[1,2,2]{2,1,0:T(2,128)}, u32[]{:S(2)}) copy-start(s32[1,2,2]{2,1,0:T(2,128)} %param.11) | copy-start | bytes 52
  0.7 0.7 copy-start
  1.4 10.0 %copy-start.5 = (bf16[1,2,12,1536]{3,1,2,0:T(2,128)(2,1)S(1)}, bf16[1,2,12,1536]{3,1,2,0:T(2,128)(2,1)}, u32[]{:S(2)}) copy-start(bf16[1,2,12,1536]{3,1,2,0:T(2,128)(2,1)} %param.14) | copy-start | bytes 221188
  3.8 22.5 %all-to-all-start = ((f32[16,96,128]{2,1,0:T(8,128)}), f32[16,96,128]{2,1,0:T(8,128)S(1)}, u32[]{:S(2)}, u32[]{:S(2)}) async-start(f32[16,96,128]{2,1,0:T(8,128)} %shard_map.105), calls=%async_computation | async-start | bytes 1572864 | tf_op jit(solution)/shard_map/all_to_all | solution.py:550
  11.4 10.9 %collective-permute-start = (f32[2,12,384]{2,1,0:T(8,128)S(1)}, f32[2,12,384]{2,1,0:T(8,128)S(1)}, u32[]{:S(2)}, u32[]{:S(2)}) collective-permute-start(f32[2,12,384]{2,1,0:T(8,128)S(1)} %slice.40), channel_id=1, source_target_pairs={{0,240},{16,0},{32,16},{48,32},{64,48},{80,64},{96,80},{112,96},{1... | collective-permute-start | bytes 110600 | tf_op jit(solution)/shard_map/ppermute | solution.py:21
  16.2 4.8 %collective-permute-start.1 = (f32[12,384]{1,0:T(8,128)S(1)}, f32[12,384]{1,0:T(8,128)S(1)}, u32[]{:S(2)}, u32[]{:S(2)}) collective-permute-start(f32[12,384]{1,0:T(8,128)S(1)} %slice_bitcast_fusion.4), channel_id=1, source_target_pairs={{0,15},{1,0},{2,1},{3,2},{4,3},{5,4},{6,5},{7,6},{8,7},{9,8},{10,9... | collective-permute-start | bytes 55304 | tf_op jit(solution)/shard_map/ppermute | solution.py:21
  26.3 16.9 %all-to-all-start.1 = ((f32[8,48,128]{2,1,0:T(8,128)}), f32[8,48,128]{2,1,0:T(8,128)S(1)}, u32[]{:S(2)}, u32[]{:S(2)}) async-start(f32[8,48,128]{2,1,0:T(8,128)} %get-tuple-element.55), calls=%async_computation.1 | async-start | bytes 393216 | tf_op jit(solution)/shard_map/all_to_all | solution.py:27
  34.5 15.2 %collective-permute-start.3 = (f32[2,384,128]{2,1,0:T(8,128)}, f32[2,384,128]{2,1,0:T(8,128)S(1)}, u32[]{:S(2)}, u32[]{:S(2)}) collective-permute-start(f32[2,384,128]{2,1,0:T(8,128)} %get-tuple-element.57.refs_0_.refs_6_), channel_id=1, source_target_pairs={{0,16},{16,32},{32,48},{48,64},{64,80},{80,96},{96,112},{112,128},... | collective-permute-start | bytes 1179656 | tf_op jit(solution)/shard_map/ppermute | solution.py:21
  43.2 4.3 %collective-permute-start.2 = (f32[8,48,128]{2,1,0:T(8,128)S(1)}, f32[8,48,128]{2,1,0:T(8,128)S(1)}, u32[]{:S(2)}, u32[]{:S(2)}) collective-permute-start(f32[8,48,128]{2,1,0:T(8,128)S(1)} %all-to-all-done.1.refs_2_), channel_id=1, source_target_pairs={{0,1},{1,0},{2,3},{3,2},{4,5},{5,4},{6,7},{7,6},{8,9},{9,8},{10,11... | collective-permute-start | bytes 589832 | tf_op jit(solution)/shard_map/ppermute | solution.py:30
  46.4 3.3 %collective-permute-start.4 = (f32[384,128]{1,0:T(8,128)}, f32[384,128]{1,0:T(8,128)S(1)}, u32[]{:S(2)}, u32[]{:S(2)}) collective-permute-start(f32[384,128]{1,0:T(8,128)} %get-tuple-element.58.refs_2_.refs_8_), channel_id=1, source_target_pairs={{0,1},{1,2},{2,3},{3,4},{4,5},{5,6},{6,7},{7,8},{8,9},{9,10},{10,1... | collective-permute-start | bytes 589832 | tf_op jit(solution)/shard_map/ppermute | solution.py:21
  49.7 19.2 %all-to-all-start.2 = ((f32[8,96,128]{2,1,0:T(8,128)}), f32[8,96,128]{2,1,0:T(8,128)S(1)}, u32[]{:S(2)}, u32[]{:S(2)}) async-start(f32[8,96,128]{2,1,0:T(8,128)} %shard_map.106), calls=%async_computation.2 | async-start | bytes 786432 | tf_op jit(solution)/shard_map/all_to_all | solution.py:27
  53.2 15.7 %collective-permute-start.5 = (f32[2,8,16,128]{3,2,1,0:T(8,128)S(1)}, f32[2,8,16,128]{3,2,1,0:T(8,128)S(1)}, u32[]{:S(2)}, u32[]{:S(2)}) collective-permute-start(f32[2,8,16,128]{3,2,1,0:T(8,128)S(1)} %pad_maximum_fusion), channel_id=1, source_target_pairs={{0,240},{16,0},{32,16},{48,32},{64,48},{80,64},{96,80},{112,96},{1... | collective-permute-start | bytes 393224 | tf_op jit(solution)/shard_map/ppermute | solution.py:21
  57.7 11.1 %collective-permute-start.6 = (f32[2,8,16,128]{3,2,1,0:T(8,128)S(1)}, f32[2,8,16,128]{3,2,1,0:T(8,128)S(1)}, u32[]{:S(2)}, u32[]{:S(2)}) collective-permute-start(f32[2,8,16,128]{3,2,1,0:T(8,128)S(1)} %pad_maximum_fusion.1), channel_id=1, source_target_pairs={{0,16},{16,32},{32,48},{48,64},{64,80},{80,96},{96,112},{112,128},... | collective-permute-start | bytes 393224 | tf_op jit(solution)/shard_map/ppermute | solution.py:21
  62.5 10.0 %copy-start.6 = (f32[2,128,256]{2,1,0:T(8,128)S(1)}, f32[2,128,256]{2,1,0:T(8,128)}, u32[]{:S(2)}) copy-start(f32[2,128,256]{2,1,0:T(8,128)} %constant.29.clone) | copy-start | bytes 786436
  62.5 10.6 %copy-start.8 = (f32[2,384,128]{2,1,0:T(8,128)S(1)}, f32[2,384,128]{2,1,0:T(8,128)}, u32[]{:S(2)}) copy-start(f32[2,384,128]{2,1,0:T(8,128)} %get-tuple-element.67) | copy-start | bytes 1179652
  68.9 9.5 %collective-permute-start.9 = (f32[8,96,128]{2,1,0:T(8,128)S(1)}, f32[8,96,128]{2,1,0:T(8,128)S(1)}, u32[]{:S(2)}, u32[]{:S(2)}) collective-permute-start(f32[8,96,128]{2,1,0:T(8,128)S(1)} %all-to-all-done.2.refs_2_), channel_id=1, source_target_pairs={{0,1},{1,0},{2,3},{3,2},{4,5},{5,4},{6,7},{7,6},{8,9},{9,8},{10,11... | collective-permute-start | bytes 1179656 | tf_op jit(solution)/shard_map/ppermute | solution.py:30
  73.1 18.9 %collective-permute-start.7 = (f32[2,384,128]{2,1,0:T(8,128)S(1)}, f32[2,384,128]{2,1,0:T(8,128)S(1)}, u32[]{:S(2)}, u32[]{:S(2)}) collective-permute-start(f32[2,384,128]{2,1,0:T(8,128)S(1)} %copy-done.8), channel_id=1, source_target_pairs={{0,240},{16,0},{32,16},{48,32},{64,48},{80,64},{96,80},{112,96},{1... | collective-permute-start | bytes 1179656 | tf_op jit(solution)/shard_map/ppermute | solution.py:21
  78.4 8.1 %copy-start.9 = (f32[384,128]{1,0:T(8,128)S(1)}, f32[384,128]{1,0:T(8,128)}, u32[]{:S(2)}) copy-start(f32[384,128]{1,0:T(8,128)} %get-tuple-element.68) | copy-start | bytes 589828
  82.9 13.1 %all-to-all-start.3 = ((f32[16,48,128]{2,1,0:T(8,128)}), f32[16,48,128]{2,1,0:T(8,128)S(1)}, u32[]{:S(2)}, u32[]{:S(2)}) async-start(f32[16,48,128]{2,1,0:T(8,128)} %shard_map.110), calls=%async_computation.3 | async-start | bytes 786432 | tf_op jit(solution)/shard_map/all_to_all | solution.py:646
  86.5 5.5 %collective-permute-start.8 = (f32[384,128]{1,0:T(8,128)S(1)}, f32[384,128]{1,0:T(8,128)S(1)}, u32[]{:S(2)}, u32[]{:S(2)}) collective-permute-start(f32[384,128]{1,0:T(8,128)S(1)} %copy-done.9), channel_id=1, source_target_pairs={{0,15},{1,0},{2,1},{3,2},{4,3},{5,4},{6,5},{7,6},{8,7},{9,8},{10,9... | collective-permute-start | bytes 589832 | tf_op jit(solution)/shard_map/ppermute | solution.py:21
  96.0 22.9 %copy-start.3 = (f32[256,128]{1,0:T(8,128)S(1)}, f32[256,128]{1,0:T(8,128)}, u32[]{:S(2)}) copy-start(f32[256,128]{1,0:T(8,128)} %shard_map.109.refs_1_.refs_2_) | copy-start | bytes 393220
  99.8 15.5 %all-to-all-start.4 = ((f32[8,48,128]{2,1,0:T(8,128)}), f32[8,48,128]{2,1,0:T(8,128)S(1)}, u32[]{:S(2)}, u32[]{:S(2)}) async-start(f32[8,48,128]{2,1,0:T(8,128)} %get-tuple-element.86), calls=%async_computation.4 | async-start | bytes 393216 | tf_op jit(solution)/shard_map/all_to_all | solution.py:27
  106.6 13.8 %collective-permute-start.10 = (f32[2,384,128]{2,1,0:T(8,128)}, f32[2,384,128]{2,1,0:T(8,128)S(1)}, u32[]{:S(2)}, u32[]{:S(2)}) collective-permute-start(f32[2,384,128]{2,1,0:T(8,128)} %get-tuple-element.76.refs_0_.refs_6_.refs_9_), channel_id=1, source_target_pairs={{0,16},{16,32},{32,48},{48,64},{64,80},{80,96},{96,112},{112,128},... | collective-permute-start | bytes 1179656 | tf_op jit(solution)/shard_map/ppermute | solution.py:21
  106.9 13.5 %collective-permute-start.11 = (f32[384,128]{1,0:T(8,128)}, f32[384,128]{1,0:T(8,128)S(1)}, u32[]{:S(2)}, u32[]{:S(2)}) collective-permute-start(f32[384,128]{1,0:T(8,128)} %get-tuple-element.78.refs_2_.refs_8_.refs_11_), channel_id=1, source_target_pairs={{0,1},{1,2},{2,3},{3,4},{4,5},{5,6},{6,7},{7,8},{8,9},{9,10},{10,1... | collective-permute-start | bytes 589832 | tf_op jit(solution)/shard_map/ppermute | solution.py:21
  115.3 15.8 %collective-permute-start.16 = (f32[8,48,128]{2,1,0:T(8,128)S(1)}, f32[8,48,128]{2,1,0:T(8,128)S(1)}, u32[]{:S(2)}, u32[]{:S(2)}) collective-permute-start(f32[8,48,128]{2,1,0:T(8,128)S(1)} %all-to-all-done.4.refs_2_), channel_id=1, source_target_pairs={{0,1},{1,0},{2,3},{3,2},{4,5},{5,4},{6,7},{7,6},{8,9},{9,8},{10,11... | collective-permute-start | bytes 589832 | tf_op jit(solution)/shard_map/ppermute | solution.py:30
  118.9 9.8 %collective-permute-start.15 = (f32[256,128]{1,0:T(8,128)S(1)}, f32[256,128]{1,0:T(8,128)S(1)}, u32[]{:S(2)}, u32[]{:S(2)}) collective-permute-start(f32[256,128]{1,0:T(8,128)S(1)} %copy-done.3), channel_id=1, source_target_pairs={{0,240},{16,0},{32,16},{48,32},{64,48},{80,64},{96,80},{112,96},{1... | collective-permute-start | bytes 393224 | tf_op jit(solution)/shard_map/ppermute | solution.py:21
  119.2 9.5 %collective-permute-start.14 = (f32[256,128]{1,0:T(8,128)S(1)}, f32[256,128]{1,0:T(8,128)S(1)}, u32[]{:S(2)}, u32[]{:S(2)}) collective-permute-start(f32[256,128]{1,0:T(8,128)S(1)} %copy-done.3), channel_id=1, source_target_pairs={{0,16},{16,32},{32,48},{48,64},{64,80},{80,96},{96,112},{112,128},... | collective-permute-start | bytes 393224 | tf_op jit(solution)/shard_map/ppermute | solution.py:21
  125.0 12.1 %copy-start.10 = (f32[384,128]{1,0:T(8,128)S(1)}, f32[384,128]{1,0:T(8,128)}, u32[]{:S(2)}) copy-start(f32[384,128]{1,0:T(8,128)} %get-tuple-element.83) | copy-start | bytes 589828
  125.0 19.3 %collective-permute-start.12 = (f32[2,384,128]{2,1,0:T(8,128)}, f32[2,384,128]{2,1,0:T(8,128)S(1)}, u32[]{:S(2)}, u32[]{:S(2)}) collective-permute-start(f32[2,384,128]{2,1,0:T(8,128)} %get-tuple-element.82), channel_id=1, source_target_pairs={{0,240},{16,0},{32,16},{48,32},{64,48},{80,64},{96,80},{112,96},{1... | collective-permute-start | bytes 1179656 | tf_op jit(solution)/shard_map/ppermute | solution.py:21
  133.6 12.8 %all-to-all-start.5 = ((f32[16,48,128]{2,1,0:T(8,128)}), f32[16,48,128]{2,1,0:T(8,128)S(1)}, u32[]{:S(2)}, u32[]{:S(2)}) async-start(f32[16,48,128]{2,1,0:T(8,128)} %shard_map.115), calls=%async_computation.5 | async-start | bytes 786432 | tf_op jit(solution)/shard_map/all_to_all | solution.py:657
  137.2 7.2 %collective-permute-start.13 = (f32[384,128]{1,0:T(8,128)S(1)}, f32[384,128]{1,0:T(8,128)S(1)}, u32[]{:S(2)}, u32[]{:S(2)}) collective-permute-start(f32[384,128]{1,0:T(8,128)S(1)} %copy-done.10), channel_id=1, source_target_pairs={{0,15},{1,0},{2,1},{3,2},{4,3},{5,4},{6,5},{7,6},{8,7},{9,8},{10,9... | collective-permute-start | bytes 589832 | tf_op jit(solution)/shard_map/ppermute | solution.py:21
  150.3 24.6 %copy-start.4 = (f32[384,128]{1,0:T(8,128)S(1)}, f32[384,128]{1,0:T(8,128)}, u32[]{:S(2)}) copy-start(f32[384,128]{1,0:T(8,128)} %get-tuple-element.90.refs_2_.refs_14_) | copy-start | bytes 589828
  162.4 4.8 %collective-permute-start.21 = (f32[8,48,128]{2,1,0:T(8,128)S(1)}, f32[8,48,128]{2,1,0:T(8,128)S(1)}, u32[]{:S(2)}, u32[]{:S(2)}) collective-permute-start(f32[8,48,128]{2,1,0:T(8,128)S(1)} %all_to_all.45.refs_2_), channel_id=1, source_target_pairs={{0,1},{1,0},{2,3},{3,2},{4,5},{5,4},{6,7},{7,6},{8,9},{9,8},{10,11... | collective-permute-start | bytes 589832 | tf_op jit(solution)/shard_map/ppermute | solution.py:30
  166.1 14.3 %collective-permute-start.17 = (f32[2,384,128]{2,1,0:T(8,128)}, f32[2,384,128]{2,1,0:T(8,128)S(1)}, u32[]{:S(2)}, u32[]{:S(2)}) collective-permute-start(f32[2,384,128]{2,1,0:T(8,128)} %get-tuple-element.88.refs_0_.refs_12_), channel_id=1, source_target_pairs={{0,16},{16,32},{32,48},{48,64},{64,80},{80,96},{96,112},{112,128},... | collective-permute-start | bytes 1179656 | tf_op jit(solution)/shard_map/ppermute | solution.py:21
  169.6 24.7 %all-to-all-start.7 = ((f32[16,48,128]{2,1,0:T(8,128)}), f32[16,48,128]{2,1,0:T(8,128)S(1)}, u32[]{:S(2)}, u32[]{:S(2)}) async-start(f32[16,48,128]{2,1,0:T(8,128)} %shard_map.119), calls=%async_computation.7 | async-start | bytes 786432 | tf_op jit(solution)/shard_map/all_to_all | solution.py:657
  174.9 3.4 %collective-permute-start.18 = (f32[384,128]{1,0:T(8,128)S(1)}, f32[384,128]{1,0:T(8,128)S(1)}, u32[]{:S(2)}, u32[]{:S(2)}) collective-permute-start(f32[384,128]{1,0:T(8,128)S(1)} %copy-done.4), channel_id=1, source_target_pairs={{0,1},{1,2},{2,3},{3,4},{4,5},{5,6},{6,7},{7,8},{8,9},{9,10},{10,1... | collective-permute-start | bytes 589832 | tf_op jit(solution)/shard_map/ppermute | solution.py:21
  185.0 26.4 %collective-permute-start.19 = (f32[2,384,128]{2,1,0:T(8,128)}, f32[2,384,128]{2,1,0:T(8,128)S(1)}, u32[]{:S(2)}, u32[]{:S(2)}) collective-permute-start(f32[2,384,128]{2,1,0:T(8,128)} %get-tuple-element.94), channel_id=1, source_target_pairs={{0,240},{16,0},{32,16},{48,32},{64,48},{80,64},{96,80},{112,96},{1... | collective-permute-start | bytes 1179656 | tf_op jit(solution)/shard_map/ppermute | solution.py:21
  188.0 16.6 %copy-start.11 = (f32[384,128]{1,0:T(8,128)S(1)}, f32[384,128]{1,0:T(8,128)}, u32[]{:S(2)}) copy-start(f32[384,128]{1,0:T(8,128)} %get-tuple-element.95) | copy-start | bytes 589828
  195.8 21.8 %all-to-all-start.8 = ((f32[256,1,128]{2,1,0:T(1,128)}), f32[256,1,128]{2,1,0:T(1,128)S(1)}, u32[]{:S(2)}, u32[]{:S(2)}) async-start(f32[256,1,128]{2,1,0:T(1,128)} %bitcast.46), calls=%async_computation.8 | async-start | bytes 262144 | tf_op jit(solution)/shard_map/all_to_all | solution.py:673
  204.6 6.7 %collective-permute-start.20 = (f32[384,128]{1,0:T(8,128)S(1)}, f32[384,128]{1,0:T(8,128)S(1)}, u32[]{:S(2)}, u32[]{:S(2)}) collective-permute-start(f32[384,128]{1,0:T(8,128)S(1)} %copy-done.11), channel_id=1, source_target_pairs={{0,15},{1,0},{2,1},{3,2},{4,3},{5,4},{6,5},{7,6},{8,7},{9,8},{10,9... | collective-permute-start | bytes 589832 | tf_op jit(solution)/shard_map/ppermute | solution.py:21

commit v4 on v3

--- a/solution.py
+++ b/solution.py
@@ -271,7 +271,8 @@
 GIVEN = (1, 5, 3)
 
 
-def give_body(own_east, own_north0, own_north1, west, below, blocks, out_east, out_north, parts, product, held, arrived):
+def give_body(weigh, own_east, own_north0, own_north1, west, below, blocks, out_east, out_north, parts, *refs):
+    *product, held, arrived = refs
     copies = fetch(blocks, held, arrived, GIVEN)
     side = west.shape[1]
     for s in range(2):
@@ -292,19 +293,27 @@
             out_north[...] = value
         if n == 1:
             out_east.send()
-        total = total + weighed(parts, s, q, value)
-    product[...] = jnp.broadcast_to(total, product.shape)
-
-
-def keep_body(parts, product_in, blocks, out, product, held, arrived):
+        if weigh:
+            total = total + weighed(parts, s, q, value)
+    if weigh:
+        product[0][...] = jnp.broadcast_to(total, product[0].shape)
+
+
+def keep_body(weigh, parts, *refs):
+    if weigh:
+        product_in, blocks, out, product, held, arrived = refs
+    else:
+        blocks, out, held, arrived = refs
     copies = fetch(blocks, held, arrived, (0, 2, 7, 4, 6))
-    total = product_in[0:1]
+    total = 0.0
     for n, (edge, s, q) in enumerate([(0, 0, 0), (1, 0, 2), (1, 1, 3), (2, 1, 0), (3, 1, 2)]):
         copies[n].wait()
         value = apply_rows(held[n], parts[s])
-        total = total + weighed(parts, s, q, value)
+        if weigh:
+            total = total + weighed(parts, s, q, value)
         out[edge] = out[edge] - value if n == 2 else value
-    product[...] = jnp.broadcast_to(total, product.shape)
+    if weigh:
+        product[...] = jnp.broadcast_to(product_in[0:1] + total, product.shape)
 
 
 def sum_body(product, rows, got, out):
@@ -314,17 +323,6 @@
     index = lax.broadcasted_iota(jnp.int32, total.shape, 0) % NEAR
     value = product[0:1] + column_sum(jnp.where(index < 4 * CS, rows[...] * total, 0.0))
     out[...] = jnp.broadcast_to(value, out.shape)
-
-
-def arrange_body(lanes, below, own, beyond, *outs):
-    lane = lanes[...].astype(BF16)
-    width = lane.shape[1]
-    for ii, source in enumerate([below, own, beyond]):
-        high, low = split(source[...])
-        high = multiply(high, lane).astype(BF16)
-        low = multiply(low, lane).astype(BF16)
-        outs[0][:, ii * width : (ii + 1) * width] = high
-        outs[1][:, ii * width : (ii + 1) * width] = low
 
 
 def row_pieces(same, other, ii):
@@ -347,21 +345,25 @@
             out[target, ii * NEAR + 8 : ii * NEAR + 16] = rest
 
 
-def coarse_body(high, low, same, other, out):
+def laid(source, lane):
+    return tuple(multiply(part, lane).astype(BF16) for part in split(source[...]))
+
+
+def coarse_body(lanes, below, own, beyond, same, other, out):
     cases = same.shape[2]
-    pieces = [row_pieces(same, other, ii) for ii in range(3)]
-    gathered = halves(jnp.concatenate(pieces[0] + pieces[1] + pieces[2], 0))
-    product = multiply(high[...], gathered)
-    value = product[:, :cases] + product[:, cases:] + multiply(low[...], gathered[:, :cases])
-    lay_out(value, pieces[0], out)
+    lane = lanes[...].astype(BF16)
+    value = 0.0
+    for ii, source in enumerate((own, below, beyond)):
+        gathered = halves(jnp.concatenate(row_pieces(same, other, (1, 0, 2)[ii]), 0))
+        high, low = laid(source, lane)
+        product = multiply(high, gathered)
+        value = value + product[:, :cases] + product[:, cases:] + multiply(low, gathered[:, :cases])
+    lay_out(value, row_pieces(same, other, 0), out)
 
 
 def first_coarse_body(lanes, own, same, other, lower, upper, out):
     cases = same.shape[2]
-    lane = lanes[...].astype(BF16)
-    high, low = split(own[...])
-    high = multiply(high, lane).astype(BF16)
-    low = multiply(low, lane).astype(BF16)
+    high, low = laid(own, lanes[...].astype(BF16))
     middle = row_pieces(same, other, 1)
     half = same.shape[0]
     pieces = [
@@ -591,21 +593,27 @@
     def held(count):
         return (pltpu.VMEM((count,) + blocks.shape[1:], BF16), pltpu.SemaphoreType.DMA((count,)))
 
-    def give(own, west, below):
-        given_east, given_north, parts, product = kernel_call(
-            give_body,
-            (shape(2, side), shape(side), double(2, 4 * side), shape(8)),
+    def give(own, west, below, weigh=False):
+        given_east, given_north, *given = kernel_call(
+            functools.partial(give_body, weigh),
+            (shape(2, side), shape(side), double(2, 4 * side)) + ((shape(8),) if weigh else ()),
             (*own, west, below),
             raw=(blocks,),
             scratch=held(3),
             fast=(3, 4),
-            fast_outs=(2,),
+            fast_outs=(2, 3),
         )
-        return (parts, product), shifted(given_east, "sx", -1), shifted(given_north, "sy", -1)
-
-    def keep(given):
+        return given, shifted(given_east, "sx", -1), shifted(given_north, "sy", -1)
+
+    def keep(given, weigh=False):
         return kernel_call(
-            keep_body, (field, shape(8)), given, raw=(blocks,), scratch=held(5), fast=(0,), fast_outs=(0,)
+            functools.partial(keep_body, weigh),
+            (field, shape(8)) if weigh else (field,),
+            given,
+            raw=(blocks,),
+            scratch=held(5),
+            fast=range(len(given)),
+            fast_outs=(0, 1),
         )
 
     west, below = halo(w0)
@@ -623,7 +631,7 @@
     )
     turned, west, below = lax.optimization_barrier((turned, west, below))
     given, back_east, back_north = give(w0, west, below)
-    kept, _ = keep(given)
+    (kept,) = keep(given)
     rows_same, rows_other, (kept, lower, upper) = along_sy(turned, (kept, lower, upper))
     numbers = jnp.concatenate([rows_same[:, 0], rows_other[:, 0]], 0).astype(jnp.int32)
     own_part = kernel_call(
@@ -647,29 +655,25 @@
     u1, *w1, kappa, spare0, _, message = image_call(
         kept, back_east, back_north, got, edges, gain, w0, None, half
     )
-    w_shape = jax.ShapeDtypeStruct((gx * NEAR, ROWS * gy), BF16)
-    high, low = kernel_call(
-        arrange_body, (w_shape, w_shape), (lanes, below_part, own_part, beyond_part), fast=(1, 3)
-    )
-
     def coarse_solve(same, other):
-        send = kernel_call(coarse_body, shape(gx, ROWS), (high, low, same, other), fast=(2, 3))
+        send = kernel_call(coarse_body, shape(gx, ROWS), (lanes, below_part, own_part, beyond_part, same, other), fast=(4, 5))
         return lax.all_to_all(send, "sx", 0, 0, tiled=True)
 
     west, below = halo(w1)
     same, other = along_sy(message)
     given, back_east, back_north = give(w1, west, below)
     got = coarse_solve(same, other)
-    kept, _ = keep(given)
+    (kept,) = keep(given)
     u2, *w2, _, spare1, rows, message = image_call(
         kept, back_east, back_north, got, edges, gain, w1, kappa, half
     )
     west, below = halo(w2)
     same, other = along_sy(message)
-    given, back_east, back_north = give(w2, west, below)
+    given, back_east, back_north = give(w2, west, below, True)
+    same, given = lax.optimization_barrier((same, given))
     got = coarse_solve(same, other)
-    kept, product = keep(given)
-    last = kernel_call(sum_body, shape(gx * gy), (product, rows, got), fast=(2,))
+    kept, product = keep(given, True)
+    last = kernel_call(sum_body, shape(gx * gy), (product, rows, got), fast=(0, 2))
     last = lax.all_to_all(last.reshape(gx * gy, 1, cases), ("sx", "sy"), 0, 0, tiled=True)
     u3, spare2 = kernel_call(
         functools.partial(image_body, True),

time: 223 us -> 214 us (0.960)
  blocking collectives: 12 us -> 0 us
  starting transfers between devices: 95.5 us -> 104 us
  Pallas kernels: 68.4 us -> 62.5 us
    all_to_all x1 -> x0, blocking collectives: 12 us -> none  [along_sy(): lax.all_to_all(copies, 'sy', 0, 0, tiled=True, axis_index_groups=groups)]
    pallas_call x19 -> x18, Pallas kernels: 68.4 us -> 62.5 us  [kernel_call(): pl.pallas_call(wrapped, in_specs=[spec(k) for k in range(len(arrays))], o...]
    ppermute x18, waiting for transfers between devices: 18.2 us -> 13.5 us  [shifted(): lax.ppermute(array, axis, [(i, (i + by) % count) for i in range(count)])]
    all_to_all x3 -> x4, waiting for transfers between devices: 12.1 us -> 16.2 us  [along_sy(): lax.all_to_all(copies, 'sy', 0, 0, tiled=True, axis_index_groups=groups)]
    all_to_all x1, starting transfers between devices: 8.77 us -> 12.3 us  [local(): lax.all_to_all(last.reshape(gx * gy, 1, cases), ('sx', 'sy'), 0, 0, tiled...]
    all_to_all x3 -> x4, starting transfers between devices: 18.5 us -> 21.3 us  [along_sy(): lax.all_to_all(copies, 'sy', 0, 0, tiled=True, axis_index_groups=groups)]
  transfers between devices with their start and end apart: 30 -> 31, of which waited for: 13 -> 11; matrix products, arithmetic and copies ran while one was open for 1% -> 1% of each run, Pallas kernels for 25% -> 22%
where the time goes in v4:
time: 214 us; the launch traced here: 212 us
  starting transfers between devices  104 us (49%)
  Pallas kernels  62.5 us (29%)
  waiting for transfers between devices  41 us (19%)
  local copies, waits for them, and re-layouts  2.95 us (1%)
    pallas_call x18, Pallas kernels, kernel_call(): pl.pallas_call(wrapped, in_specs=[spec(k) for k in range(len(arrays))], o...  62.5 us
    ppermute x18, starting transfers between devices, shifted(): lax.ppermute(array, axis, [(i, (i + by) % count) for i in range(count)])  36.2 us
    all_to_all x4, starting transfers between devices, along_sy(): lax.all_to_all(copies, 'sy', 0, 0, tiled=True, axis_index_groups=groups)  21.3 us
    all_to_all x4, waiting for transfers between devices, along_sy(): lax.all_to_all(copies, 'sy', 0, 0, tiled=True, axis_index_groups=groups)  16.2 us
    ppermute x4, starting transfers between devices, along_sy(): other = lax.ppermute(same, 'sy', [(i, i ^ 1) for i in range(count)])  15.1 us
    ppermute x18, waiting for transfers between devices, shifted(): lax.ppermute(array, axis, [(i, (i + by) % count) for i in range(count)])  13.5 us
    all_to_all x1, starting transfers between devices, local(): lax.all_to_all(last.reshape(gx * gy, 1, cases), ('sx', 'sy'), 0, 0, tiled...  12.3 us
    all_to_all x2, starting transfers between devices, coarse_solve(): return lax.all_to_all(send, 'sx', 0, 0, tiled=True)  8.4 us
  transfers between devices with their start and end apart: 31, of which 11 were waited for; matrix products, arithmetic and copies ran while one was open for 1% of the time, Pallas kernels for 22%

profile of v4, /device:TPU:1, one launch (start us, length us, event | category | flops | bytes accessed | tf_op | source)
XLA Modules:
  0.0 212.3 jit_solution(3810609489861454223)
XLA Ops:
  1.4 2.4 %shard_map.105 = f32[16,96,128]{2,1,0:T(8,128)} custom-call(s32[2]{0:T(128)S(1)} %pad_add_fusion.refs_0_.refs_1_, s32[2,4]{1,0:T(2,128)S(1)} %bitcast.35, f32[96,96]{1,0:T(8,128)} %refs_2_.1), custom_call_target="tpu_custom_call" | custom-call | flops 3293344 | bytes 823336 | tf_op jit(solution)/shard_map/pallas_call | solution.py:110
  3.8 7.6 %all-to-all-start = ((f32[16,96,128]{2,1,0:T(8,128)}), f32[16,96,128]{2,1,0:T(8,128)S(1)}, u32[]{:S(2)}, u32[]{:S(2)}) async-start(f32[16,96,128]{2,1,0:T(8,128)} %shard_map.105), calls=%async_computation | async-start | bytes 1572864 | tf_op jit(solution)/shard_map/all_to_all | solution.py:552
  11.4 4.8 %collective-permute-start = (f32[2,12,384]{2,1,0:T(8,128)S(1)}, f32[2,12,384]{2,1,0:T(8,128)S(1)}, u32[]{:S(2)}, u32[]{:S(2)}) collective-permute-start(f32[2,12,384]{2,1,0:T(8,128)S(1)} %slice.40), channel_id=1, source_target_pairs={{0,240},{16,0},{32,16},{48,32},{64,48},{80,64},{96,80},{112,96},{1... | collective-permute-start | bytes 110600 | tf_op jit(solution)/shard_map/ppermute | solution.py:21
  16.2 1.5 collective-permute-start.1
  18.3 2.7 %collective-permute-done.1.refs_6_ = f32[12,384]{1,0:T(8,128)S(1)} collective-permute-done((f32[12,384]{1,0:T(8,128)S(1)}, f32[12,384]{1,0:T(8,128)S(1)}, u32[]{:S(2)}, u32[]{:S(2)}) %collective-permute-start.1) | collective-permute-done | bytes 18464 | tf_op jit(solution)/shard_map/ppermute | solution.py:21
  22.3 4.1 %shard_map.104 = (f32[4,384,128]{2,1,0:T(8,128)}, f32[2,384,128]{2,1,0:T(8,128)}, f32[384,128]{1,0:T(8,128)}, f32[384,128]{1,0:T(8,128)}, f32[4,384,128]{2,1,0:T...) custom-call(s32[2,2]{1,0:T(2,128)S(1)} %bitcast.37, s32[2,4]{1,0:T(2,128)S(1)} %bitcast.36, ...), custom_call_target="tpu_custom_call" | custom-call | flops 92307648 | bytes 23076912 | tf_op jit(solution)/shard_map/pallas_call | solution.py:110
  26.4 8.2 %all-to-all-start.1 = ((f32[8,48,128]{2,1,0:T(8,128)}), f32[8,48,128]{2,1,0:T(8,128)S(1)}, u32[]{:S(2)}, u32[]{:S(2)}) async-start(f32[8,48,128]{2,1,0:T(8,128)} %get-tuple-element.52), calls=%async_computation.1 | async-start | bytes 393216 | tf_op jit(solution)/shard_map/all_to_all | solution.py:27
  35.9 7.4 %all-to-all-done.1.refs_2_ = f32[8,48,128]{2,1,0:T(8,128)S(1)} async-done(((f32[8,48,128]{2,1,0:T(8,128)}), f32[8,48,128]{2,1,0:T(8,128)S(1)}, u32[]{:S(2)}, u32[]{:S(2)}) %all-to-all-start.1) | async-done | bytes 196640 | tf_op jit(solution)/shard_map/all_to_all | solution.py:27
  43.3 3.2 %collective-permute-start.2 = (f32[8,48,128]{2,1,0:T(8,128)S(1)}, f32[8,48,128]{2,1,0:T(8,128)S(1)}, u32[]{:S(2)}, u32[]{:S(2)}) collective-permute-start(f32[8,48,128]{2,1,0:T(8,128)S(1)} %all-to-all-done.1.refs_2_), channel_id=1, source_target_pairs={{0,1},{1,0},{2,3},{3,2},{4,5},{5,4},{6,7},{7,6},{8,9},{9,8},{10,11... | collective-permute-start | bytes 589832 | tf_op jit(solution)/shard_map/ppermute | solution.py:30
  47.6 2.2 %shard_map.106 = f32[8,96,128]{2,1,0:T(8,128)} custom-call(s32[16,128]{1,0:T(8,128)S(1)} %maximum_convert_fusion.refs_0_, s32[2]{0:T(128)S(1)} %pad_add_fusion.refs_0_.refs_1_, f32[16,96,128]{2,1,0:T(8,128)S(1)} %all-to-all-done.refs_2_), custom_call_target="tpu_custom_call" | custom-call | flops 4751392 | bytes 1187848 | tf_op jit(solution)/shard_map/pallas_call | solution.py:110
  49.8 3.5 %all-to-all-start.2 = ((f32[8,96,128]{2,1,0:T(8,128)}), f32[8,96,128]{2,1,0:T(8,128)S(1)}, u32[]{:S(2)}, u32[]{:S(2)}) async-start(f32[8,96,128]{2,1,0:T(8,128)} %shard_map.106), calls=%async_computation.2 | async-start | bytes 786432 | tf_op jit(solution)/shard_map/all_to_all | solution.py:27
  54.3 4.0 %collective-permute-start.5 = (f32[2,8,16,128]{3,2,1,0:T(8,128)S(1)}, f32[2,8,16,128]{3,2,1,0:T(8,128)S(1)}, u32[]{:S(2)}, u32[]{:S(2)}) collective-permute-start(f32[2,8,16,128]{3,2,1,0:T(8,128)S(1)} %pad_maximum_fusion), channel_id=1, source_target_pairs={{0,240},{16,0},{32,16},{48,32},{64,48},{80,64},{96,80},{112,96},{1... | collective-permute-start | bytes 393224 | tf_op jit(solution)/shard_map/ppermute | solution.py:21
  58.3 4.6 %shard_map.107 = (f32[2,384,128]{2,1,0:T(8,128)}, f32[384,128]{1,0:T(8,128)}, bf16[2,1536,256]{2,1,0:T(8,128)(2,1)S(1)}) custom-call(f32[2,384,128]{2,1,0:T(8,128)} %get-tuple-element.54.refs_0_.refs_6_, f32[384,128]{1,0:T(8,128)} %get-tuple-element.57.refs_1_.refs_7_, f32[384,128]{1,0:T(8,128)} %get-tuple-element.55.refs_2_.refs_8_, ...), custom_call_target="tpu_custom_call" | custom-call | flops 95944704 | bytes 23986176 | tf_op jit(solution)/shard_map/pallas_call | solution.py:110
  62.9 4.9 %shard_map.108.refs_0_ = f32[4,384,128]{2,1,0:T(8,128)S(1)} custom-call(bf16[2,1536,256]{2,1,0:T(8,128)(2,1)S(1)} %get-tuple-element.60.refs_0_, bf16[8,384,1536]{2,1,0:T(8,128)(2,1)} %bitcast.40), custom_call_target="tpu_custom_call" | custom-call | flops 91226112 | bytes 22806528 | tf_op jit(solution)/shard_map/pallas_call | solution.py:110
  67.9 3.9 %collective-permute-start.9 = (f32[8,96,128]{2,1,0:T(8,128)S(1)}, f32[8,96,128]{2,1,0:T(8,128)S(1)}, u32[]{:S(2)}, u32[]{:S(2)}) collective-permute-start(f32[8,96,128]{2,1,0:T(8,128)S(1)} %all-to-all-done.2.refs_2_), channel_id=1, source_target_pairs={{0,1},{1,0},{2,3},{3,2},{4,5},{5,4},{6,7},{7,6},{8,9},{9,8},{10,11... | collective-permute-start | bytes 1179656 | tf_op jit(solution)/shard_map/ppermute | solution.py:30
  72.5 1.6 collective-permute-start.7
  74.3 2.4 %shard_map.109.refs_1_.refs_2_ = f32[256,128]{1,0:T(8,128)} custom-call(s32[16,128]{1,0:T(8,128)S(1)} %maximum_convert_fusion.1.refs_0_, s32[2]{0:T(128)S(1)} %pad_add_fusion.refs_0_.refs_1_, f32[8,96,128]{2,1,0:T(8,128)S(1)} %all-to-all-done.2.refs_2_, f32[8,96,128]{2,1,0:T(8,128)S(1)} %collective-permute-done.9.refs_3_), custom_call_target="tpu_custom_call" | custom-call | flops 3702816 | bytes 925704 | tf_op jit(solution)/shard_map/pallas_call | solution.py:110
  76.7 2.1 shard_map.110
  78.8 3.6 %all-to-all-start.3 = ((f32[16,48,128]{2,1,0:T(8,128)}), f32[16,48,128]{2,1,0:T(8,128)S(1)}, u32[]{:S(2)}, u32[]{:S(2)}) async-start(f32[16,48,128]{2,1,0:T(8,128)} %shard_map.110), calls=%async_computation.3 | async-start | bytes 786432 | tf_op jit(solution)/shard_map/all_to_all | solution.py:654
  82.7 5.1 %collective-permute-done.8.refs_2_ = f32[384,128]{1,0:T(8,128)S(1)} collective-permute-done((f32[384,128]{1,0:T(8,128)S(1)}, f32[384,128]{1,0:T(8,128)S(1)}, u32[]{:S(2)}, u32[]{:S(2)}) %collective-permute-start.8) | collective-permute-done | bytes 196640 | tf_op jit(solution)/shard_map/ppermute | solution.py:21
  87.8 4.2 %all-to-all-done.3.refs_3_ = f32[16,48,128]{2,1,0:T(8,128)S(1)} async-done(((f32[16,48,128]{2,1,0:T(8,128)}), f32[16,48,128]{2,1,0:T(8,128)S(1)}, u32[]{:S(2)}, u32[]{:S(2)}) %all-to-all-start.3) | async-done | bytes 393248 | tf_op jit(solution)/shard_map/all_to_all | solution.py:654
  92.0 3.7 %shard_map.111 = (f32[4,384,128]{2,1,0:T(8,128)}, f32[2,384,128]{2,1,0:T(8,128)}, f32[384,128]{1,0:T(8,128)}, f32[384,128]{1,0:T(8,128)}, f32[8,128]{1,0:T(8,128...) custom-call(f32[4,384,128]{2,1,0:T(8,128)S(1)} %shard_map.108.refs_0_, ...), custom_call_target="tpu_custom_call" | custom-call | flops 22937600 | bytes 5734400 | tf_op jit(solution)/shard_map/pallas_call | solution.py:110
  95.7 6.3 %all-to-all-start.4 = ((f32[8,48,128]{2,1,0:T(8,128)}), f32[8,48,128]{2,1,0:T(8,128)S(1)}, u32[]{:S(2)}, u32[]{:S(2)}) async-start(f32[8,48,128]{2,1,0:T(8,128)} %get-tuple-element.77), calls=%async_computation.4 | async-start | bytes 393216 | tf_op jit(solution)/shard_map/all_to_all | solution.py:27
  102.2 3.6 %collective-permute-start.11 = (f32[384,128]{1,0:T(8,128)}, f32[384,128]{1,0:T(8,128)S(1)}, u32[]{:S(2)}, u32[]{:S(2)}) collective-permute-start(f32[384,128]{1,0:T(8,128)} %get-tuple-element.73.refs_2_.refs_8_.refs_11_), channel_id=1, source_target_pairs={{0,1},{1,2},{2,3},{3,4},{4,5},{5,6},{6,7},{7,8},{8,9},{9,10},{10,1... | collective-permute-start | bytes 589832 | tf_op jit(solution)/shard_map/ppermute | solution.py:21
  105.9 4.7 %all-to-all-done.4.refs_4_ = f32[8,48,128]{2,1,0:T(8,128)S(1)} async-done(((f32[8,48,128]{2,1,0:T(8,128)}), f32[8,48,128]{2,1,0:T(8,128)S(1)}, u32[]{:S(2)}, u32[]{:S(2)}) %all-to-all-start.4) | async-done | bytes 196640 | tf_op jit(solution)/shard_map/all_to_all | solution.py:27
  110.6 3.7 %collective-permute-start.16 = (f32[8,48,128]{2,1,0:T(8,128)S(1)}, f32[8,48,128]{2,1,0:T(8,128)S(1)}, u32[]{:S(2)}, u32[]{:S(2)}) collective-permute-start(f32[8,48,128]{2,1,0:T(8,128)S(1)} %all-to-all-done.4.refs_4_), channel_id=1, source_target_pairs={{0,1},{1,0},{2,3},{3,2},{4,5},{5,4},{6,7},{7,6},{8,9},{9,8},{10,11... | collective-permute-start | bytes 589832 | tf_op jit(solution)/shard_map/ppermute | solution.py:30
  114.7 4.4 %collective-permute-start.15 = (f32[256,128]{1,0:T(8,128)S(1)}, f32[256,128]{1,0:T(8,128)S(1)}, u32[]{:S(2)}, u32[]{:S(2)}) collective-permute-start(f32[256,128]{1,0:T(8,128)S(1)} %copy-done.3), channel_id=1, source_target_pairs={{0,240},{16,0},{32,16},{48,32},{64,48},{80,64},{96,80},{112,96},{1... | collective-permute-start | bytes 393224 | tf_op jit(solution)/shard_map/ppermute | solution.py:21
  119.0 4.6 %shard_map.112 = (f32[2,384,128]{2,1,0:T(8,128)}, f32[384,128]{1,0:T(8,128)}, bf16[2,1536,256]{2,1,0:T(8,128)(2,1)S(1)}) custom-call(f32[2,384,128]{2,1,0:T(8,128)} %get-tuple-element.71.refs_0_.refs_6_.refs_9_, f32[384,128]{1,0:T(8,128)} %get-tuple-element.72.refs_1_.refs_7_.refs_10_, f32[384,128]{1,0:T(8,128)} %get-tuple-element.73.refs_2_.refs_8_.refs_11_, ...), custom_call_target="tpu_custom_call" | custom-call | flops 95944704 | bytes 23986176 | tf_op jit(solution)/shard_map/pallas_call | solution.py:110
  124.4 2.9 %shard_map.114 = f32[16,48,128]{2,1,0:T(8,128)} custom-call(f32[128,256]{1,0:T(8,128)} %dynamic-slice_bitcast_fusion.refs_0_, f32[256,128]{1,0:T(8,128)} %copy-done.4, f32[256,128]{1,0:T(8,128)} %shard_map.109.refs_1_.refs_2_, f32[256,128]{1,0:T(8,128)} %copy-done.5, f32[8,48,128]{2,1,0:T(8,128)S(1)} %all-to-all-done.4.refs_4_, ...), custom_call_target="tpu_custom_call" | custom-call | flops 5242880 | bytes 1310720 | tf_op jit(solution)/shard_map/pallas_call | solution.py:110
  127.3 4.8 %all-to-all-start.5 = ((f32[16,48,128]{2,1,0:T(8,128)}), f32[16,48,128]{2,1,0:T(8,128)S(1)}, u32[]{:S(2)}, u32[]{:S(2)}) async-start(f32[16,48,128]{2,1,0:T(8,128)} %shard_map.114), calls=%async_computation.5 | async-start | bytes 786432 | tf_op jit(solution)/shard_map/all_to_all | solution.py:660
  133.5 4.8 %shard_map.113.refs_0_ = f32[4,384,128]{2,1,0:T(8,128)S(1)} custom-call(bf16[2,1536,256]{2,1,0:T(8,128)(2,1)S(1)} %get-tuple-element.74.refs_0_, bf16[8,384,1536]{2,1,0:T(8,128)(2,1)} %bitcast.42), custom_call_target="tpu_custom_call" | custom-call | flops 91226112 | bytes 22806528 | tf_op jit(solution)/shard_map/pallas_call | solution.py:110
  138.3 2.5 %all-to-all-done.5.refs_3_ = f32[16,48,128]{2,1,0:T(8,128)S(1)} async-done(((f32[16,48,128]{2,1,0:T(8,128)}), f32[16,48,128]{2,1,0:T(8,128)S(1)}, u32[]{:S(2)}, u32[]{:S(2)}) %all-to-all-start.5) | async-done | bytes 393248 | tf_op jit(solution)/shard_map/all_to_all | solution.py:660
  140.8 3.9 %shard_map.115 = (f32[4,384,128]{2,1,0:T(8,128)}, f32[2,384,128]{2,1,0:T(8,128)}, f32[384,128]{1,0:T(8,128)}, f32[384,128]{1,0:T(8,128)}, f32[8,128]{1,0:T(8,128...) custom-call(f32[4,384,128]{2,1,0:T(8,128)S(1)} %shard_map.113.refs_0_, ...), custom_call_target="tpu_custom_call" | custom-call | flops 22953984 | bytes 5738496 | tf_op jit(solution)/shard_map/pallas_call | solution.py:110
  144.7 3.4 %all-to-all-start.6 = ((f32[8,48,128]{2,1,0:T(8,128)}), f32[8,48,128]{2,1,0:T(8,128)S(1)}, u32[]{:S(2)}, u32[]{:S(2)}) async-start(f32[8,48,128]{2,1,0:T(8,128)} %get-tuple-element.79), calls=%async_computation.6 | async-start | bytes 393216 | tf_op jit(solution)/shard_map/all_to_all | solution.py:27
  148.7 3.9 %collective-permute-start.18 = (f32[384,128]{1,0:T(8,128)}, f32[384,128]{1,0:T(8,128)S(1)}, u32[]{:S(2)}, u32[]{:S(2)}) collective-permute-start(f32[384,128]{1,0:T(8,128)} %get-tuple-element.82.refs_2_.refs_14_), channel_id=1, source_target_pairs={{0,1},{1,2},{2,3},{3,4},{4,5},{5,6},{6,7},{7,8},{8,9},{9,10},{10,1... | collective-permute-start | bytes 589832 | tf_op jit(solution)/shard_map/ppermute | solution.py:21
  152.6 4.1 %all-to-all-done.6.refs_4_ = f32[8,48,128]{2,1,0:T(8,128)S(1)} async-done(((f32[8,48,128]{2,1,0:T(8,128)}), f32[8,48,128]{2,1,0:T(8,128)S(1)}, u32[]{:S(2)}, u32[]{:S(2)}) %all-to-all-start.6) | async-done | bytes 196640 | tf_op jit(solution)/shard_map/all_to_all | solution.py:27
  156.7 4.3 %collective-permute-start.21 = (f32[8,48,128]{2,1,0:T(8,128)S(1)}, f32[8,48,128]{2,1,0:T(8,128)S(1)}, u32[]{:S(2)}, u32[]{:S(2)}) collective-permute-start(f32[8,48,128]{2,1,0:T(8,128)S(1)} %all-to-all-done.6.refs_4_), channel_id=1, source_target_pairs={{0,1},{1,0},{2,3},{3,2},{4,5},{5,4},{6,7},{7,6},{8,9},{9,8},{10,11... | collective-permute-start | bytes 589832 | tf_op jit(solution)/shard_map/ppermute | solution.py:30
  161.0 4.6 %shard_map.116 = (f32[2,384,128]{2,1,0:T(8,128)}, f32[384,128]{1,0:T(8,128)}, bf16[2,1536,256]{2,1,0:T(8,128)(2,1)S(1)}, f32[8,128]{1,0:T(8,128)S(1)}) custom-call(f32[2,384,128]{2,1,0:T(8,128)} %get-tuple-element.80.refs_0_.refs_12_, f32[384,128]{1,0:T(8,128)} %get-tuple-element.81.refs_1_.refs_13_, f32[384,128]{1,0:T(8,128)} %get-tuple-element.82.refs_2_.refs_14_, ...), custom_call_target="tpu_custom_call" | custom-call | flops 95961088 | bytes 23990272 | tf_op jit(solution)/shard_map/pallas_call | solution.py:110
  165.6 2.9 %shard_map.118 = f32[16,48,128]{2,1,0:T(8,128)} custom-call(f32[128,256]{1,0:T(8,128)} %dynamic-slice_bitcast_fusion.refs_0_, f32[256,128]{1,0:T(8,128)} %copy-done.4, f32[256,128]{1,0:T(8,128)} %shard_map.109.refs_1_.refs_2_, f32[256,128]{1,0:T(8,128)} %copy-done.5, f32[8,48,128]{2,1,0:T(8,128)S(1)} %all-to-all-done.6.refs_4_, ...), custom_call_target="tpu_custom_call" | custom-call | flops 5242880 | bytes 1310720 | tf_op jit(solution)/shard_map/pallas_call | solution.py:110
  168.5 3.6 %all-to-all-start.7 = ((f32[16,48,128]{2,1,0:T(8,128)}), f32[16,48,128]{2,1,0:T(8,128)S(1)}, u32[]{:S(2)}, u32[]{:S(2)}) async-start(f32[16,48,128]{2,1,0:T(8,128)} %shard_map.118), calls=%async_computation.7 | async-start | bytes 786432 | tf_op jit(solution)/shard_map/all_to_all | solution.py:660
  172.2 4.8 %collective-permute-start.19 = (f32[2,384,128]{2,1,0:T(8,128)}, f32[2,384,128]{2,1,0:T(8,128)S(1)}, u32[]{:S(2)}, u32[]{:S(2)}) collective-permute-start(f32[2,384,128]{2,1,0:T(8,128)} %get-tuple-element.88), channel_id=1, source_target_pairs={{0,240},{16,0},{32,16},{48,32},{64,48},{80,64},{96,80},{112,96},{1... | collective-permute-start | bytes 1179656 | tf_op jit(solution)/shard_map/ppermute | solution.py:21
  176.9 4.9 %shard_map.117 = (f32[4,384,128]{2,1,0:T(8,128)S(1)}, f32[8,128]{1,0:T(8,128)S(1)}) custom-call(bf16[2,1536,256]{2,1,0:T(8,128)(2,1)S(1)} %get-tuple-element.85.refs_0_, f32[8,128]{1,0:T(8,128)S(1)} %get-tuple-element.86.refs_1_, bf16[8,384,1536]{2,1,0:T(8,128)(2,1)} %bitcast.44), custom_call_target="tpu_custom_call" | custom-call | flops 91258880 | bytes 22814720 | tf_op jit(solution)/shard_map/pallas_call | solution.py:110
  183.3 12.3 %all-to-all-start.8 = ((f32[256,1,128]{2,1,0:T(1,128)}), f32[256,1,128]{2,1,0:T(1,128)S(1)}, u32[]{:S(2)}, u32[]{:S(2)}) async-start(f32[256,1,128]{2,1,0:T(1,128)} %bitcast.46), calls=%async_computation.8 | async-start | bytes 262144 | tf_op jit(solution)/shard_map/all_to_all | solution.py:677
  195.5 2.2 %collective-permute-start.20 = (f32[384,128]{1,0:T(8,128)S(1)}, f32[384,128]{1,0:T(8,128)S(1)}, u32[]{:S(2)}, u32[]{:S(2)}) collective-permute-start(f32[384,128]{1,0:T(8,128)S(1)} %copy-done.11), channel_id=1, source_target_pairs={{0,15},{1,0},{2,1},{3,2},{4,3},{5,4},{6,5},{7,6},{8,7},{9,8},{10,9... | collective-permute-start | bytes 589832 | tf_op jit(solution)/shard_map/ppermute | solution.py:21
  197.7 4.4 %collective-permute-done.20.refs_2_ = f32[384,128]{1,0:T(8,128)S(1)} collective-permute-done((f32[384,128]{1,0:T(8,128)S(1)}, f32[384,128]{1,0:T(8,128)S(1)}, u32[]{:S(2)}, u32[]{:S(2)}) %collective-permute-start.20) | collective-permute-done | bytes 196640 | tf_op jit(solution)/shard_map/ppermute | solution.py:21
  202.1 2.6 %shard_map.119 = (f32[4,384,128]{2,1,0:T(8,128)}, f32[8,128]{1,0:T(8,128)}) custom-call(f32[4,384,128]{2,1,0:T(8,128)S(1)} %get-tuple-element.87.refs_0_, f32[2,384,128]{2,1,0:T(8,128)S(1)} %collective-permute-done.19.refs_1_, f32[384,128]{1,0:T(8,128)S(1)} %collective-permute-done.20.refs_2_, f32[16,48,128]{2,1,0:T(8,128)S(1)} %all-to-all-done.7.refs_3_.refs_2_, ...), custom_call_target="tpu_custom_call" | custom-call | flops 15745024 | bytes 3936256 | tf_op jit(solution)/shard_map/pallas_call | solution.py:110
  204.7 3.7 %all-to-all-done.8 = f32[256,1,128]{2,1,0:T(1,128)S(1)} async-done(((f32[256,1,128]{2,1,0:T(1,128)}), f32[256,1,128]{2,1,0:T(1,128)S(1)}, u32[]{:S(2)}, u32[]{:S(2)}) %all-to-all-start.8) | async-done | bytes 131104 | tf_op jit(solution)/shard_map/all_to_all | solution.py:677
  208.4 3.8 %shard_map.121 = (f32[4,384,128]{2,1,0:T(8,128)}, f32[4,384,128]{2,1,0:T(8,128)}) custom-call(f32[8,128]{1,0:T(8,128)} %get-tuple-element.69.refs_9_.refs_0_, f32[8,128]{1,0:T(8,128)} %get-tuple-element.70.refs_1_, f32[8,128]{1,0:T(8,128)} %get-tuple-element.78.refs_2_, f32[8,128]{1,0:T(8,128)} %get-tuple-element.91.refs_3_, f32[256,128]{1,0:T(8,128)S(1)} %bitcast.34, ...), custom_call_target="tpu_custom_call" | custom-call | flops 28901376 | bytes 7225344 | tf_op jit(solution)/shard_map/pallas_call | solution.py:110
  (73 shorter events, 12.1 us)
Async XLA Ops:
  0.6 21.7 %copy-start.1 = (s32[1,2,4]{2,1,0:T(2,128)S(1)}, s32[1,2,4]{2,1,0:T(2,128)}, u32[]{:S(2)}) copy-start(s32[1,2,4]{2,1,0:T(2,128)} %param.12) | copy-start | bytes 100
  0.6 17.1 %copy-start.8 = (f32[1,2,2,384]{3,2,1,0:T(2,128)S(1)}, f32[1,2,2,384]{3,2,1,0:T(2,128)}, u32[]{:S(2)}) copy-start(f32[1,2,2,384]{3,2,1,0:T(2,128)} %param.10) | copy-start | bytes 18436
  0.7 21.7 %copy-start.2 = (s32[1,2,2]{2,1,0:T(2,128)S(1)}, s32[1,2,2]{2,1,0:T(2,128)}, u32[]{:S(2)}) copy-start(s32[1,2,2]{2,1,0:T(2,128)} %param.11) | copy-start | bytes 52
  0.7 0.7 copy-start
  1.4 10.0 %copy-start.6 = (bf16[1,2,12,1536]{3,1,2,0:T(2,128)(2,1)S(1)}, bf16[1,2,12,1536]{3,1,2,0:T(2,128)(2,1)}, u32[]{:S(2)}) copy-start(bf16[1,2,12,1536]{3,1,2,0:T(2,128)(2,1)} %param.14) | copy-start | bytes 221188
  3.8 22.6 %all-to-all-start = ((f32[16,96,128]{2,1,0:T(8,128)}), f32[16,96,128]{2,1,0:T(8,128)S(1)}, u32[]{:S(2)}, u32[]{:S(2)}) async-start(f32[16,96,128]{2,1,0:T(8,128)} %shard_map.105), calls=%async_computation | async-start | bytes 1572864 | tf_op jit(solution)/shard_map/all_to_all | solution.py:552
  11.4 10.9 %collective-permute-start = (f32[2,12,384]{2,1,0:T(8,128)S(1)}, f32[2,12,384]{2,1,0:T(8,128)S(1)}, u32[]{:S(2)}, u32[]{:S(2)}) collective-permute-start(f32[2,12,384]{2,1,0:T(8,128)S(1)} %slice.40), channel_id=1, source_target_pairs={{0,240},{16,0},{32,16},{48,32},{64,48},{80,64},{96,80},{112,96},{1... | collective-permute-start | bytes 110600 | tf_op jit(solution)/shard_map/ppermute | solution.py:21
  16.2 4.8 %collective-permute-start.1 = (f32[12,384]{1,0:T(8,128)S(1)}, f32[12,384]{1,0:T(8,128)S(1)}, u32[]{:S(2)}, u32[]{:S(2)}) collective-permute-start(f32[12,384]{1,0:T(8,128)S(1)} %slice_bitcast_fusion.4), channel_id=1, source_target_pairs={{0,15},{1,0},{2,1},{3,2},{4,3},{5,4},{6,5},{7,6},{8,7},{9,8},{10,9... | collective-permute-start | bytes 55304 | tf_op jit(solution)/shard_map/ppermute | solution.py:21
  26.4 16.9 %all-to-all-start.1 = ((f32[8,48,128]{2,1,0:T(8,128)}), f32[8,48,128]{2,1,0:T(8,128)S(1)}, u32[]{:S(2)}, u32[]{:S(2)}) async-start(f32[8,48,128]{2,1,0:T(8,128)} %get-tuple-element.52), calls=%async_computation.1 | async-start | bytes 393216 | tf_op jit(solution)/shard_map/all_to_all | solution.py:27
  34.6 15.2 %collective-permute-start.3 = (f32[2,384,128]{2,1,0:T(8,128)}, f32[2,384,128]{2,1,0:T(8,128)S(1)}, u32[]{:S(2)}, u32[]{:S(2)}) collective-permute-start(f32[2,384,128]{2,1,0:T(8,128)} %get-tuple-element.54.refs_0_.refs_6_), channel_id=1, source_target_pairs={{0,16},{16,32},{32,48},{48,64},{64,80},{80,96},{96,112},{112,128},... | collective-permute-start | bytes 1179656 | tf_op jit(solution)/shard_map/ppermute | solution.py:21
  43.3 4.3 %collective-permute-start.2 = (f32[8,48,128]{2,1,0:T(8,128)S(1)}, f32[8,48,128]{2,1,0:T(8,128)S(1)}, u32[]{:S(2)}, u32[]{:S(2)}) collective-permute-start(f32[8,48,128]{2,1,0:T(8,128)S(1)} %all-to-all-done.1.refs_2_), channel_id=1, source_target_pairs={{0,1},{1,0},{2,3},{3,2},{4,5},{5,4},{6,7},{7,6},{8,9},{9,8},{10,11... | collective-permute-start | bytes 589832 | tf_op jit(solution)/shard_map/ppermute | solution.py:30
  46.5 3.3 %collective-permute-start.4 = (f32[384,128]{1,0:T(8,128)}, f32[384,128]{1,0:T(8,128)S(1)}, u32[]{:S(2)}, u32[]{:S(2)}) collective-permute-start(f32[384,128]{1,0:T(8,128)} %get-tuple-element.55.refs_2_.refs_8_), channel_id=1, source_target_pairs={{0,1},{1,2},{2,3},{3,4},{4,5},{5,6},{6,7},{7,8},{8,9},{9,10},{10,1... | collective-permute-start | bytes 589832 | tf_op jit(solution)/shard_map/ppermute | solution.py:21
  49.8 18.0 %all-to-all-start.2 = ((f32[8,96,128]{2,1,0:T(8,128)}), f32[8,96,128]{2,1,0:T(8,128)S(1)}, u32[]{:S(2)}, u32[]{:S(2)}) async-start(f32[8,96,128]{2,1,0:T(8,128)} %shard_map.106), calls=%async_computation.2 | async-start | bytes 786432 | tf_op jit(solution)/shard_map/all_to_all | solution.py:27
  53.4 14.5 %collective-permute-start.6 = (f32[2,8,16,128]{3,2,1,0:T(8,128)S(1)}, f32[2,8,16,128]{3,2,1,0:T(8,128)S(1)}, u32[]{:S(2)}, u32[]{:S(2)}) collective-permute-start(f32[2,8,16,128]{3,2,1,0:T(8,128)S(1)} %pad_maximum_fusion.1), channel_id=1, source_target_pairs={{0,16},{16,32},{32,48},{48,64},{64,80},{80,96},{96,112},{112,128},... | collective-permute-start | bytes 393224 | tf_op jit(solution)/shard_map/ppermute | solution.py:21
  54.3 13.6 %collective-permute-start.5 = (f32[2,8,16,128]{3,2,1,0:T(8,128)S(1)}, f32[2,8,16,128]{3,2,1,0:T(8,128)S(1)}, u32[]{:S(2)}, u32[]{:S(2)}) collective-permute-start(f32[2,8,16,128]{3,2,1,0:T(8,128)S(1)} %pad_maximum_fusion), channel_id=1, source_target_pairs={{0,240},{16,0},{32,16},{48,32},{64,48},{80,64},{96,80},{112,96},{1... | collective-permute-start | bytes 393224 | tf_op jit(solution)/shard_map/ppermute | solution.py:21
  62.9 8.9 %copy-start.7 = (f32[2,128,256]{2,1,0:T(8,128)S(1)}, f32[2,128,256]{2,1,0:T(8,128)}, u32[]{:S(2)}) copy-start(f32[2,128,256]{2,1,0:T(8,128)} %constant.29.clone) | copy-start | bytes 786436
  62.9 9.5 %copy-start.9 = (f32[2,384,128]{2,1,0:T(8,128)S(1)}, f32[2,384,128]{2,1,0:T(8,128)}, u32[]{:S(2)}) copy-start(f32[2,384,128]{2,1,0:T(8,128)} %get-tuple-element.62) | copy-start | bytes 1179652
  67.9 6.4 %collective-permute-start.9 = (f32[8,96,128]{2,1,0:T(8,128)S(1)}, f32[8,96,128]{2,1,0:T(8,128)S(1)}, u32[]{:S(2)}, u32[]{:S(2)}) collective-permute-start(f32[8,96,128]{2,1,0:T(8,128)S(1)} %all-to-all-done.2.refs_2_), channel_id=1, source_target_pairs={{0,1},{1,0},{2,3},{3,2},{4,5},{5,4},{6,7},{7,6},{8,9},{9,8},{10,11... | collective-permute-start | bytes 1179656 | tf_op jit(solution)/shard_map/ppermute | solution.py:30
  72.5 15.3 %collective-permute-start.7 = (f32[2,384,128]{2,1,0:T(8,128)S(1)}, f32[2,384,128]{2,1,0:T(8,128)S(1)}, u32[]{:S(2)}, u32[]{:S(2)}) collective-permute-start(f32[2,384,128]{2,1,0:T(8,128)S(1)} %copy-done.9), channel_id=1, source_target_pairs={{0,240},{16,0},{32,16},{48,32},{64,48},{80,64},{96,80},{112,96},{1... | collective-permute-start | bytes 1179656 | tf_op jit(solution)/shard_map/ppermute | solution.py:21
  74.3 8.1 %copy-start.10 = (f32[384,128]{1,0:T(8,128)S(1)}, f32[384,128]{1,0:T(8,128)}, u32[]{:S(2)}) copy-start(f32[384,128]{1,0:T(8,128)} %get-tuple-element.63) | copy-start | bytes 589828
  78.8 13.2 %all-to-all-start.3 = ((f32[16,48,128]{2,1,0:T(8,128)}), f32[16,48,128]{2,1,0:T(8,128)S(1)}, u32[]{:S(2)}, u32[]{:S(2)}) async-start(f32[16,48,128]{2,1,0:T(8,128)} %shard_map.110), calls=%async_computation.3 | async-start | bytes 786432 | tf_op jit(solution)/shard_map/all_to_all | solution.py:654
  82.4 5.4 %collective-permute-start.8 = (f32[384,128]{1,0:T(8,128)S(1)}, f32[384,128]{1,0:T(8,128)S(1)}, u32[]{:S(2)}, u32[]{:S(2)}) collective-permute-start(f32[384,128]{1,0:T(8,128)S(1)} %copy-done.10), channel_id=1, source_target_pairs={{0,15},{1,0},{2,1},{3,2},{4,3},{5,4},{6,5},{7,6},{8,7},{9,8},{10,9... | collective-permute-start | bytes 589832 | tf_op jit(solution)/shard_map/ppermute | solution.py:21
  92.0 22.3 %copy-start.3 = (f32[256,128]{1,0:T(8,128)S(1)}, f32[256,128]{1,0:T(8,128)}, u32[]{:S(2)}) copy-start(f32[256,128]{1,0:T(8,128)} %shard_map.109.refs_1_.refs_2_) | copy-start | bytes 393220
  95.7 14.9 %all-to-all-start.4 = ((f32[8,48,128]{2,1,0:T(8,128)}), f32[8,48,128]{2,1,0:T(8,128)S(1)}, u32[]{:S(2)}, u32[]{:S(2)}) async-start(f32[8,48,128]{2,1,0:T(8,128)} %get-tuple-element.77), calls=%async_computation.4 | async-start | bytes 393216 | tf_op jit(solution)/shard_map/all_to_all | solution.py:27
  102.0 17.1 %collective-permute-start.10 = (f32[2,384,128]{2,1,0:T(8,128)}, f32[2,384,128]{2,1,0:T(8,128)S(1)}, u32[]{:S(2)}, u32[]{:S(2)}) collective-permute-start(f32[2,384,128]{2,1,0:T(8,128)} %get-tuple-element.71.refs_0_.refs_6_.refs_9_), channel_id=1, source_target_pairs={{0,16},{16,32},{32,48},{48,64},{64,80},{80,96},{96,112},{112,128},... | collective-permute-start | bytes 1179656 | tf_op jit(solution)/shard_map/ppermute | solution.py:21
  102.2 16.8 %collective-permute-start.11 = (f32[384,128]{1,0:T(8,128)}, f32[384,128]{1,0:T(8,128)S(1)}, u32[]{:S(2)}, u32[]{:S(2)}) collective-permute-start(f32[384,128]{1,0:T(8,128)} %get-tuple-element.73.refs_2_.refs_8_.refs_11_), channel_id=1, source_target_pairs={{0,1},{1,2},{2,3},{3,4},{4,5},{5,6},{6,7},{7,8},{8,9},{9,10},{10,1... | collective-permute-start | bytes 589832 | tf_op jit(solution)/shard_map/ppermute | solution.py:21
  110.6 13.2 %collective-permute-start.16 = (f32[8,48,128]{2,1,0:T(8,128)S(1)}, f32[8,48,128]{2,1,0:T(8,128)S(1)}, u32[]{:S(2)}, u32[]{:S(2)}) collective-permute-start(f32[8,48,128]{2,1,0:T(8,128)S(1)} %all-to-all-done.4.refs_4_), channel_id=1, source_target_pairs={{0,1},{1,0},{2,3},{3,2},{4,5},{5,4},{6,7},{7,6},{8,9},{9,8},{10,11... | collective-permute-start | bytes 589832 | tf_op jit(solution)/shard_map/ppermute | solution.py:30
  114.2 9.5 %collective-permute-start.14 = (f32[256,128]{1,0:T(8,128)S(1)}, f32[256,128]{1,0:T(8,128)S(1)}, u32[]{:S(2)}, u32[]{:S(2)}) collective-permute-start(f32[256,128]{1,0:T(8,128)S(1)} %copy-done.3), channel_id=1, source_target_pairs={{0,16},{16,32},{32,48},{48,64},{64,80},{80,96},{96,112},{112,128},... | collective-permute-start | bytes 393224 | tf_op jit(solution)/shard_map/ppermute | solution.py:21
  114.7 9.1 %collective-permute-start.15 = (f32[256,128]{1,0:T(8,128)S(1)}, f32[256,128]{1,0:T(8,128)S(1)}, u32[]{:S(2)}, u32[]{:S(2)}) collective-permute-start(f32[256,128]{1,0:T(8,128)S(1)} %copy-done.3), channel_id=1, source_target_pairs={{0,240},{16,0},{32,16},{48,32},{64,48},{80,64},{96,80},{112,96},{1... | collective-permute-start | bytes 393224 | tf_op jit(solution)/shard_map/ppermute | solution.py:21
  123.6 14.7 %collective-permute-start.12 = (f32[2,384,128]{2,1,0:T(8,128)}, f32[2,384,128]{2,1,0:T(8,128)S(1)}, u32[]{:S(2)}, u32[]{:S(2)}) collective-permute-start(f32[2,384,128]{2,1,0:T(8,128)} %get-tuple-element.75), channel_id=1, source_target_pairs={{0,240},{16,0},{32,16},{48,32},{64,48},{80,64},{96,80},{112,96},{1... | collective-permute-start | bytes 1179656 | tf_op jit(solution)/shard_map/ppermute | solution.py:21
  123.7 0.7 copy-start.4
  123.8 0.7 copy-start.5
  127.3 13.5 %all-to-all-start.5 = ((f32[16,48,128]{2,1,0:T(8,128)}), f32[16,48,128]{2,1,0:T(8,128)S(1)}, u32[]{:S(2)}, u32[]{:S(2)}) async-start(f32[16,48,128]{2,1,0:T(8,128)} %shard_map.114), calls=%async_computation.5 | async-start | bytes 786432 | tf_op jit(solution)/shard_map/all_to_all | solution.py:660
  132.1 6.2 %collective-permute-start.13 = (f32[384,128]{1,0:T(8,128)}, f32[384,128]{1,0:T(8,128)S(1)}, u32[]{:S(2)}, u32[]{:S(2)}) collective-permute-start(f32[384,128]{1,0:T(8,128)} %get-tuple-element.76), channel_id=1, source_target_pairs={{0,15},{1,0},{2,1},{3,2},{4,3},{5,4},{6,5},{7,6},{8,7},{9,8},{10,9... | collective-permute-start | bytes 589832 | tf_op jit(solution)/shard_map/ppermute | solution.py:21
  144.7 12.0 %all-to-all-start.6 = ((f32[8,48,128]{2,1,0:T(8,128)}), f32[8,48,128]{2,1,0:T(8,128)S(1)}, u32[]{:S(2)}, u32[]{:S(2)}) async-start(f32[8,48,128]{2,1,0:T(8,128)} %get-tuple-element.79), calls=%async_computation.6 | async-start | bytes 393216 | tf_op jit(solution)/shard_map/all_to_all | solution.py:27
  148.1 12.9 %collective-permute-start.17 = (f32[2,384,128]{2,1,0:T(8,128)}, f32[2,384,128]{2,1,0:T(8,128)S(1)}, u32[]{:S(2)}, u32[]{:S(2)}) collective-permute-start(f32[2,384,128]{2,1,0:T(8,128)} %get-tuple-element.80.refs_0_.refs_12_), channel_id=1, source_target_pairs={{0,16},{16,32},{32,48},{48,64},{64,80},{80,96},{96,112},{112,128},... | collective-permute-start | bytes 1179656 | tf_op jit(solution)/shard_map/ppermute | solution.py:21
  148.7 12.3 %collective-permute-start.18 = (f32[384,128]{1,0:T(8,128)}, f32[384,128]{1,0:T(8,128)S(1)}, u32[]{:S(2)}, u32[]{:S(2)}) collective-permute-start(f32[384,128]{1,0:T(8,128)} %get-tuple-element.82.refs_2_.refs_14_), channel_id=1, source_target_pairs={{0,1},{1,2},{2,3},{3,4},{4,5},{5,6},{6,7},{7,8},{8,9},{9,10},{10,1... | collective-permute-start | bytes 589832 | tf_op jit(solution)/shard_map/ppermute | solution.py:21
  156.7 8.9 %collective-permute-start.21 = (f32[8,48,128]{2,1,0:T(8,128)S(1)}, f32[8,48,128]{2,1,0:T(8,128)S(1)}, u32[]{:S(2)}, u32[]{:S(2)}) collective-permute-start(f32[8,48,128]{2,1,0:T(8,128)S(1)} %all-to-all-done.6.refs_4_), channel_id=1, source_target_pairs={{0,1},{1,0},{2,3},{3,2},{4,5},{5,4},{6,7},{7,6},{8,9},{9,8},{10,11... | collective-permute-start | bytes 589832 | tf_op jit(solution)/shard_map/ppermute | solution.py:30
  168.5 13.3 %all-to-all-start.7 = ((f32[16,48,128]{2,1,0:T(8,128)}), f32[16,48,128]{2,1,0:T(8,128)S(1)}, u32[]{:S(2)}, u32[]{:S(2)}) async-start(f32[16,48,128]{2,1,0:T(8,128)} %shard_map.118), calls=%async_computation.7 | async-start | bytes 786432 | tf_op jit(solution)/shard_map/all_to_all | solution.py:660
  172.2 23.4 %copy-start.11 = (f32[384,128]{1,0:T(8,128)S(1)}, f32[384,128]{1,0:T(8,128)}, u32[]{:S(2)}) copy-start(f32[384,128]{1,0:T(8,128)} %get-tuple-element.89) | copy-start | bytes 589828
  172.2 29.9 %collective-permute-start.19 = (f32[2,384,128]{2,1,0:T(8,128)}, f32[2,384,128]{2,1,0:T(8,128)S(1)}, u32[]{:S(2)}, u32[]{:S(2)}) collective-permute-start(f32[2,384,128]{2,1,0:T(8,128)} %get-tuple-element.88), channel_id=1, source_target_pairs={{0,240},{16,0},{32,16},{48,32},{64,48},{80,64},{96,80},{112,96},{1... | collective-permute-start | bytes 1179656 | tf_op jit(solution)/shard_map/ppermute | solution.py:21
  183.3 25.1 %all-to-all-start.8 = ((f32[256,1,128]{2,1,0:T(1,128)}), f32[256,1,128]{2,1,0:T(1,128)S(1)}, u32[]{:S(2)}, u32[]{:S(2)}) async-start(f32[256,1,128]{2,1,0:T(1,128)} %bitcast.46), calls=%async_computation.8 | async-start | bytes 262144 | tf_op jit(solution)/shard_map/all_to_all | solution.py:677
  195.5 6.6 %collective-permute-start.20 = (f32[384,128]{1,0:T(8,128)S(1)}, f32[384,128]{1,0:T(8,128)S(1)}, u32[]{:S(2)}, u32[]{:S(2)}) collective-permute-start(f32[384,128]{1,0:T(8,128)S(1)} %copy-done.11), channel_id=1, source_target_pairs={{0,15},{1,0},{2,1},{3,2},{4,3},{5,4},{6,5},{7,6},{8,7},{9,8},{10,9... | collective-permute-start | bytes 589832 | tf_op jit(solution)/shard_map/ppermute | solution.py:21

commit v5 on v4

--- a/solution.py
+++ b/solution.py
@@ -593,7 +593,7 @@
     def held(count):
         return (pltpu.VMEM((count,) + blocks.shape[1:], BF16), pltpu.SemaphoreType.DMA((count,)))
 
-    def give(own, west, below, weigh=False):
+    def give(own, west, below, weigh=False, near=(2, 3)):
         given_east, given_north, *given = kernel_call(
             functools.partial(give_body, weigh),
             (shape(2, side), shape(side), double(2, 4 * side)) + ((shape(8),) if weigh else ()),
@@ -601,18 +601,18 @@
             raw=(blocks,),
             scratch=held(3),
             fast=(3, 4),
-            fast_outs=(2, 3),
+            fast_outs=near,
         )
         return given, shifted(given_east, "sx", -1), shifted(given_north, "sy", -1)
 
-    def keep(given, weigh=False):
+    def keep(given, weigh=False, near=True):
         return kernel_call(
             functools.partial(keep_body, weigh),
             (field, shape(8)) if weigh else (field,),
             given,
             raw=(blocks,),
             scratch=held(5),
-            fast=range(len(given)),
+            fast=range(len(given) if near else 0),
             fast_outs=(0, 1),
         )
 
@@ -630,9 +630,9 @@
         fast=(2,),
     )
     turned, west, below = lax.optimization_barrier((turned, west, below))
-    given, back_east, back_north = give(w0, west, below)
-    (kept,) = keep(given)
-    rows_same, rows_other, (kept, lower, upper) = along_sy(turned, (kept, lower, upper))
+    given, back_east, back_north = give(w0, west, below, near=())
+    lanes = lax.dynamic_index_in_dim(jnp.asarray(lane_matrices(gy)), b % 2, 0, keepdims=False)
+    rows_same, rows_other, (given, lower, upper, lanes) = along_sy(turned, (given, lower, upper, lanes))
     numbers = jnp.concatenate([rows_same[:, 0], rows_other[:, 0]], 0).astype(jnp.int32)
     own_part = kernel_call(
         functools.partial(near_body, gx),
@@ -643,7 +643,6 @@
     )
     below_part = shifted(own_part, "sx", 1)
     beyond_part = shifted(own_part, "sx", -1)
-    lanes = lax.dynamic_index_in_dim(jnp.asarray(lane_matrices(gy)), b % 2, 0, keepdims=False)
 
     send = kernel_call(
         first_coarse_body,
@@ -651,7 +650,9 @@
         (lanes, own_part, same, other, lower, upper),
         fast=range(2, 6),
     )
+    send, given = lax.optimization_barrier((send, given))
     got = lax.all_to_all(send, "sx", 0, 0, tiled=True)
+    (kept,) = keep(given, near=False)
     u1, *w1, kappa, spare0, _, message = image_call(
         kept, back_east, back_north, got, edges, gain, w0, None, half
     )
@@ -660,7 +661,7 @@
         return lax.all_to_all(send, "sx", 0, 0, tiled=True)
 
     west, below = halo(w1)
-    same, other = along_sy(message)
+    same, other, (below_part, beyond_part) = along_sy(message, (below_part, beyond_part))
     given, back_east, back_north = give(w1, west, below)
     got = coarse_solve(same, other)
     (kept,) = keep(given)

time: 214 us -> 214 us (level)
    all_to_all x4, waiting for transfers between devices: 16.2 us -> 12.2 us  [along_sy(): lax.all_to_all(copies, 'sy', 0, 0, tiled=True, axis_index_groups=groups)]
    ppermute x18, waiting for transfers between devices: 13.5 us -> 15.8 us  [shifted(): lax.ppermute(array, axis, [(i, (i + by) % count) for i in range(count)])]
  transfers between devices with their start and end apart: 31 -> 31, of which waited for: 11 -> 13; matrix products, arithmetic and copies ran while one was open for 1% -> 1% of each run, Pallas kernels for 22% -> 23%
where the time goes in v5:
time: 214 us; the launch traced here: 213 us
  starting transfers between devices  105 us (49%)
  Pallas kernels  64.5 us (30%)
  waiting for transfers between devices  39.6 us (19%)
  local copies, waits for them, and re-layouts  2.27 us (1%)
    pallas_call x18, Pallas kernels, kernel_call(): pl.pallas_call(wrapped, in_specs=[spec(k) for k in range(len(arrays))], o...  64.5 us
    ppermute x18, starting transfers between devices, shifted(): lax.ppermute(array, axis, [(i, (i + by) % count) for i in range(count)])  37.3 us
    all_to_all x4, starting transfers between devices, along_sy(): lax.all_to_all(copies, 'sy', 0, 0, tiled=True, axis_index_groups=groups)  22.1 us
    ppermute x18, waiting for transfers between devices, shifted(): lax.ppermute(array, axis, [(i, (i + by) % count) for i in range(count)])  15.8 us
    ppermute x4, starting transfers between devices, along_sy(): other = lax.ppermute(same, 'sy', [(i, i ^ 1) for i in range(count)])  14.4 us
    all_to_all x1, starting transfers between devices, local(): lax.all_to_all(last.reshape(gx * gy, 1, cases), ('sx', 'sy'), 0, 0, tiled...  12.6 us
    all_to_all x4, waiting for transfers between devices, along_sy(): lax.all_to_all(copies, 'sy', 0, 0, tiled=True, axis_index_groups=groups)  12.2 us
    all_to_all x1, starting transfers between devices, local(): columns_all = lax.all_to_all(wide, 'sx', 0, 0, tiled=True)  7.6 us
  transfers between devices with their start and end apart: 31, of which 13 were waited for; matrix products, arithmetic and copies ran while one was open for 1% of the time, Pallas kernels for 23%

profile of v5, /device:TPU:1, one launch (start us, length us, event | category | flops | bytes accessed | tf_op | source)
XLA Modules:
  0.0 212.6 jit_solution(4565967962116520207)
XLA Ops:
  1.4 2.4 %shard_map.105 = f32[16,96,128]{2,1,0:T(8,128)} custom-call(s32[2]{0:T(128)S(1)} %pad_add_fusion.refs_0_.refs_1_, s32[2,4]{1,0:T(2,128)S(1)} %bitcast.35, f32[96,96]{1,0:T(8,128)} %refs_2_.1), custom_call_target="tpu_custom_call" | custom-call | flops 3293344 | bytes 823336 | tf_op jit(solution)/shard_map/pallas_call | solution.py:110
  3.8 7.6 %all-to-all-start = ((f32[16,96,128]{2,1,0:T(8,128)}), f32[16,96,128]{2,1,0:T(8,128)S(1)}, u32[]{:S(2)}, u32[]{:S(2)}) async-start(f32[16,96,128]{2,1,0:T(8,128)} %shard_map.105), calls=%async_computation | async-start | bytes 1572864 | tf_op jit(solution)/shard_map/all_to_all | solution.py:552
  11.4 4.8 %collective-permute-start = (f32[2,12,384]{2,1,0:T(8,128)S(1)}, f32[2,12,384]{2,1,0:T(8,128)S(1)}, u32[]{:S(2)}, u32[]{:S(2)}) collective-permute-start(f32[2,12,384]{2,1,0:T(8,128)S(1)} %slice.40), channel_id=1, source_target_pairs={{0,240},{16,0},{32,16},{48,32},{64,48},{80,64},{96,80},{112,96},{1... | collective-permute-start | bytes 110600 | tf_op jit(solution)/shard_map/ppermute | solution.py:21
  16.2 1.5 collective-permute-start.1
  18.3 2.7 %collective-permute-done.1.refs_6_ = f32[12,384]{1,0:T(8,128)S(1)} collective-permute-done((f32[12,384]{1,0:T(8,128)S(1)}, f32[12,384]{1,0:T(8,128)S(1)}, u32[]{:S(2)}, u32[]{:S(2)}) %collective-permute-start.1) | collective-permute-done | bytes 18464 | tf_op jit(solution)/shard_map/ppermute | solution.py:21
  22.3 4.0 %shard_map.104 = (f32[4,384,128]{2,1,0:T(8,128)}, f32[2,384,128]{2,1,0:T(8,128)}, f32[384,128]{1,0:T(8,128)}, f32[384,128]{1,0:T(8,128)}, f32[4,384,128]{2,1,0:T...) custom-call(s32[2,2]{1,0:T(2,128)S(1)} %bitcast.37, s32[2,4]{1,0:T(2,128)S(1)} %bitcast.36, ...), custom_call_target="tpu_custom_call" | custom-call | flops 92307648 | bytes 23076912 | tf_op jit(solution)/shard_map/pallas_call | solution.py:110
  26.4 8.2 %all-to-all-start.1 = ((f32[8,48,128]{2,1,0:T(8,128)}), f32[8,48,128]{2,1,0:T(8,128)S(1)}, u32[]{:S(2)}, u32[]{:S(2)}) async-start(f32[8,48,128]{2,1,0:T(8,128)} %get-tuple-element.58), calls=%async_computation.1 | async-start | bytes 393216 | tf_op jit(solution)/shard_map/all_to_all | solution.py:27
  35.9 7.3 %all-to-all-done.1.refs_2_ = f32[8,48,128]{2,1,0:T(8,128)S(1)} async-done(((f32[8,48,128]{2,1,0:T(8,128)}), f32[8,48,128]{2,1,0:T(8,128)S(1)}, u32[]{:S(2)}, u32[]{:S(2)}) %all-to-all-start.1) | async-done | bytes 196640 | tf_op jit(solution)/shard_map/all_to_all | solution.py:27
  43.2 3.2 %collective-permute-start.2 = (f32[8,48,128]{2,1,0:T(8,128)S(1)}, f32[8,48,128]{2,1,0:T(8,128)S(1)}, u32[]{:S(2)}, u32[]{:S(2)}) collective-permute-start(f32[8,48,128]{2,1,0:T(8,128)S(1)} %all-to-all-done.1.refs_2_), channel_id=1, source_target_pairs={{0,1},{1,0},{2,3},{3,2},{4,5},{5,4},{6,7},{7,6},{8,9},{9,8},{10,11... | collective-permute-start | bytes 589832 | tf_op jit(solution)/shard_map/ppermute | solution.py:30
  47.5 2.2 %shard_map.106 = f32[8,96,128]{2,1,0:T(8,128)} custom-call(s32[16,128]{1,0:T(8,128)S(1)} %maximum_convert_fusion.refs_0_, s32[2]{0:T(128)S(1)} %pad_add_fusion.refs_0_.refs_1_, f32[16,96,128]{2,1,0:T(8,128)S(1)} %all-to-all-done.refs_2_), custom_call_target="tpu_custom_call" | custom-call | flops 4751392 | bytes 1187848 | tf_op jit(solution)/shard_map/pallas_call | solution.py:110
  49.8 3.5 %all-to-all-start.2 = ((f32[8,96,128]{2,1,0:T(8,128)}), f32[8,96,128]{2,1,0:T(8,128)S(1)}, u32[]{:S(2)}, u32[]{:S(2)}) async-start(f32[8,96,128]{2,1,0:T(8,128)} %shard_map.106), calls=%async_computation.2 | async-start | bytes 786432 | tf_op jit(solution)/shard_map/all_to_all | solution.py:27
  54.2 4.0 %collective-permute-start.5 = (f32[2,8,16,128]{3,2,1,0:T(8,128)S(1)}, f32[2,8,16,128]{3,2,1,0:T(8,128)S(1)}, u32[]{:S(2)}, u32[]{:S(2)}) collective-permute-start(f32[2,8,16,128]{3,2,1,0:T(8,128)S(1)} %pad_maximum_fusion), channel_id=1, source_target_pairs={{0,240},{16,0},{32,16},{48,32},{64,48},{80,64},{96,80},{112,96},{1... | collective-permute-start | bytes 393224 | tf_op jit(solution)/shard_map/ppermute | solution.py:21
  58.9 5.2 %shard_map.107 = (f32[2,384,128]{2,1,0:T(8,128)}, f32[384,128]{1,0:T(8,128)}, bf16[2,1536,256]{2,1,0:T(8,128)(2,1)}) custom-call(f32[2,384,128]{2,1,0:T(8,128)} %get-tuple-element.60.refs_0_.refs_6_, f32[384,128]{1,0:T(8,128)} %get-tuple-element.63.refs_1_.refs_7_, f32[384,128]{1,0:T(8,128)} %get-tuple-element.61.refs_2_.refs_8_, ...), custom_call_target="tpu_custom_call" | custom-call | flops 95944704 | bytes 23986176 | tf_op jit(solution)/shard_map/pallas_call | solution.py:110
  64.2 4.7 %collective-permute-start.7 = (f32[8,96,128]{2,1,0:T(8,128)S(1)}, f32[8,96,128]{2,1,0:T(8,128)S(1)}, u32[]{:S(2)}, u32[]{:S(2)}) collective-permute-start(f32[8,96,128]{2,1,0:T(8,128)S(1)} %all-to-all-done.2.refs_2_), channel_id=1, source_target_pairs={{0,1},{1,0},{2,3},{3,2},{4,5},{5,4},{6,7},{7,6},{8,9},{9,8},{10,11... | collective-permute-start | bytes 1179656 | tf_op jit(solution)/shard_map/ppermute | solution.py:30
  68.9 4.4 %collective-permute-start.8 = (f32[2,384,128]{2,1,0:T(8,128)}, f32[2,384,128]{2,1,0:T(8,128)S(1)}, u32[]{:S(2)}, u32[]{:S(2)}) collective-permute-start(f32[2,384,128]{2,1,0:T(8,128)} %get-tuple-element.73), channel_id=1, source_target_pairs={{0,240},{16,0},{32,16},{48,32},{64,48},{80,64},{96,80},{112,96},{1... | collective-permute-start | bytes 1179656 | tf_op jit(solution)/shard_map/ppermute | solution.py:21
  73.6 2.4 %shard_map.108.refs_1_.refs_2_ = f32[256,128]{1,0:T(8,128)} custom-call(s32[16,128]{1,0:T(8,128)S(1)} %maximum_convert_fusion.1.refs_0_, s32[2]{0:T(128)S(1)} %pad_add_fusion.refs_0_.refs_1_, f32[8,96,128]{2,1,0:T(8,128)S(1)} %all-to-all-done.2.refs_2_, f32[8,96,128]{2,1,0:T(8,128)S(1)} %collective-permute-done.7.refs_3_), custom_call_target="tpu_custom_call" | custom-call | flops 3702816 | bytes 925704 | tf_op jit(solution)/shard_map/pallas_call | solution.py:110
  76.0 2.1 shard_map.109
  78.1 3.7 %all-to-all-start.3 = ((f32[16,48,128]{2,1,0:T(8,128)}), f32[16,48,128]{2,1,0:T(8,128)S(1)}, u32[]{:S(2)}, u32[]{:S(2)}) async-start(f32[16,48,128]{2,1,0:T(8,128)} %shard_map.109), calls=%async_computation.3 | async-start | bytes 786432 | tf_op jit(solution)/shard_map/all_to_all | solution.py:654
  82.1 6.4 %shard_map.110.refs_0_ = f32[4,384,128]{2,1,0:T(8,128)S(1)} custom-call(bf16[2,1536,256]{2,1,0:T(8,128)(2,1)} %get-tuple-element.72.refs_0_, bf16[8,384,1536]{2,1,0:T(8,128)(2,1)} %bitcast.40), custom_call_target="tpu_custom_call" | custom-call | flops 91226112 | bytes 22806528 | tf_op jit(solution)/shard_map/pallas_call | solution.py:110
  88.5 2.7 %all-to-all-done.3.refs_3_ = f32[16,48,128]{2,1,0:T(8,128)S(1)} async-done(((f32[16,48,128]{2,1,0:T(8,128)}), f32[16,48,128]{2,1,0:T(8,128)S(1)}, u32[]{:S(2)}, u32[]{:S(2)}) %all-to-all-start.3) | async-done | bytes 393248 | tf_op jit(solution)/shard_map/all_to_all | solution.py:654
  91.2 3.7 %shard_map.111 = (f32[4,384,128]{2,1,0:T(8,128)}, f32[2,384,128]{2,1,0:T(8,128)}, f32[384,128]{1,0:T(8,128)}, f32[384,128]{1,0:T(8,128)}, f32[8,128]{1,0:T(8,128...) custom-call(f32[4,384,128]{2,1,0:T(8,128)S(1)} %shard_map.110.refs_0_, ...), custom_call_target="tpu_custom_call" | custom-call | flops 22937600 | bytes 5734400 | tf_op jit(solution)/shard_map/pallas_call | solution.py:110
  95.0 3.8 %all-to-all-start.4 = ((f32[8,48,128]{2,1,0:T(8,128)}), f32[8,48,128]{2,1,0:T(8,128)S(1)}, u32[]{:S(2)}, u32[]{:S(2)}) async-start(f32[8,48,128]{2,1,0:T(8,128)} %get-tuple-element.86), calls=%async_computation.4 | async-start | bytes 393216 | tf_op jit(solution)/shard_map/all_to_all | solution.py:27
  99.7 4.1 %collective-permute-start.15 = (f32[256,128]{1,0:T(8,128)S(1)}, f32[256,128]{1,0:T(8,128)S(1)}, u32[]{:S(2)}, u32[]{:S(2)}) collective-permute-start(f32[256,128]{1,0:T(8,128)S(1)} %copy-done.3), channel_id=1, source_target_pairs={{0,240},{16,0},{32,16},{48,32},{64,48},{80,64},{96,80},{112,96},{1... | collective-permute-start | bytes 393224 | tf_op jit(solution)/shard_map/ppermute | solution.py:21
  103.8 4.1 %collective-permute-start.11 = (f32[384,128]{1,0:T(8,128)}, f32[384,128]{1,0:T(8,128)S(1)}, u32[]{:S(2)}, u32[]{:S(2)}) collective-permute-start(f32[384,128]{1,0:T(8,128)} %get-tuple-element.82.refs_2_.refs_8_.refs_11_), channel_id=1, source_target_pairs={{0,1},{1,2},{2,3},{3,4},{4,5},{5,6},{6,7},{7,8},{8,9},{9,10},{10,1... | collective-permute-start | bytes 589832 | tf_op jit(solution)/shard_map/ppermute | solution.py:21
  108.0 6.0 %collective-permute-done.14.refs_1_ = f32[256,128]{1,0:T(8,128)S(1)} collective-permute-done((f32[256,128]{1,0:T(8,128)S(1)}, f32[256,128]{1,0:T(8,128)S(1)}, u32[]{:S(2)}, u32[]{:S(2)}) %collective-permute-start.14) | collective-permute-done | bytes 131104 | tf_op jit(solution)/shard_map/ppermute | solution.py:21
  114.0 2.7 %collective-permute-start.16 = (f32[8,48,128]{2,1,0:T(8,128)S(1)}, f32[8,48,128]{2,1,0:T(8,128)S(1)}, u32[]{:S(2)}, u32[]{:S(2)}) collective-permute-start(f32[8,48,128]{2,1,0:T(8,128)S(1)} %all-to-all-done.4.refs_4_), channel_id=1, source_target_pairs={{0,1},{1,0},{2,3},{3,2},{4,5},{5,4},{6,7},{7,6},{8,9},{9,8},{10,11... | collective-permute-start | bytes 589832 | tf_op jit(solution)/shard_map/ppermute | solution.py:30
  116.7 4.6 %shard_map.112 = (f32[2,384,128]{2,1,0:T(8,128)}, f32[384,128]{1,0:T(8,128)}, bf16[2,1536,256]{2,1,0:T(8,128)(2,1)S(1)}) custom-call(f32[2,384,128]{2,1,0:T(8,128)} %get-tuple-element.80.refs_0_.refs_6_.refs_9_, f32[384,128]{1,0:T(8,128)} %get-tuple-element.81.refs_1_.refs_7_.refs_10_, f32[384,128]{1,0:T(8,128)} %get-tuple-element.82.refs_2_.refs_8_.refs_11_, ...), custom_call_target="tpu_custom_call" | custom-call | flops 95944704 | bytes 23986176 | tf_op jit(solution)/shard_map/pallas_call | solution.py:110
  121.4 2.9 %shard_map.114 = f32[16,48,128]{2,1,0:T(8,128)} custom-call(f32[128,256]{1,0:T(8,128)} %dynamic-slice_bitcast_fusion.refs_0_, f32[256,128]{1,0:T(8,128)} %copy-done.4, f32[256,128]{1,0:T(8,128)} %shard_map.108.refs_1_.refs_2_, f32[256,128]{1,0:T(8,128)} %copy-done.5, f32[8,48,128]{2,1,0:T(8,128)S(1)} %all-to-all-done.4.refs_4_, ...), custom_call_target="tpu_custom_call" | custom-call | flops 5242880 | bytes 1310720 | tf_op jit(solution)/shard_map/pallas_call | solution.py:110
  124.3 3.6 %all-to-all-start.5 = ((f32[16,48,128]{2,1,0:T(8,128)}), f32[16,48,128]{2,1,0:T(8,128)S(1)}, u32[]{:S(2)}, u32[]{:S(2)}) async-start(f32[16,48,128]{2,1,0:T(8,128)} %shard_map.114), calls=%async_computation.5 | async-start | bytes 786432 | tf_op jit(solution)/shard_map/all_to_all | solution.py:661
  127.9 4.8 %shard_map.113.refs_0_ = f32[4,384,128]{2,1,0:T(8,128)S(1)} custom-call(bf16[2,1536,256]{2,1,0:T(8,128)(2,1)S(1)} %get-tuple-element.83.refs_0_, bf16[8,384,1536]{2,1,0:T(8,128)(2,1)} %bitcast.42), custom_call_target="tpu_custom_call" | custom-call | flops 91226112 | bytes 22806528 | tf_op jit(solution)/shard_map/pallas_call | solution.py:110
  133.5 4.3 %all-to-all-done.5.refs_3_ = f32[16,48,128]{2,1,0:T(8,128)S(1)} async-done(((f32[16,48,128]{2,1,0:T(8,128)}), f32[16,48,128]{2,1,0:T(8,128)S(1)}, u32[]{:S(2)}, u32[]{:S(2)}) %all-to-all-start.5) | async-done | bytes 393248 | tf_op jit(solution)/shard_map/all_to_all | solution.py:661
  137.8 3.9 %shard_map.115 = (f32[4,384,128]{2,1,0:T(8,128)}, f32[2,384,128]{2,1,0:T(8,128)}, f32[384,128]{1,0:T(8,128)}, f32[384,128]{1,0:T(8,128)}, f32[8,128]{1,0:T(8,128...) custom-call(f32[4,384,128]{2,1,0:T(8,128)S(1)} %shard_map.113.refs_0_, ...), custom_call_target="tpu_custom_call" | custom-call | flops 22953984 | bytes 5738496 | tf_op jit(solution)/shard_map/pallas_call | solution.py:110
  141.7 6.7 %all-to-all-start.6 = ((f32[8,48,128]{2,1,0:T(8,128)}), f32[8,48,128]{2,1,0:T(8,128)S(1)}, u32[]{:S(2)}, u32[]{:S(2)}) async-start(f32[8,48,128]{2,1,0:T(8,128)} %get-tuple-element.91), calls=%async_computation.6 | async-start | bytes 393216 | tf_op jit(solution)/shard_map/all_to_all | solution.py:27
  148.6 3.3 %collective-permute-start.18 = (f32[384,128]{1,0:T(8,128)}, f32[384,128]{1,0:T(8,128)S(1)}, u32[]{:S(2)}, u32[]{:S(2)}) collective-permute-start(f32[384,128]{1,0:T(8,128)} %get-tuple-element.94.refs_2_.refs_14_), channel_id=1, source_target_pairs={{0,1},{1,2},{2,3},{3,4},{4,5},{5,6},{6,7},{7,8},{8,9},{9,10},{10,1... | collective-permute-start | bytes 589832 | tf_op jit(solution)/shard_map/ppermute | solution.py:21
  151.9 4.8 %all-to-all-done.6.refs_4_ = f32[8,48,128]{2,1,0:T(8,128)S(1)} async-done(((f32[8,48,128]{2,1,0:T(8,128)}), f32[8,48,128]{2,1,0:T(8,128)S(1)}, u32[]{:S(2)}, u32[]{:S(2)}) %all-to-all-start.6) | async-done | bytes 196640 | tf_op jit(solution)/shard_map/all_to_all | solution.py:27
  156.7 3.8 %collective-permute-start.21 = (f32[8,48,128]{2,1,0:T(8,128)S(1)}, f32[8,48,128]{2,1,0:T(8,128)S(1)}, u32[]{:S(2)}, u32[]{:S(2)}) collective-permute-start(f32[8,48,128]{2,1,0:T(8,128)S(1)} %all-to-all-done.6.refs_4_), channel_id=1, source_target_pairs={{0,1},{1,0},{2,3},{3,2},{4,5},{5,4},{6,7},{7,6},{8,9},{9,8},{10,11... | collective-permute-start | bytes 589832 | tf_op jit(solution)/shard_map/ppermute | solution.py:30
  161.1 4.6 %shard_map.116 = (f32[2,384,128]{2,1,0:T(8,128)}, f32[384,128]{1,0:T(8,128)}, bf16[2,1536,256]{2,1,0:T(8,128)(2,1)S(1)}, f32[8,128]{1,0:T(8,128)S(1)}) custom-call(f32[2,384,128]{2,1,0:T(8,128)} %get-tuple-element.92.refs_0_.refs_12_, f32[384,128]{1,0:T(8,128)} %get-tuple-element.93.refs_1_.refs_13_, f32[384,128]{1,0:T(8,128)} %get-tuple-element.94.refs_2_.refs_14_, ...), custom_call_target="tpu_custom_call" | custom-call | flops 95961088 | bytes 23990272 | tf_op jit(solution)/shard_map/pallas_call | solution.py:110
  165.7 2.9 %shard_map.118 = f32[16,48,128]{2,1,0:T(8,128)} custom-call(f32[128,256]{1,0:T(8,128)} %dynamic-slice_bitcast_fusion.refs_0_, f32[256,128]{1,0:T(8,128)} %copy-done.4, f32[256,128]{1,0:T(8,128)} %shard_map.108.refs_1_.refs_2_, f32[256,128]{1,0:T(8,128)} %copy-done.5, f32[8,48,128]{2,1,0:T(8,128)S(1)} %all-to-all-done.6.refs_4_, ...), custom_call_target="tpu_custom_call" | custom-call | flops 5242880 | bytes 1310720 | tf_op jit(solution)/shard_map/pallas_call | solution.py:110
  168.6 3.6 %all-to-all-start.7 = ((f32[16,48,128]{2,1,0:T(8,128)}), f32[16,48,128]{2,1,0:T(8,128)S(1)}, u32[]{:S(2)}, u32[]{:S(2)}) async-start(f32[16,48,128]{2,1,0:T(8,128)} %shard_map.118), calls=%async_computation.7 | async-start | bytes 786432 | tf_op jit(solution)/shard_map/all_to_all | solution.py:661
  172.2 4.7 %collective-permute-start.19 = (f32[2,384,128]{2,1,0:T(8,128)}, f32[2,384,128]{2,1,0:T(8,128)S(1)}, u32[]{:S(2)}, u32[]{:S(2)}) collective-permute-start(f32[2,384,128]{2,1,0:T(8,128)} %get-tuple-element.100), channel_id=1, source_target_pairs={{0,240},{16,0},{32,16},{48,32},{64,48},{80,64},{96,80},{112,96},{1... | collective-permute-start | bytes 1179656 | tf_op jit(solution)/shard_map/ppermute | solution.py:21
  176.9 4.9 %shard_map.117 = (f32[4,384,128]{2,1,0:T(8,128)S(1)}, f32[8,128]{1,0:T(8,128)S(1)}) custom-call(bf16[2,1536,256]{2,1,0:T(8,128)(2,1)S(1)} %get-tuple-element.97.refs_0_, f32[8,128]{1,0:T(8,128)S(1)} %get-tuple-element.98.refs_1_, bf16[8,384,1536]{2,1,0:T(8,128)(2,1)} %bitcast.44), custom_call_target="tpu_custom_call" | custom-call | flops 91258880 | bytes 22814720 | tf_op jit(solution)/shard_map/pallas_call | solution.py:110
  181.8 1.4 shard_map.120
  183.2 12.6 %all-to-all-start.8 = ((f32[256,1,128]{2,1,0:T(1,128)}), f32[256,1,128]{2,1,0:T(1,128)S(1)}, u32[]{:S(2)}, u32[]{:S(2)}) async-start(f32[256,1,128]{2,1,0:T(1,128)} %bitcast.46), calls=%async_computation.8 | async-start | bytes 262144 | tf_op jit(solution)/shard_map/all_to_all | solution.py:678
  195.8 2.2 %collective-permute-start.20 = (f32[384,128]{1,0:T(8,128)S(1)}, f32[384,128]{1,0:T(8,128)S(1)}, u32[]{:S(2)}, u32[]{:S(2)}) collective-permute-start(f32[384,128]{1,0:T(8,128)S(1)} %copy-done.10), channel_id=1, source_target_pairs={{0,15},{1,0},{2,1},{3,2},{4,3},{5,4},{6,5},{7,6},{8,7},{9,8},{10,9... | collective-permute-start | bytes 589832 | tf_op jit(solution)/shard_map/ppermute | solution.py:21
  198.0 4.4 %collective-permute-done.20.refs_2_ = f32[384,128]{1,0:T(8,128)S(1)} collective-permute-done((f32[384,128]{1,0:T(8,128)S(1)}, f32[384,128]{1,0:T(8,128)S(1)}, u32[]{:S(2)}, u32[]{:S(2)}) %collective-permute-start.20) | collective-permute-done | bytes 196640 | tf_op jit(solution)/shard_map/ppermute | solution.py:21
  202.4 2.5 %shard_map.119 = (f32[4,384,128]{2,1,0:T(8,128)}, f32[8,128]{1,0:T(8,128)}) custom-call(f32[4,384,128]{2,1,0:T(8,128)S(1)} %get-tuple-element.99.refs_0_, f32[2,384,128]{2,1,0:T(8,128)S(1)} %collective-permute-done.19.refs_1_, f32[384,128]{1,0:T(8,128)S(1)} %collective-permute-done.20.refs_2_, f32[16,48,128]{2,1,0:T(8,128)S(1)} %all-to-all-done.7.refs_3_.refs_2_, ...), custom_call_target="tpu_custom_call" | custom-call | flops 15745024 | bytes 3936256 | tf_op jit(solution)/shard_map/pallas_call | solution.py:110
  205.0 3.7 %all-to-all-done.8 = f32[256,1,128]{2,1,0:T(1,128)S(1)} async-done(((f32[256,1,128]{2,1,0:T(1,128)}), f32[256,1,128]{2,1,0:T(1,128)S(1)}, u32[]{:S(2)}, u32[]{:S(2)}) %all-to-all-start.8) | async-done | bytes 131104 | tf_op jit(solution)/shard_map/all_to_all | solution.py:678
  208.7 3.8 %shard_map.121 = (f32[4,384,128]{2,1,0:T(8,128)}, f32[4,384,128]{2,1,0:T(8,128)}) custom-call(f32[8,128]{1,0:T(8,128)} %get-tuple-element.78.refs_9_.refs_0_, f32[8,128]{1,0:T(8,128)} %get-tuple-element.79.refs_1_, f32[8,128]{1,0:T(8,128)} %get-tuple-element.90.refs_2_, f32[8,128]{1,0:T(8,128)} %get-tuple-element.103.refs_3_, f32[256,128]{1,0:T(8,128)S(1)} %bitcast.34, ...), custom_call_target="tpu_custom_call" | custom-call | flops 28901376 | bytes 7225344 | tf_op jit(solution)/shard_map/pallas_call | solution.py:110
  (71 shorter events, 10.1 us)
Async XLA Ops:
  0.6 21.7 %copy-start.1 = (s32[1,2,4]{2,1,0:T(2,128)S(1)}, s32[1,2,4]{2,1,0:T(2,128)}, u32[]{:S(2)}) copy-start(s32[1,2,4]{2,1,0:T(2,128)} %param.12) | copy-start | bytes 100
  0.6 17.1 %copy-start.8 = (f32[1,2,2,384]{3,2,1,0:T(2,128)S(1)}, f32[1,2,2,384]{3,2,1,0:T(2,128)}, u32[]{:S(2)}) copy-start(f32[1,2,2,384]{3,2,1,0:T(2,128)} %param.10) | copy-start | bytes 18436
  0.7 21.7 %copy-start.2 = (s32[1,2,2]{2,1,0:T(2,128)S(1)}, s32[1,2,2]{2,1,0:T(2,128)}, u32[]{:S(2)}) copy-start(s32[1,2,2]{2,1,0:T(2,128)} %param.11) | copy-start | bytes 52
  0.7 0.7 copy-start
  1.4 10.0 %copy-start.6 = (bf16[1,2,12,1536]{3,1,2,0:T(2,128)(2,1)S(1)}, bf16[1,2,12,1536]{3,1,2,0:T(2,128)(2,1)}, u32[]{:S(2)}) copy-start(bf16[1,2,12,1536]{3,1,2,0:T(2,128)(2,1)} %param.14) | copy-start | bytes 221188
  3.8 22.6 %all-to-all-start = ((f32[16,96,128]{2,1,0:T(8,128)}), f32[16,96,128]{2,1,0:T(8,128)S(1)}, u32[]{:S(2)}, u32[]{:S(2)}) async-start(f32[16,96,128]{2,1,0:T(8,128)} %shard_map.105), calls=%async_computation | async-start | bytes 1572864 | tf_op jit(solution)/shard_map/all_to_all | solution.py:552
  11.4 10.9 %collective-permute-start = (f32[2,12,384]{2,1,0:T(8,128)S(1)}, f32[2,12,384]{2,1,0:T(8,128)S(1)}, u32[]{:S(2)}, u32[]{:S(2)}) collective-permute-start(f32[2,12,384]{2,1,0:T(8,128)S(1)} %slice.40), channel_id=1, source_target_pairs={{0,240},{16,0},{32,16},{48,32},{64,48},{80,64},{96,80},{112,96},{1... | collective-permute-start | bytes 110600 | tf_op jit(solution)/shard_map/ppermute | solution.py:21
  16.2 4.8 %collective-permute-start.1 = (f32[12,384]{1,0:T(8,128)S(1)}, f32[12,384]{1,0:T(8,128)S(1)}, u32[]{:S(2)}, u32[]{:S(2)}) collective-permute-start(f32[12,384]{1,0:T(8,128)S(1)} %slice_bitcast_fusion.4), channel_id=1, source_target_pairs={{0,15},{1,0},{2,1},{3,2},{4,3},{5,4},{6,5},{7,6},{8,7},{9,8},{10,9... | collective-permute-start | bytes 55304 | tf_op jit(solution)/shard_map/ppermute | solution.py:21
  26.4 16.9 %all-to-all-start.1 = ((f32[8,48,128]{2,1,0:T(8,128)}), f32[8,48,128]{2,1,0:T(8,128)S(1)}, u32[]{:S(2)}, u32[]{:S(2)}) async-start(f32[8,48,128]{2,1,0:T(8,128)} %get-tuple-element.58), calls=%async_computation.1 | async-start | bytes 393216 | tf_op jit(solution)/shard_map/all_to_all | solution.py:27
  34.6 23.7 %copy-start.7 = (f32[2,128,256]{2,1,0:T(8,128)S(1)}, f32[2,128,256]{2,1,0:T(8,128)}, u32[]{:S(2)}) copy-start(f32[2,128,256]{2,1,0:T(8,128)} %constant.29.clone) | copy-start | bytes 786436
  34.6 15.2 %collective-permute-start.3 = (f32[2,384,128]{2,1,0:T(8,128)}, f32[2,384,128]{2,1,0:T(8,128)S(1)}, u32[]{:S(2)}, u32[]{:S(2)}) collective-permute-start(f32[2,384,128]{2,1,0:T(8,128)} %get-tuple-element.60.refs_0_.refs_6_), channel_id=1, source_target_pairs={{0,16},{16,32},{32,48},{48,64},{64,80},{80,96},{96,112},{112,128},... | collective-permute-start | bytes 1179656 | tf_op jit(solution)/shard_map/ppermute | solution.py:21
  43.2 4.3 %collective-permute-start.2 = (f32[8,48,128]{2,1,0:T(8,128)S(1)}, f32[8,48,128]{2,1,0:T(8,128)S(1)}, u32[]{:S(2)}, u32[]{:S(2)}) collective-permute-start(f32[8,48,128]{2,1,0:T(8,128)S(1)} %all-to-all-done.1.refs_2_), channel_id=1, source_target_pairs={{0,1},{1,0},{2,3},{3,2},{4,5},{5,4},{6,7},{7,6},{8,9},{9,8},{10,11... | collective-permute-start | bytes 589832 | tf_op jit(solution)/shard_map/ppermute | solution.py:30
  46.4 3.3 %collective-permute-start.4 = (f32[384,128]{1,0:T(8,128)}, f32[384,128]{1,0:T(8,128)S(1)}, u32[]{:S(2)}, u32[]{:S(2)}) collective-permute-start(f32[384,128]{1,0:T(8,128)} %get-tuple-element.61.refs_2_.refs_8_), channel_id=1, source_target_pairs={{0,1},{1,2},{2,3},{3,4},{4,5},{5,6},{6,7},{7,8},{8,9},{9,10},{10,1... | collective-permute-start | bytes 589832 | tf_op jit(solution)/shard_map/ppermute | solution.py:21
  49.8 14.4 %all-to-all-start.2 = ((f32[8,96,128]{2,1,0:T(8,128)}), f32[8,96,128]{2,1,0:T(8,128)S(1)}, u32[]{:S(2)}, u32[]{:S(2)}) async-start(f32[8,96,128]{2,1,0:T(8,128)} %shard_map.106), calls=%async_computation.2 | async-start | bytes 786432 | tf_op jit(solution)/shard_map/all_to_all | solution.py:27
  53.3 10.8 %collective-permute-start.6 = (f32[2,8,16,128]{3,2,1,0:T(8,128)S(1)}, f32[2,8,16,128]{3,2,1,0:T(8,128)S(1)}, u32[]{:S(2)}, u32[]{:S(2)}) collective-permute-start(f32[2,8,16,128]{3,2,1,0:T(8,128)S(1)} %pad_maximum_fusion.1), channel_id=1, source_target_pairs={{0,16},{16,32},{32,48},{48,64},{64,80},{80,96},{96,112},{112,128},... | collective-permute-start | bytes 393224 | tf_op jit(solution)/shard_map/ppermute | solution.py:21
  54.2 9.9 %collective-permute-start.5 = (f32[2,8,16,128]{3,2,1,0:T(8,128)S(1)}, f32[2,8,16,128]{3,2,1,0:T(8,128)S(1)}, u32[]{:S(2)}, u32[]{:S(2)}) collective-permute-start(f32[2,8,16,128]{3,2,1,0:T(8,128)S(1)} %pad_maximum_fusion), channel_id=1, source_target_pairs={{0,240},{16,0},{32,16},{48,32},{64,48},{80,64},{96,80},{112,96},{1... | collective-permute-start | bytes 393224 | tf_op jit(solution)/shard_map/ppermute | solution.py:21
  64.2 9.4 %collective-permute-start.7 = (f32[8,96,128]{2,1,0:T(8,128)S(1)}, f32[8,96,128]{2,1,0:T(8,128)S(1)}, u32[]{:S(2)}, u32[]{:S(2)}) collective-permute-start(f32[8,96,128]{2,1,0:T(8,128)S(1)} %all-to-all-done.2.refs_2_), channel_id=1, source_target_pairs={{0,1},{1,0},{2,3},{3,2},{4,5},{5,4},{6,7},{7,6},{8,9},{9,8},{10,11... | collective-permute-start | bytes 1179656 | tf_op jit(solution)/shard_map/ppermute | solution.py:30
  68.9 19.7 %collective-permute-start.8 = (f32[2,384,128]{2,1,0:T(8,128)}, f32[2,384,128]{2,1,0:T(8,128)S(1)}, u32[]{:S(2)}, u32[]{:S(2)}) collective-permute-start(f32[2,384,128]{2,1,0:T(8,128)} %get-tuple-element.73), channel_id=1, source_target_pairs={{0,240},{16,0},{32,16},{48,32},{64,48},{80,64},{96,80},{112,96},{1... | collective-permute-start | bytes 1179656 | tf_op jit(solution)/shard_map/ppermute | solution.py:21
  73.5 8.3 %copy-start.9 = (f32[384,128]{1,0:T(8,128)S(1)}, f32[384,128]{1,0:T(8,128)}, u32[]{:S(2)}) copy-start(f32[384,128]{1,0:T(8,128)} %get-tuple-element.74) | copy-start | bytes 589828
  78.1 13.2 %all-to-all-start.3 = ((f32[16,48,128]{2,1,0:T(8,128)}), f32[16,48,128]{2,1,0:T(8,128)S(1)}, u32[]{:S(2)}, u32[]{:S(2)}) async-start(f32[16,48,128]{2,1,0:T(8,128)} %shard_map.109), calls=%async_computation.3 | async-start | bytes 786432 | tf_op jit(solution)/shard_map/all_to_all | solution.py:654
  81.8 6.7 %collective-permute-start.9 = (f32[384,128]{1,0:T(8,128)S(1)}, f32[384,128]{1,0:T(8,128)S(1)}, u32[]{:S(2)}, u32[]{:S(2)}) collective-permute-start(f32[384,128]{1,0:T(8,128)S(1)} %copy-done.9), channel_id=1, source_target_pairs={{0,15},{1,0},{2,1},{3,2},{4,3},{5,4},{6,5},{7,6},{8,7},{9,8},{10,9... | collective-permute-start | bytes 589832 | tf_op jit(solution)/shard_map/ppermute | solution.py:21
  91.2 7.8 %copy-start.3 = (f32[256,128]{1,0:T(8,128)S(1)}, f32[256,128]{1,0:T(8,128)}, u32[]{:S(2)}) copy-start(f32[256,128]{1,0:T(8,128)} %shard_map.108.refs_1_.refs_2_) | copy-start | bytes 393220
  95.0 19.0 %all-to-all-start.4 = ((f32[8,48,128]{2,1,0:T(8,128)}), f32[8,48,128]{2,1,0:T(8,128)S(1)}, u32[]{:S(2)}, u32[]{:S(2)}) async-start(f32[8,48,128]{2,1,0:T(8,128)} %get-tuple-element.86), calls=%async_computation.4 | async-start | bytes 393216 | tf_op jit(solution)/shard_map/all_to_all | solution.py:27
  98.7 18.0 %collective-permute-start.10 = (f32[2,384,128]{2,1,0:T(8,128)}, f32[2,384,128]{2,1,0:T(8,128)S(1)}, u32[]{:S(2)}, u32[]{:S(2)}) collective-permute-start(f32[2,384,128]{2,1,0:T(8,128)} %get-tuple-element.80.refs_0_.refs_6_.refs_9_), channel_id=1, source_target_pairs={{0,16},{16,32},{32,48},{48,64},{64,80},{80,96},{96,112},{112,128},... | collective-permute-start | bytes 1179656 | tf_op jit(solution)/shard_map/ppermute | solution.py:21
  99.0 15.0 %collective-permute-start.14 = (f32[256,128]{1,0:T(8,128)S(1)}, f32[256,128]{1,0:T(8,128)S(1)}, u32[]{:S(2)}, u32[]{:S(2)}) collective-permute-start(f32[256,128]{1,0:T(8,128)S(1)} %copy-done.3), channel_id=1, source_target_pairs={{0,16},{16,32},{32,48},{48,64},{64,80},{80,96},{96,112},{112,128},... | collective-permute-start | bytes 393224 | tf_op jit(solution)/shard_map/ppermute | solution.py:21
  99.7 14.3 %collective-permute-start.15 = (f32[256,128]{1,0:T(8,128)S(1)}, f32[256,128]{1,0:T(8,128)S(1)}, u32[]{:S(2)}, u32[]{:S(2)}) collective-permute-start(f32[256,128]{1,0:T(8,128)S(1)} %copy-done.3), channel_id=1, source_target_pairs={{0,240},{16,0},{32,16},{48,32},{64,48},{80,64},{96,80},{112,96},{1... | collective-permute-start | bytes 393224 | tf_op jit(solution)/shard_map/ppermute | solution.py:21
  103.8 12.9 %collective-permute-start.11 = (f32[384,128]{1,0:T(8,128)}, f32[384,128]{1,0:T(8,128)S(1)}, u32[]{:S(2)}, u32[]{:S(2)}) collective-permute-start(f32[384,128]{1,0:T(8,128)} %get-tuple-element.82.refs_2_.refs_8_.refs_11_), channel_id=1, source_target_pairs={{0,1},{1,2},{2,3},{3,4},{4,5},{5,6},{6,7},{7,8},{8,9},{9,10},{10,1... | collective-permute-start | bytes 589832 | tf_op jit(solution)/shard_map/ppermute | solution.py:21
  114.0 7.3 %copy-start.4 = (f32[256,128]{1,0:T(8,128)}, f32[256,128]{1,0:T(8,128)S(1)}, u32[]{:S(2)}) copy-start(f32[256,128]{1,0:T(8,128)S(1)} %collective-permute-done.14.refs_1_) | copy-start | bytes 393220
  114.0 7.3 %copy-start.5 = (f32[256,128]{1,0:T(8,128)}, f32[256,128]{1,0:T(8,128)S(1)}, u32[]{:S(2)}) copy-start(f32[256,128]{1,0:T(8,128)S(1)} %collective-permute-done.15.refs_3_) | copy-start | bytes 393220
  114.0 7.4 %collective-permute-start.16 = (f32[8,48,128]{2,1,0:T(8,128)S(1)}, f32[8,48,128]{2,1,0:T(8,128)S(1)}, u32[]{:S(2)}, u32[]{:S(2)}) collective-permute-start(f32[8,48,128]{2,1,0:T(8,128)S(1)} %all-to-all-done.4.refs_4_), channel_id=1, source_target_pairs={{0,1},{1,0},{2,3},{3,2},{4,5},{5,4},{6,7},{7,6},{8,9},{9,8},{10,11... | collective-permute-start | bytes 589832 | tf_op jit(solution)/shard_map/ppermute | solution.py:30
  121.3 12.2 %collective-permute-start.12 = (f32[2,384,128]{2,1,0:T(8,128)}, f32[2,384,128]{2,1,0:T(8,128)S(1)}, u32[]{:S(2)}, u32[]{:S(2)}) collective-permute-start(f32[2,384,128]{2,1,0:T(8,128)} %get-tuple-element.84), channel_id=1, source_target_pairs={{0,240},{16,0},{32,16},{48,32},{64,48},{80,64},{96,80},{112,96},{1... | collective-permute-start | bytes 1179656 | tf_op jit(solution)/shard_map/ppermute | solution.py:21
  124.3 13.5 %all-to-all-start.5 = ((f32[16,48,128]{2,1,0:T(8,128)}), f32[16,48,128]{2,1,0:T(8,128)S(1)}, u32[]{:S(2)}, u32[]{:S(2)}) async-start(f32[16,48,128]{2,1,0:T(8,128)} %shard_map.114), calls=%async_computation.5 | async-start | bytes 786432 | tf_op jit(solution)/shard_map/all_to_all | solution.py:661
  127.9 5.6 %collective-permute-start.13 = (f32[384,128]{1,0:T(8,128)}, f32[384,128]{1,0:T(8,128)S(1)}, u32[]{:S(2)}, u32[]{:S(2)}) collective-permute-start(f32[384,128]{1,0:T(8,128)} %get-tuple-element.85), channel_id=1, source_target_pairs={{0,15},{1,0},{2,1},{3,2},{4,3},{5,4},{6,5},{7,6},{8,7},{9,8},{10,9... | collective-permute-start | bytes 589832 | tf_op jit(solution)/shard_map/ppermute | solution.py:21
  141.7 15.1 %all-to-all-start.6 = ((f32[8,48,128]{2,1,0:T(8,128)}), f32[8,48,128]{2,1,0:T(8,128)S(1)}, u32[]{:S(2)}, u32[]{:S(2)}) async-start(f32[8,48,128]{2,1,0:T(8,128)} %get-tuple-element.91), calls=%async_computation.6 | async-start | bytes 393216 | tf_op jit(solution)/shard_map/all_to_all | solution.py:27
  148.3 12.7 %collective-permute-start.17 = (f32[2,384,128]{2,1,0:T(8,128)}, f32[2,384,128]{2,1,0:T(8,128)S(1)}, u32[]{:S(2)}, u32[]{:S(2)}) collective-permute-start(f32[2,384,128]{2,1,0:T(8,128)} %get-tuple-element.92.refs_0_.refs_12_), channel_id=1, source_target_pairs={{0,16},{16,32},{32,48},{48,64},{64,80},{80,96},{96,112},{112,128},... | collective-permute-start | bytes 1179656 | tf_op jit(solution)/shard_map/ppermute | solution.py:21
  148.6 11.9 %collective-permute-start.18 = (f32[384,128]{1,0:T(8,128)}, f32[384,128]{1,0:T(8,128)S(1)}, u32[]{:S(2)}, u32[]{:S(2)}) collective-permute-start(f32[384,128]{1,0:T(8,128)} %get-tuple-element.94.refs_2_.refs_14_), channel_id=1, source_target_pairs={{0,1},{1,2},{2,3},{3,4},{4,5},{5,6},{6,7},{7,8},{8,9},{9,10},{10,1... | collective-permute-start | bytes 589832 | tf_op jit(solution)/shard_map/ppermute | solution.py:21
  156.7 8.9 %collective-permute-start.21 = (f32[8,48,128]{2,1,0:T(8,128)S(1)}, f32[8,48,128]{2,1,0:T(8,128)S(1)}, u32[]{:S(2)}, u32[]{:S(2)}) collective-permute-start(f32[8,48,128]{2,1,0:T(8,128)S(1)} %all-to-all-done.6.refs_4_), channel_id=1, source_target_pairs={{0,1},{1,0},{2,3},{3,2},{4,5},{5,4},{6,7},{7,6},{8,9},{9,8},{10,11... | collective-permute-start | bytes 589832 | tf_op jit(solution)/shard_map/ppermute | solution.py:30
  168.6 13.2 %all-to-all-start.7 = ((f32[16,48,128]{2,1,0:T(8,128)}), f32[16,48,128]{2,1,0:T(8,128)S(1)}, u32[]{:S(2)}, u32[]{:S(2)}) async-start(f32[16,48,128]{2,1,0:T(8,128)} %shard_map.118), calls=%async_computation.7 | async-start | bytes 786432 | tf_op jit(solution)/shard_map/all_to_all | solution.py:661
  172.2 23.7 %copy-start.10 = (f32[384,128]{1,0:T(8,128)S(1)}, f32[384,128]{1,0:T(8,128)}, u32[]{:S(2)}) copy-start(f32[384,128]{1,0:T(8,128)} %get-tuple-element.101) | copy-start | bytes 589828
  172.2 30.3 %collective-permute-start.19 = (f32[2,384,128]{2,1,0:T(8,128)}, f32[2,384,128]{2,1,0:T(8,128)S(1)}, u32[]{:S(2)}, u32[]{:S(2)}) collective-permute-start(f32[2,384,128]{2,1,0:T(8,128)} %get-tuple-element.100), channel_id=1, source_target_pairs={{0,240},{16,0},{32,16},{48,32},{64,48},{80,64},{96,80},{112,96},{1... | collective-permute-start | bytes 1179656 | tf_op jit(solution)/shard_map/ppermute | solution.py:21
  183.2 25.5 %all-to-all-start.8 = ((f32[256,1,128]{2,1,0:T(1,128)}), f32[256,1,128]{2,1,0:T(1,128)S(1)}, u32[]{:S(2)}, u32[]{:S(2)}) async-start(f32[256,1,128]{2,1,0:T(1,128)} %bitcast.46), calls=%async_computation.8 | async-start | bytes 262144 | tf_op jit(solution)/shard_map/all_to_all | solution.py:678
  195.8 6.6 %collective-permute-start.20 = (f32[384,128]{1,0:T(8,128)S(1)}, f32[384,128]{1,0:T(8,128)S(1)}, u32[]{:S(2)}, u32[]{:S(2)}) collective-permute-start(f32[384,128]{1,0:T(8,128)S(1)} %copy-done.10), channel_id=1, source_target_pairs={{0,15},{1,0},{2,1},{3,2},{4,3},{5,4},{6,5},{7,6},{8,7},{9,8},{10,9... | collective-permute-start | bytes 589832 | tf_op jit(solution)/shard_map/ppermute | solution.py:21

commit v6 on v5

--- a/solution.py
+++ b/solution.py
@@ -661,7 +661,7 @@
         return lax.all_to_all(send, "sx", 0, 0, tiled=True)
 
     west, below = halo(w1)
-    same, other, (below_part, beyond_part) = along_sy(message, (below_part, beyond_part))
+    same, other = along_sy(message)
     given, back_east, back_north = give(w1, west, below)
     got = coarse_solve(same, other)
     (kept,) = keep(given)

time: 214 us -> 210 us (0.981)
  waiting for transfers between devices: 39.6 us -> 34.4 us
    ppermute x18, waiting for transfers between devices: 15.8 us -> 8.44 us  [shifted(): lax.ppermute(array, axis, [(i, (i + by) % count) for i in range(count)])]
    all_to_all x4, waiting for transfers between devices: 12.2 us -> 16.1 us  [along_sy(): lax.all_to_all(copies, 'sy', 0, 0, tiled=True, axis_index_groups=groups)]
    all_to_all x4, starting transfers between devices: 22.1 us -> 18.8 us  [along_sy(): lax.all_to_all(copies, 'sy', 0, 0, tiled=True, axis_index_groups=groups)]
  transfers between devices with their start and end apart: 31 -> 31, of which waited for: 13 -> 11; matrix products, arithmetic and copies ran while one was open for 1% -> 1% of each run, Pallas kernels for 23% -> 23%
where the time goes in v6:
time: 210 us; the launch traced here: 209 us
  starting transfers between devices  106 us (50%)
  Pallas kernels  64.6 us (31%)
  waiting for transfers between devices  34.4 us (16%)
  local copies, waits for them, and re-layouts  2.93 us (1%)
    pallas_call x18, Pallas kernels, kernel_call(): pl.pallas_call(wrapped, in_specs=[spec(k) for k in range(len(arrays))], o...  64.6 us
    ppermute x18, starting transfers between devices, shifted(): lax.ppermute(array, axis, [(i, (i + by) % count) for i in range(count)])  39.1 us
    all_to_all x4, starting transfers between devices, along_sy(): lax.all_to_all(copies, 'sy', 0, 0, tiled=True, axis_index_groups=groups)  18.8 us
    all_to_all x4, waiting for transfers between devices, along_sy(): lax.all_to_all(copies, 'sy', 0, 0, tiled=True, axis_index_groups=groups)  16.1 us
    ppermute x4, starting transfers between devices, along_sy(): other = lax.ppermute(same, 'sy', [(i, i ^ 1) for i in range(count)])  15.9 us
    all_to_all x1, starting transfers between devices, local(): lax.all_to_all(last.reshape(gx * gy, 1, cases), ('sx', 'sy'), 0, 0, tiled...  12.2 us
    ppermute x18, waiting for transfers between devices, shifted(): lax.ppermute(array, axis, [(i, (i + by) % count) for i in range(count)])  8.44 us
    all_to_all x2, starting transfers between devices, coarse_solve(): return lax.all_to_all(send, 'sx', 0, 0, tiled=True)  8.39 us
  transfers between devices with their start and end apart: 31, of which 11 were waited for; matrix products, arithmetic and copies ran while one was open for 1% of the time, Pallas kernels for 23%

profile of v6, /device:TPU:1, one launch (start us, length us, event | category | flops | bytes accessed | tf_op | source)
XLA Modules:
  0.0 209.1 jit_solution(11830642262464845332)
XLA Ops:
  1.4 2.4 %shard_map.105 = f32[16,96,128]{2,1,0:T(8,128)} custom-call(s32[2]{0:T(128)S(1)} %pad_add_fusion.refs_0_.refs_1_, s32[2,4]{1,0:T(2,128)S(1)} %bitcast.35, f32[96,96]{1,0:T(8,128)} %refs_2_.1), custom_call_target="tpu_custom_call" | custom-call | flops 3293344 | bytes 823336 | tf_op jit(solution)/shard_map/pallas_call | solution.py:110
  3.8 7.6 %all-to-all-start = ((f32[16,96,128]{2,1,0:T(8,128)}), f32[16,96,128]{2,1,0:T(8,128)S(1)}, u32[]{:S(2)}, u32[]{:S(2)}) async-start(f32[16,96,128]{2,1,0:T(8,128)} %shard_map.105), calls=%async_computation | async-start | bytes 1572864 | tf_op jit(solution)/shard_map/all_to_all | solution.py:552
  11.4 4.8 %collective-permute-start = (f32[2,12,384]{2,1,0:T(8,128)S(1)}, f32[2,12,384]{2,1,0:T(8,128)S(1)}, u32[]{:S(2)}, u32[]{:S(2)}) collective-permute-start(f32[2,12,384]{2,1,0:T(8,128)S(1)} %slice.40), channel_id=1, source_target_pairs={{0,240},{16,0},{32,16},{48,32},{64,48},{80,64},{96,80},{112,96},{1... | collective-permute-start | bytes 110600 | tf_op jit(solution)/shard_map/ppermute | solution.py:21
  16.2 1.5 collective-permute-start.1
  18.3 2.7 %collective-permute-done.1.refs_6_ = f32[12,384]{1,0:T(8,128)S(1)} collective-permute-done((f32[12,384]{1,0:T(8,128)S(1)}, f32[12,384]{1,0:T(8,128)S(1)}, u32[]{:S(2)}, u32[]{:S(2)}) %collective-permute-start.1) | collective-permute-done | bytes 18464 | tf_op jit(solution)/shard_map/ppermute | solution.py:21
  22.3 4.0 %shard_map.104 = (f32[4,384,128]{2,1,0:T(8,128)}, f32[2,384,128]{2,1,0:T(8,128)}, f32[384,128]{1,0:T(8,128)}, f32[384,128]{1,0:T(8,128)}, f32[4,384,128]{2,1,0:T...) custom-call(s32[2,2]{1,0:T(2,128)S(1)} %bitcast.37, s32[2,4]{1,0:T(2,128)S(1)} %bitcast.36, ...), custom_call_target="tpu_custom_call" | custom-call | flops 92307648 | bytes 23076912 | tf_op jit(solution)/shard_map/pallas_call | solution.py:110
  26.4 8.2 %all-to-all-start.1 = ((f32[8,48,128]{2,1,0:T(8,128)}), f32[8,48,128]{2,1,0:T(8,128)S(1)}, u32[]{:S(2)}, u32[]{:S(2)}) async-start(f32[8,48,128]{2,1,0:T(8,128)} %get-tuple-element.55), calls=%async_computation.1 | async-start | bytes 393216 | tf_op jit(solution)/shard_map/all_to_all | solution.py:27
  35.9 7.3 %all-to-all-done.1.refs_2_ = f32[8,48,128]{2,1,0:T(8,128)S(1)} async-done(((f32[8,48,128]{2,1,0:T(8,128)}), f32[8,48,128]{2,1,0:T(8,128)S(1)}, u32[]{:S(2)}, u32[]{:S(2)}) %all-to-all-start.1) | async-done | bytes 196640 | tf_op jit(solution)/shard_map/all_to_all | solution.py:27
  43.2 3.2 %collective-permute-start.2 = (f32[8,48,128]{2,1,0:T(8,128)S(1)}, f32[8,48,128]{2,1,0:T(8,128)S(1)}, u32[]{:S(2)}, u32[]{:S(2)}) collective-permute-start(f32[8,48,128]{2,1,0:T(8,128)S(1)} %all-to-all-done.1.refs_2_), channel_id=1, source_target_pairs={{0,1},{1,0},{2,3},{3,2},{4,5},{5,4},{6,7},{7,6},{8,9},{9,8},{10,11... | collective-permute-start | bytes 589832 | tf_op jit(solution)/shard_map/ppermute | solution.py:30
  47.5 2.2 %shard_map.106 = f32[8,96,128]{2,1,0:T(8,128)} custom-call(s32[16,128]{1,0:T(8,128)S(1)} %maximum_convert_fusion.refs_0_, s32[2]{0:T(128)S(1)} %pad_add_fusion.refs_0_.refs_1_, f32[16,96,128]{2,1,0:T(8,128)S(1)} %all-to-all-done.refs_2_), custom_call_target="tpu_custom_call" | custom-call | flops 4751392 | bytes 1187848 | tf_op jit(solution)/shard_map/pallas_call | solution.py:110
  49.8 3.5 %all-to-all-start.2 = ((f32[8,96,128]{2,1,0:T(8,128)}), f32[8,96,128]{2,1,0:T(8,128)S(1)}, u32[]{:S(2)}, u32[]{:S(2)}) async-start(f32[8,96,128]{2,1,0:T(8,128)} %shard_map.106), calls=%async_computation.2 | async-start | bytes 786432 | tf_op jit(solution)/shard_map/all_to_all | solution.py:27
  54.2 4.0 %collective-permute-start.5 = (f32[2,8,16,128]{3,2,1,0:T(8,128)S(1)}, f32[2,8,16,128]{3,2,1,0:T(8,128)S(1)}, u32[]{:S(2)}, u32[]{:S(2)}) collective-permute-start(f32[2,8,16,128]{3,2,1,0:T(8,128)S(1)} %pad_maximum_fusion), channel_id=1, source_target_pairs={{0,240},{16,0},{32,16},{48,32},{64,48},{80,64},{96,80},{112,96},{1... | collective-permute-start | bytes 393224 | tf_op jit(solution)/shard_map/ppermute | solution.py:21
  58.9 5.2 %shard_map.107 = (f32[2,384,128]{2,1,0:T(8,128)}, f32[384,128]{1,0:T(8,128)}, bf16[2,1536,256]{2,1,0:T(8,128)(2,1)}) custom-call(f32[2,384,128]{2,1,0:T(8,128)} %get-tuple-element.57.refs_0_.refs_6_, f32[384,128]{1,0:T(8,128)} %get-tuple-element.60.refs_1_.refs_7_, f32[384,128]{1,0:T(8,128)} %get-tuple-element.58.refs_2_.refs_8_, ...), custom_call_target="tpu_custom_call" | custom-call | flops 95944704 | bytes 23986176 | tf_op jit(solution)/shard_map/pallas_call | solution.py:110
  64.2 4.7 %collective-permute-start.7 = (f32[8,96,128]{2,1,0:T(8,128)S(1)}, f32[8,96,128]{2,1,0:T(8,128)S(1)}, u32[]{:S(2)}, u32[]{:S(2)}) collective-permute-start(f32[8,96,128]{2,1,0:T(8,128)S(1)} %all-to-all-done.2.refs_2_), channel_id=1, source_target_pairs={{0,1},{1,0},{2,3},{3,2},{4,5},{5,4},{6,7},{7,6},{8,9},{9,8},{10,11... | collective-permute-start | bytes 1179656 | tf_op jit(solution)/shard_map/ppermute | solution.py:30
  68.9 4.4 %collective-permute-start.8 = (f32[2,384,128]{2,1,0:T(8,128)}, f32[2,384,128]{2,1,0:T(8,128)S(1)}, u32[]{:S(2)}, u32[]{:S(2)}) collective-permute-start(f32[2,384,128]{2,1,0:T(8,128)} %get-tuple-element.70), channel_id=1, source_target_pairs={{0,240},{16,0},{32,16},{48,32},{64,48},{80,64},{96,80},{112,96},{1... | collective-permute-start | bytes 1179656 | tf_op jit(solution)/shard_map/ppermute | solution.py:21
  73.6 2.4 %shard_map.108.refs_1_.refs_2_ = f32[256,128]{1,0:T(8,128)} custom-call(s32[16,128]{1,0:T(8,128)S(1)} %maximum_convert_fusion.1.refs_0_, s32[2]{0:T(128)S(1)} %pad_add_fusion.refs_0_.refs_1_, f32[8,96,128]{2,1,0:T(8,128)S(1)} %all-to-all-done.2.refs_2_, f32[8,96,128]{2,1,0:T(8,128)S(1)} %collective-permute-done.7.refs_3_), custom_call_target="tpu_custom_call" | custom-call | flops 3702816 | bytes 925704 | tf_op jit(solution)/shard_map/pallas_call | solution.py:110
  76.0 2.1 %shard_map.109 = f32[16,48,128]{2,1,0:T(8,128)} custom-call(f32[128,256]{1,0:T(8,128)} %dynamic-slice_bitcast_fusion.refs_0_, f32[256,128]{1,0:T(8,128)} %shard_map.108.refs_1_.refs_2_, f32[8,48,128]{2,1,0:T(8,128)S(1)} %all-to-all-done.1.refs_2_, f32[8,48,128]{2,1,0:T(8,128)S(1)} %collective-permute-done.2.refs_3_, ...), custom_call_target="tpu_custom_call" | custom-call | flops 5242880 | bytes 1310720 | tf_op jit(solution)/shard_map/pallas_call | solution.py:110
  78.1 3.7 %all-to-all-start.3 = ((f32[16,48,128]{2,1,0:T(8,128)}), f32[16,48,128]{2,1,0:T(8,128)S(1)}, u32[]{:S(2)}, u32[]{:S(2)}) async-start(f32[16,48,128]{2,1,0:T(8,128)} %shard_map.109), calls=%async_computation.3 | async-start | bytes 786432 | tf_op jit(solution)/shard_map/all_to_all | solution.py:654
  82.1 6.4 %shard_map.110.refs_0_ = f32[4,384,128]{2,1,0:T(8,128)S(1)} custom-call(bf16[2,1536,256]{2,1,0:T(8,128)(2,1)} %get-tuple-element.69.refs_0_, bf16[8,384,1536]{2,1,0:T(8,128)(2,1)} %bitcast.40), custom_call_target="tpu_custom_call" | custom-call | flops 91226112 | bytes 22806528 | tf_op jit(solution)/shard_map/pallas_call | solution.py:110
  88.5 2.7 %all-to-all-done.3.refs_3_ = f32[16,48,128]{2,1,0:T(8,128)S(1)} async-done(((f32[16,48,128]{2,1,0:T(8,128)}), f32[16,48,128]{2,1,0:T(8,128)S(1)}, u32[]{:S(2)}, u32[]{:S(2)}) %all-to-all-start.3) | async-done | bytes 393248 | tf_op jit(solution)/shard_map/all_to_all | solution.py:654
  91.2 3.7 %shard_map.111 = (f32[4,384,128]{2,1,0:T(8,128)}, f32[2,384,128]{2,1,0:T(8,128)}, f32[384,128]{1,0:T(8,128)}, f32[384,128]{1,0:T(8,128)}, f32[8,128]{1,0:T(8,128...) custom-call(f32[4,384,128]{2,1,0:T(8,128)S(1)} %shard_map.110.refs_0_, ...), custom_call_target="tpu_custom_call" | custom-call | flops 22937600 | bytes 5734400 | tf_op jit(solution)/shard_map/pallas_call | solution.py:110
  95.0 3.8 %all-to-all-start.4 = ((f32[8,48,128]{2,1,0:T(8,128)}), f32[8,48,128]{2,1,0:T(8,128)S(1)}, u32[]{:S(2)}, u32[]{:S(2)}) async-start(f32[8,48,128]{2,1,0:T(8,128)} %get-tuple-element.83), calls=%async_computation.4 | async-start | bytes 393216 | tf_op jit(solution)/shard_map/all_to_all | solution.py:27
  99.0 3.6 %collective-permute-start.11 = (f32[384,128]{1,0:T(8,128)}, f32[384,128]{1,0:T(8,128)S(1)}, u32[]{:S(2)}, u32[]{:S(2)}) collective-permute-start(f32[384,128]{1,0:T(8,128)} %get-tuple-element.79.refs_2_.refs_8_.refs_11_), channel_id=1, source_target_pairs={{0,1},{1,2},{2,3},{3,4},{4,5},{5,6},{6,7},{7,8},{8,9},{9,10},{10,1... | collective-permute-start | bytes 589832 | tf_op jit(solution)/shard_map/ppermute | solution.py:21
  102.6 4.7 %all-to-all-done.4.refs_4_ = f32[8,48,128]{2,1,0:T(8,128)S(1)} async-done(((f32[8,48,128]{2,1,0:T(8,128)}), f32[8,48,128]{2,1,0:T(8,128)S(1)}, u32[]{:S(2)}, u32[]{:S(2)}) %all-to-all-start.4) | async-done | bytes 196640 | tf_op jit(solution)/shard_map/all_to_all | solution.py:27
  107.3 3.6 %collective-permute-start.16 = (f32[8,48,128]{2,1,0:T(8,128)S(1)}, f32[8,48,128]{2,1,0:T(8,128)S(1)}, u32[]{:S(2)}, u32[]{:S(2)}) collective-permute-start(f32[8,48,128]{2,1,0:T(8,128)S(1)} %all-to-all-done.4.refs_4_), channel_id=1, source_target_pairs={{0,1},{1,0},{2,3},{3,2},{4,5},{5,4},{6,7},{7,6},{8,9},{9,8},{10,11... | collective-permute-start | bytes 589832 | tf_op jit(solution)/shard_map/ppermute | solution.py:30
  111.3 4.4 %collective-permute-start.15 = (f32[256,128]{1,0:T(8,128)S(1)}, f32[256,128]{1,0:T(8,128)S(1)}, u32[]{:S(2)}, u32[]{:S(2)}) collective-permute-start(f32[256,128]{1,0:T(8,128)S(1)} %copy-done.3), channel_id=1, source_target_pairs={{0,240},{16,0},{32,16},{48,32},{64,48},{80,64},{96,80},{112,96},{1... | collective-permute-start | bytes 393224 | tf_op jit(solution)/shard_map/ppermute | solution.py:21
  115.8 4.6 %shard_map.112 = (f32[2,384,128]{2,1,0:T(8,128)}, f32[384,128]{1,0:T(8,128)}, bf16[2,1536,256]{2,1,0:T(8,128)(2,1)S(1)}) custom-call(f32[2,384,128]{2,1,0:T(8,128)} %get-tuple-element.77.refs_0_.refs_6_.refs_9_, f32[384,128]{1,0:T(8,128)} %get-tuple-element.78.refs_1_.refs_7_.refs_10_, f32[384,128]{1,0:T(8,128)} %get-tuple-element.79.refs_2_.refs_8_.refs_11_, ...), custom_call_target="tpu_custom_call" | custom-call | flops 95944704 | bytes 23986176 | tf_op jit(solution)/shard_map/pallas_call | solution.py:110
  121.2 2.9 %shard_map.114 = f32[16,48,128]{2,1,0:T(8,128)} custom-call(f32[128,256]{1,0:T(8,128)} %dynamic-slice_bitcast_fusion.refs_0_, f32[256,128]{1,0:T(8,128)} %copy-done.4, f32[256,128]{1,0:T(8,128)} %shard_map.108.refs_1_.refs_2_, f32[256,128]{1,0:T(8,128)} %copy-done.5, f32[8,48,128]{2,1,0:T(8,128)S(1)} %all-to-all-done.4.refs_4_, ...), custom_call_target="tpu_custom_call" | custom-call | flops 5242880 | bytes 1310720 | tf_op jit(solution)/shard_map/pallas_call | solution.py:110
  124.1 4.8 %all-to-all-start.5 = ((f32[16,48,128]{2,1,0:T(8,128)}), f32[16,48,128]{2,1,0:T(8,128)S(1)}, u32[]{:S(2)}, u32[]{:S(2)}) async-start(f32[16,48,128]{2,1,0:T(8,128)} %shard_map.114), calls=%async_computation.5 | async-start | bytes 786432 | tf_op jit(solution)/shard_map/all_to_all | solution.py:661
  130.2 4.8 %shard_map.113.refs_0_ = f32[4,384,128]{2,1,0:T(8,128)S(1)} custom-call(bf16[2,1536,256]{2,1,0:T(8,128)(2,1)S(1)} %get-tuple-element.80.refs_0_, bf16[8,384,1536]{2,1,0:T(8,128)(2,1)} %bitcast.42), custom_call_target="tpu_custom_call" | custom-call | flops 91226112 | bytes 22806528 | tf_op jit(solution)/shard_map/pallas_call | solution.py:110
  135.1 2.5 %all-to-all-done.5.refs_3_ = f32[16,48,128]{2,1,0:T(8,128)S(1)} async-done(((f32[16,48,128]{2,1,0:T(8,128)}), f32[16,48,128]{2,1,0:T(8,128)S(1)}, u32[]{:S(2)}, u32[]{:S(2)}) %all-to-all-start.5) | async-done | bytes 393248 | tf_op jit(solution)/shard_map/all_to_all | solution.py:661
  137.6 3.9 %shard_map.115 = (f32[4,384,128]{2,1,0:T(8,128)}, f32[2,384,128]{2,1,0:T(8,128)}, f32[384,128]{1,0:T(8,128)}, f32[384,128]{1,0:T(8,128)}, f32[8,128]{1,0:T(8,128...) custom-call(f32[4,384,128]{2,1,0:T(8,128)S(1)} %shard_map.113.refs_0_, ...), custom_call_target="tpu_custom_call" | custom-call | flops 22953984 | bytes 5738496 | tf_op jit(solution)/shard_map/pallas_call | solution.py:110
  141.5 3.4 %all-to-all-start.6 = ((f32[8,48,128]{2,1,0:T(8,128)}), f32[8,48,128]{2,1,0:T(8,128)S(1)}, u32[]{:S(2)}, u32[]{:S(2)}) async-start(f32[8,48,128]{2,1,0:T(8,128)} %get-tuple-element.85), calls=%async_computation.6 | async-start | bytes 393216 | tf_op jit(solution)/shard_map/all_to_all | solution.py:27
  145.5 4.0 %collective-permute-start.18 = (f32[384,128]{1,0:T(8,128)}, f32[384,128]{1,0:T(8,128)S(1)}, u32[]{:S(2)}, u32[]{:S(2)}) collective-permute-start(f32[384,128]{1,0:T(8,128)} %get-tuple-element.88.refs_2_.refs_14_), channel_id=1, source_target_pairs={{0,1},{1,2},{2,3},{3,4},{4,5},{5,6},{6,7},{7,8},{8,9},{9,10},{10,1... | collective-permute-start | bytes 589832 | tf_op jit(solution)/shard_map/ppermute | solution.py:21
  149.4 4.0 %all-to-all-done.6.refs_4_ = f32[8,48,128]{2,1,0:T(8,128)S(1)} async-done(((f32[8,48,128]{2,1,0:T(8,128)}), f32[8,48,128]{2,1,0:T(8,128)S(1)}, u32[]{:S(2)}, u32[]{:S(2)}) %all-to-all-start.6) | async-done | bytes 196640 | tf_op jit(solution)/shard_map/all_to_all | solution.py:27
  153.5 4.4 %collective-permute-start.21 = (f32[8,48,128]{2,1,0:T(8,128)S(1)}, f32[8,48,128]{2,1,0:T(8,128)S(1)}, u32[]{:S(2)}, u32[]{:S(2)}) collective-permute-start(f32[8,48,128]{2,1,0:T(8,128)S(1)} %all-to-all-done.6.refs_4_), channel_id=1, source_target_pairs={{0,1},{1,0},{2,3},{3,2},{4,5},{5,4},{6,7},{7,6},{8,9},{9,8},{10,11... | collective-permute-start | bytes 589832 | tf_op jit(solution)/shard_map/ppermute | solution.py:30
  157.8 4.6 %shard_map.116 = (f32[2,384,128]{2,1,0:T(8,128)}, f32[384,128]{1,0:T(8,128)}, bf16[2,1536,256]{2,1,0:T(8,128)(2,1)S(1)}, f32[8,128]{1,0:T(8,128)S(1)}) custom-call(f32[2,384,128]{2,1,0:T(8,128)} %get-tuple-element.86.refs_0_.refs_12_, f32[384,128]{1,0:T(8,128)} %get-tuple-element.87.refs_1_.refs_13_, f32[384,128]{1,0:T(8,128)} %get-tuple-element.88.refs_2_.refs_14_, ...), custom_call_target="tpu_custom_call" | custom-call | flops 95961088 | bytes 23990272 | tf_op jit(solution)/shard_map/pallas_call | solution.py:110
  162.4 2.9 %shard_map.118 = f32[16,48,128]{2,1,0:T(8,128)} custom-call(f32[128,256]{1,0:T(8,128)} %dynamic-slice_bitcast_fusion.refs_0_, f32[256,128]{1,0:T(8,128)} %copy-done.4, f32[256,128]{1,0:T(8,128)} %shard_map.108.refs_1_.refs_2_, f32[256,128]{1,0:T(8,128)} %copy-done.5, f32[8,48,128]{2,1,0:T(8,128)S(1)} %all-to-all-done.6.refs_4_, ...), custom_call_target="tpu_custom_call" | custom-call | flops 5242880 | bytes 1310720 | tf_op jit(solution)/shard_map/pallas_call | solution.py:110
  165.3 3.6 %all-to-all-start.7 = ((f32[16,48,128]{2,1,0:T(8,128)}), f32[16,48,128]{2,1,0:T(8,128)S(1)}, u32[]{:S(2)}, u32[]{:S(2)}) async-start(f32[16,48,128]{2,1,0:T(8,128)} %shard_map.118), calls=%async_computation.7 | async-start | bytes 786432 | tf_op jit(solution)/shard_map/all_to_all | solution.py:661
  169.0 4.8 %collective-permute-start.19 = (f32[2,384,128]{2,1,0:T(8,128)}, f32[2,384,128]{2,1,0:T(8,128)S(1)}, u32[]{:S(2)}, u32[]{:S(2)}) collective-permute-start(f32[2,384,128]{2,1,0:T(8,128)} %get-tuple-element.94), channel_id=1, source_target_pairs={{0,240},{16,0},{32,16},{48,32},{64,48},{80,64},{96,80},{112,96},{1... | collective-permute-start | bytes 1179656 | tf_op jit(solution)/shard_map/ppermute | solution.py:21
  173.8 4.9 %shard_map.117 = (f32[4,384,128]{2,1,0:T(8,128)S(1)}, f32[8,128]{1,0:T(8,128)S(1)}) custom-call(bf16[2,1536,256]{2,1,0:T(8,128)(2,1)S(1)} %get-tuple-element.91.refs_0_, f32[8,128]{1,0:T(8,128)S(1)} %get-tuple-element.92.refs_1_, bf16[8,384,1536]{2,1,0:T(8,128)(2,1)} %bitcast.44), custom_call_target="tpu_custom_call" | custom-call | flops 91258880 | bytes 22814720 | tf_op jit(solution)/shard_map/pallas_call | solution.py:110
  178.6 1.4 shard_map.120
  180.1 12.2 %all-to-all-start.8 = ((f32[256,1,128]{2,1,0:T(1,128)}), f32[256,1,128]{2,1,0:T(1,128)S(1)}, u32[]{:S(2)}, u32[]{:S(2)}) async-start(f32[256,1,128]{2,1,0:T(1,128)} %bitcast.46), calls=%async_computation.8 | async-start | bytes 262144 | tf_op jit(solution)/shard_map/all_to_all | solution.py:678
  192.3 2.2 %collective-permute-start.20 = (f32[384,128]{1,0:T(8,128)S(1)}, f32[384,128]{1,0:T(8,128)S(1)}, u32[]{:S(2)}, u32[]{:S(2)}) collective-permute-start(f32[384,128]{1,0:T(8,128)S(1)} %copy-done.10), channel_id=1, source_target_pairs={{0,15},{1,0},{2,1},{3,2},{4,3},{5,4},{6,5},{7,6},{8,7},{9,8},{10,9... | collective-permute-start | bytes 589832 | tf_op jit(solution)/shard_map/ppermute | solution.py:21
  194.5 4.4 %collective-permute-done.20.refs_2_ = f32[384,128]{1,0:T(8,128)S(1)} collective-permute-done((f32[384,128]{1,0:T(8,128)S(1)}, f32[384,128]{1,0:T(8,128)S(1)}, u32[]{:S(2)}, u32[]{:S(2)}) %collective-permute-start.20) | collective-permute-done | bytes 196640 | tf_op jit(solution)/shard_map/ppermute | solution.py:21
  198.9 2.5 %shard_map.119 = (f32[4,384,128]{2,1,0:T(8,128)}, f32[8,128]{1,0:T(8,128)}) custom-call(f32[4,384,128]{2,1,0:T(8,128)S(1)} %get-tuple-element.93.refs_0_, f32[2,384,128]{2,1,0:T(8,128)S(1)} %collective-permute-done.19.refs_1_, f32[384,128]{1,0:T(8,128)S(1)} %collective-permute-done.20.refs_2_, f32[16,48,128]{2,1,0:T(8,128)S(1)} %all-to-all-done.7.refs_3_.refs_2_, ...), custom_call_target="tpu_custom_call" | custom-call | flops 15745024 | bytes 3936256 | tf_op jit(solution)/shard_map/pallas_call | solution.py:110
  201.4 3.7 %all-to-all-done.8 = f32[256,1,128]{2,1,0:T(1,128)S(1)} async-done(((f32[256,1,128]{2,1,0:T(1,128)}), f32[256,1,128]{2,1,0:T(1,128)S(1)}, u32[]{:S(2)}, u32[]{:S(2)}) %all-to-all-start.8) | async-done | bytes 131104 | tf_op jit(solution)/shard_map/all_to_all | solution.py:678
  205.2 3.8 %shard_map.121 = (f32[4,384,128]{2,1,0:T(8,128)}, f32[4,384,128]{2,1,0:T(8,128)}) custom-call(f32[8,128]{1,0:T(8,128)} %get-tuple-element.75.refs_9_.refs_0_, f32[8,128]{1,0:T(8,128)} %get-tuple-element.76.refs_1_, f32[8,128]{1,0:T(8,128)} %get-tuple-element.84.refs_2_, f32[8,128]{1,0:T(8,128)} %get-tuple-element.97.refs_3_, f32[256,128]{1,0:T(8,128)S(1)} %bitcast.34, ...), custom_call_target="tpu_custom_call" | custom-call | flops 28901376 | bytes 7225344 | tf_op jit(solution)/shard_map/pallas_call | solution.py:110
  (71 shorter events, 10.8 us)
Async XLA Ops:
  0.6 21.7 %copy-start.1 = (s32[1,2,4]{2,1,0:T(2,128)S(1)}, s32[1,2,4]{2,1,0:T(2,128)}, u32[]{:S(2)}) copy-start(s32[1,2,4]{2,1,0:T(2,128)} %param.12) | copy-start | bytes 100
  0.6 17.1 %copy-start.8 = (f32[1,2,2,384]{3,2,1,0:T(2,128)S(1)}, f32[1,2,2,384]{3,2,1,0:T(2,128)}, u32[]{:S(2)}) copy-start(f32[1,2,2,384]{3,2,1,0:T(2,128)} %param.10) | copy-start | bytes 18436
  0.7 21.7 %copy-start.2 = (s32[1,2,2]{2,1,0:T(2,128)S(1)}, s32[1,2,2]{2,1,0:T(2,128)}, u32[]{:S(2)}) copy-start(s32[1,2,2]{2,1,0:T(2,128)} %param.11) | copy-start | bytes 52
  0.7 0.7 copy-start
  1.4 10.0 %copy-start.6 = (bf16[1,2,12,1536]{3,1,2,0:T(2,128)(2,1)S(1)}, bf16[1,2,12,1536]{3,1,2,0:T(2,128)(2,1)}, u32[]{:S(2)}) copy-start(bf16[1,2,12,1536]{3,1,2,0:T(2,128)(2,1)} %param.14) | copy-start | bytes 221188
  3.8 22.6 %all-to-all-start = ((f32[16,96,128]{2,1,0:T(8,128)}), f32[16,96,128]{2,1,0:T(8,128)S(1)}, u32[]{:S(2)}, u32[]{:S(2)}) async-start(f32[16,96,128]{2,1,0:T(8,128)} %shard_map.105), calls=%async_computation | async-start | bytes 1572864 | tf_op jit(solution)/shard_map/all_to_all | solution.py:552
  11.4 10.9 %collective-permute-start = (f32[2,12,384]{2,1,0:T(8,128)S(1)}, f32[2,12,384]{2,1,0:T(8,128)S(1)}, u32[]{:S(2)}, u32[]{:S(2)}) collective-permute-start(f32[2,12,384]{2,1,0:T(8,128)S(1)} %slice.40), channel_id=1, source_target_pairs={{0,240},{16,0},{32,16},{48,32},{64,48},{80,64},{96,80},{112,96},{1... | collective-permute-start | bytes 110600 | tf_op jit(solution)/shard_map/ppermute | solution.py:21
  16.2 4.8 %collective-permute-start.1 = (f32[12,384]{1,0:T(8,128)S(1)}, f32[12,384]{1,0:T(8,128)S(1)}, u32[]{:S(2)}, u32[]{:S(2)}) collective-permute-start(f32[12,384]{1,0:T(8,128)S(1)} %slice_bitcast_fusion.4), channel_id=1, source_target_pairs={{0,15},{1,0},{2,1},{3,2},{4,3},{5,4},{6,5},{7,6},{8,7},{9,8},{10,9... | collective-permute-start | bytes 55304 | tf_op jit(solution)/shard_map/ppermute | solution.py:21
  26.4 16.9 %all-to-all-start.1 = ((f32[8,48,128]{2,1,0:T(8,128)}), f32[8,48,128]{2,1,0:T(8,128)S(1)}, u32[]{:S(2)}, u32[]{:S(2)}) async-start(f32[8,48,128]{2,1,0:T(8,128)} %get-tuple-element.55), calls=%async_computation.1 | async-start | bytes 393216 | tf_op jit(solution)/shard_map/all_to_all | solution.py:27
  34.6 23.7 %copy-start.7 = (f32[2,128,256]{2,1,0:T(8,128)S(1)}, f32[2,128,256]{2,1,0:T(8,128)}, u32[]{:S(2)}) copy-start(f32[2,128,256]{2,1,0:T(8,128)} %constant.29.clone) | copy-start | bytes 786436
  34.6 15.2 %collective-permute-start.3 = (f32[2,384,128]{2,1,0:T(8,128)}, f32[2,384,128]{2,1,0:T(8,128)S(1)}, u32[]{:S(2)}, u32[]{:S(2)}) collective-permute-start(f32[2,384,128]{2,1,0:T(8,128)} %get-tuple-element.57.refs_0_.refs_6_), channel_id=1, source_target_pairs={{0,16},{16,32},{32,48},{48,64},{64,80},{80,96},{96,112},{112,128},... | collective-permute-start | bytes 1179656 | tf_op jit(solution)/shard_map/ppermute | solution.py:21
  43.2 4.3 %collective-permute-start.2 = (f32[8,48,128]{2,1,0:T(8,128)S(1)}, f32[8,48,128]{2,1,0:T(8,128)S(1)}, u32[]{:S(2)}, u32[]{:S(2)}) collective-permute-start(f32[8,48,128]{2,1,0:T(8,128)S(1)} %all-to-all-done.1.refs_2_), channel_id=1, source_target_pairs={{0,1},{1,0},{2,3},{3,2},{4,5},{5,4},{6,7},{7,6},{8,9},{9,8},{10,11... | collective-permute-start | bytes 589832 | tf_op jit(solution)/shard_map/ppermute | solution.py:30
  46.4 3.3 %collective-permute-start.4 = (f32[384,128]{1,0:T(8,128)}, f32[384,128]{1,0:T(8,128)S(1)}, u32[]{:S(2)}, u32[]{:S(2)}) collective-permute-start(f32[384,128]{1,0:T(8,128)} %get-tuple-element.58.refs_2_.refs_8_), channel_id=1, source_target_pairs={{0,1},{1,2},{2,3},{3,4},{4,5},{5,6},{6,7},{7,8},{8,9},{9,10},{10,1... | collective-permute-start | bytes 589832 | tf_op jit(solution)/shard_map/ppermute | solution.py:21
  49.8 14.4 %all-to-all-start.2 = ((f32[8,96,128]{2,1,0:T(8,128)}), f32[8,96,128]{2,1,0:T(8,128)S(1)}, u32[]{:S(2)}, u32[]{:S(2)}) async-start(f32[8,96,128]{2,1,0:T(8,128)} %shard_map.106), calls=%async_computation.2 | async-start | bytes 786432 | tf_op jit(solution)/shard_map/all_to_all | solution.py:27
  53.3 10.8 %collective-permute-start.6 = (f32[2,8,16,128]{3,2,1,0:T(8,128)S(1)}, f32[2,8,16,128]{3,2,1,0:T(8,128)S(1)}, u32[]{:S(2)}, u32[]{:S(2)}) collective-permute-start(f32[2,8,16,128]{3,2,1,0:T(8,128)S(1)} %pad_maximum_fusion.1), channel_id=1, source_target_pairs={{0,16},{16,32},{32,48},{48,64},{64,80},{80,96},{96,112},{112,128},... | collective-permute-start | bytes 393224 | tf_op jit(solution)/shard_map/ppermute | solution.py:21
  54.2 9.9 %collective-permute-start.5 = (f32[2,8,16,128]{3,2,1,0:T(8,128)S(1)}, f32[2,8,16,128]{3,2,1,0:T(8,128)S(1)}, u32[]{:S(2)}, u32[]{:S(2)}) collective-permute-start(f32[2,8,16,128]{3,2,1,0:T(8,128)S(1)} %pad_maximum_fusion), channel_id=1, source_target_pairs={{0,240},{16,0},{32,16},{48,32},{64,48},{80,64},{96,80},{112,96},{1... | collective-permute-start | bytes 393224 | tf_op jit(solution)/shard_map/ppermute | solution.py:21
  64.2 9.4 %collective-permute-start.7 = (f32[8,96,128]{2,1,0:T(8,128)S(1)}, f32[8,96,128]{2,1,0:T(8,128)S(1)}, u32[]{:S(2)}, u32[]{:S(2)}) collective-permute-start(f32[8,96,128]{2,1,0:T(8,128)S(1)} %all-to-all-done.2.refs_2_), channel_id=1, source_target_pairs={{0,1},{1,0},{2,3},{3,2},{4,5},{5,4},{6,7},{7,6},{8,9},{9,8},{10,11... | collective-permute-start | bytes 1179656 | tf_op jit(solution)/shard_map/ppermute | solution.py:30
  68.9 19.7 %collective-permute-start.8 = (f32[2,384,128]{2,1,0:T(8,128)}, f32[2,384,128]{2,1,0:T(8,128)S(1)}, u32[]{:S(2)}, u32[]{:S(2)}) collective-permute-start(f32[2,384,128]{2,1,0:T(8,128)} %get-tuple-element.70), channel_id=1, source_target_pairs={{0,240},{16,0},{32,16},{48,32},{64,48},{80,64},{96,80},{112,96},{1... | collective-permute-start | bytes 1179656 | tf_op jit(solution)/shard_map/ppermute | solution.py:21
  73.5 8.3 %copy-start.9 = (f32[384,128]{1,0:T(8,128)S(1)}, f32[384,128]{1,0:T(8,128)}, u32[]{:S(2)}) copy-start(f32[384,128]{1,0:T(8,128)} %get-tuple-element.71) | copy-start | bytes 589828
  78.1 13.2 %all-to-all-start.3 = ((f32[16,48,128]{2,1,0:T(8,128)}), f32[16,48,128]{2,1,0:T(8,128)S(1)}, u32[]{:S(2)}, u32[]{:S(2)}) async-start(f32[16,48,128]{2,1,0:T(8,128)} %shard_map.109), calls=%async_computation.3 | async-start | bytes 786432 | tf_op jit(solution)/shard_map/all_to_all | solution.py:654
  81.8 6.7 %collective-permute-start.9 = (f32[384,128]{1,0:T(8,128)S(1)}, f32[384,128]{1,0:T(8,128)S(1)}, u32[]{:S(2)}, u32[]{:S(2)}) collective-permute-start(f32[384,128]{1,0:T(8,128)S(1)} %copy-done.9), channel_id=1, source_target_pairs={{0,15},{1,0},{2,1},{3,2},{4,3},{5,4},{6,5},{7,6},{8,7},{9,8},{10,9... | collective-permute-start | bytes 589832 | tf_op jit(solution)/shard_map/ppermute | solution.py:21
  91.2 19.7 %copy-start.3 = (f32[256,128]{1,0:T(8,128)S(1)}, f32[256,128]{1,0:T(8,128)}, u32[]{:S(2)}) copy-start(f32[256,128]{1,0:T(8,128)} %shard_map.108.refs_1_.refs_2_) | copy-start | bytes 393220
  95.0 12.4 %all-to-all-start.4 = ((f32[8,48,128]{2,1,0:T(8,128)}), f32[8,48,128]{2,1,0:T(8,128)S(1)}, u32[]{:S(2)}, u32[]{:S(2)}) async-start(f32[8,48,128]{2,1,0:T(8,128)} %get-tuple-element.83), calls=%async_computation.4 | async-start | bytes 393216 | tf_op jit(solution)/shard_map/all_to_all | solution.py:27
  98.7 17.0 %collective-permute-start.10 = (f32[2,384,128]{2,1,0:T(8,128)}, f32[2,384,128]{2,1,0:T(8,128)S(1)}, u32[]{:S(2)}, u32[]{:S(2)}) collective-permute-start(f32[2,384,128]{2,1,0:T(8,128)} %get-tuple-element.77.refs_0_.refs_6_.refs_9_), channel_id=1, source_target_pairs={{0,16},{16,32},{32,48},{48,64},{64,80},{80,96},{96,112},{112,128},... | collective-permute-start | bytes 1179656 | tf_op jit(solution)/shard_map/ppermute | solution.py:21
  99.0 16.8 %collective-permute-start.11 = (f32[384,128]{1,0:T(8,128)}, f32[384,128]{1,0:T(8,128)S(1)}, u32[]{:S(2)}, u32[]{:S(2)}) collective-permute-start(f32[384,128]{1,0:T(8,128)} %get-tuple-element.79.refs_2_.refs_8_.refs_11_), channel_id=1, source_target_pairs={{0,1},{1,2},{2,3},{3,4},{4,5},{5,6},{6,7},{7,8},{8,9},{9,10},{10,1... | collective-permute-start | bytes 589832 | tf_op jit(solution)/shard_map/ppermute | solution.py:21
  107.3 13.2 %collective-permute-start.16 = (f32[8,48,128]{2,1,0:T(8,128)S(1)}, f32[8,48,128]{2,1,0:T(8,128)S(1)}, u32[]{:S(2)}, u32[]{:S(2)}) collective-permute-start(f32[8,48,128]{2,1,0:T(8,128)S(1)} %all-to-all-done.4.refs_4_), channel_id=1, source_target_pairs={{0,1},{1,0},{2,3},{3,2},{4,5},{5,4},{6,7},{7,6},{8,9},{9,8},{10,11... | collective-permute-start | bytes 589832 | tf_op jit(solution)/shard_map/ppermute | solution.py:30
  111.0 9.5 %collective-permute-start.14 = (f32[256,128]{1,0:T(8,128)S(1)}, f32[256,128]{1,0:T(8,128)S(1)}, u32[]{:S(2)}, u32[]{:S(2)}) collective-permute-start(f32[256,128]{1,0:T(8,128)S(1)} %copy-done.3), channel_id=1, source_target_pairs={{0,16},{16,32},{32,48},{48,64},{64,80},{80,96},{96,112},{112,128},... | collective-permute-start | bytes 393224 | tf_op jit(solution)/shard_map/ppermute | solution.py:21
  111.3 9.1 %collective-permute-start.15 = (f32[256,128]{1,0:T(8,128)S(1)}, f32[256,128]{1,0:T(8,128)S(1)}, u32[]{:S(2)}, u32[]{:S(2)}) collective-permute-start(f32[256,128]{1,0:T(8,128)S(1)} %copy-done.3), channel_id=1, source_target_pairs={{0,240},{16,0},{32,16},{48,32},{64,48},{80,64},{96,80},{112,96},{1... | collective-permute-start | bytes 393224 | tf_op jit(solution)/shard_map/ppermute | solution.py:21
  120.4 14.7 %collective-permute-start.12 = (f32[2,384,128]{2,1,0:T(8,128)}, f32[2,384,128]{2,1,0:T(8,128)S(1)}, u32[]{:S(2)}, u32[]{:S(2)}) collective-permute-start(f32[2,384,128]{2,1,0:T(8,128)} %get-tuple-element.81), channel_id=1, source_target_pairs={{0,240},{16,0},{32,16},{48,32},{64,48},{80,64},{96,80},{112,96},{1... | collective-permute-start | bytes 1179656 | tf_op jit(solution)/shard_map/ppermute | solution.py:21
  120.5 0.7 copy-start.4
  120.5 0.7 copy-start.5
  124.1 13.5 %all-to-all-start.5 = ((f32[16,48,128]{2,1,0:T(8,128)}), f32[16,48,128]{2,1,0:T(8,128)S(1)}, u32[]{:S(2)}, u32[]{:S(2)}) async-start(f32[16,48,128]{2,1,0:T(8,128)} %shard_map.114), calls=%async_computation.5 | async-start | bytes 786432 | tf_op jit(solution)/shard_map/all_to_all | solution.py:661
  128.8 6.2 %collective-permute-start.13 = (f32[384,128]{1,0:T(8,128)}, f32[384,128]{1,0:T(8,128)S(1)}, u32[]{:S(2)}, u32[]{:S(2)}) collective-permute-start(f32[384,128]{1,0:T(8,128)} %get-tuple-element.82), channel_id=1, source_target_pairs={{0,15},{1,0},{2,1},{3,2},{4,3},{5,4},{6,5},{7,6},{8,7},{9,8},{10,9... | collective-permute-start | bytes 589832 | tf_op jit(solution)/shard_map/ppermute | solution.py:21
  141.5 12.0 %all-to-all-start.6 = ((f32[8,48,128]{2,1,0:T(8,128)}), f32[8,48,128]{2,1,0:T(8,128)S(1)}, u32[]{:S(2)}, u32[]{:S(2)}) async-start(f32[8,48,128]{2,1,0:T(8,128)} %get-tuple-element.85), calls=%async_computation.6 | async-start | bytes 393216 | tf_op jit(solution)/shard_map/all_to_all | solution.py:27
  144.9 13.0 %collective-permute-start.17 = (f32[2,384,128]{2,1,0:T(8,128)}, f32[2,384,128]{2,1,0:T(8,128)S(1)}, u32[]{:S(2)}, u32[]{:S(2)}) collective-permute-start(f32[2,384,128]{2,1,0:T(8,128)} %get-tuple-element.86.refs_0_.refs_12_), channel_id=1, source_target_pairs={{0,16},{16,32},{32,48},{48,64},{64,80},{80,96},{96,112},{112,128},... | collective-permute-start | bytes 1179656 | tf_op jit(solution)/shard_map/ppermute | solution.py:21
  145.5 12.3 %collective-permute-start.18 = (f32[384,128]{1,0:T(8,128)}, f32[384,128]{1,0:T(8,128)S(1)}, u32[]{:S(2)}, u32[]{:S(2)}) collective-permute-start(f32[384,128]{1,0:T(8,128)} %get-tuple-element.88.refs_2_.refs_14_), channel_id=1, source_target_pairs={{0,1},{1,2},{2,3},{3,4},{4,5},{5,6},{6,7},{7,8},{8,9},{9,10},{10,1... | collective-permute-start | bytes 589832 | tf_op jit(solution)/shard_map/ppermute | solution.py:21
  153.5 9.0 %collective-permute-start.21 = (f32[8,48,128]{2,1,0:T(8,128)S(1)}, f32[8,48,128]{2,1,0:T(8,128)S(1)}, u32[]{:S(2)}, u32[]{:S(2)}) collective-permute-start(f32[8,48,128]{2,1,0:T(8,128)S(1)} %all-to-all-done.6.refs_4_), channel_id=1, source_target_pairs={{0,1},{1,0},{2,3},{3,2},{4,5},{5,4},{6,7},{7,6},{8,9},{9,8},{10,11... | collective-permute-start | bytes 589832 | tf_op jit(solution)/shard_map/ppermute | solution.py:30
  165.3 13.3 %all-to-all-start.7 = ((f32[16,48,128]{2,1,0:T(8,128)}), f32[16,48,128]{2,1,0:T(8,128)S(1)}, u32[]{:S(2)}, u32[]{:S(2)}) async-start(f32[16,48,128]{2,1,0:T(8,128)} %shard_map.118), calls=%async_computation.7 | async-start | bytes 786432 | tf_op jit(solution)/shard_map/all_to_all | solution.py:661
  169.0 23.3 %copy-start.10 = (f32[384,128]{1,0:T(8,128)S(1)}, f32[384,128]{1,0:T(8,128)}, u32[]{:S(2)}) copy-start(f32[384,128]{1,0:T(8,128)} %get-tuple-element.95) | copy-start | bytes 589828
  169.0 29.9 %collective-permute-start.19 = (f32[2,384,128]{2,1,0:T(8,128)}, f32[2,384,128]{2,1,0:T(8,128)S(1)}, u32[]{:S(2)}, u32[]{:S(2)}) collective-permute-start(f32[2,384,128]{2,1,0:T(8,128)} %get-tuple-element.94), channel_id=1, source_target_pairs={{0,240},{16,0},{32,16},{48,32},{64,48},{80,64},{96,80},{112,96},{1... | collective-permute-start | bytes 1179656 | tf_op jit(solution)/shard_map/ppermute | solution.py:21
  180.1 25.1 %all-to-all-start.8 = ((f32[256,1,128]{2,1,0:T(1,128)}), f32[256,1,128]{2,1,0:T(1,128)S(1)}, u32[]{:S(2)}, u32[]{:S(2)}) async-start(f32[256,1,128]{2,1,0:T(1,128)} %bitcast.46), calls=%async_computation.8 | async-start | bytes 262144 | tf_op jit(solution)/shard_map/all_to_all | solution.py:678
  192.3 6.6 %collective-permute-start.20 = (f32[384,128]{1,0:T(8,128)S(1)}, f32[384,128]{1,0:T(8,128)S(1)}, u32[]{:S(2)}, u32[]{:S(2)}) collective-permute-start(f32[384,128]{1,0:T(8,128)S(1)} %copy-done.10), channel_id=1, source_target_pairs={{0,15},{1,0},{2,1},{3,2},{4,3},{5,4},{6,5},{7,6},{8,7},{9,8},{10,9... | collective-permute-start | bytes 589832 | tf_op jit(solution)/shard_map/ppermute | solution.py:21
